TPU v7x, 32 devices: a whole 2x2x4 slice. The times are simulated.
32 devices in a mesh: tower: 2 (over core), group: 4 (over y, x), blk: 4 (over z).
Axes of the slice: x: 2, y: 2, z: 4, core: 2. Of those that a mesh axis runs over, the one named last changes fastest.
Arguments:
- queries: bfloat16 [128, 384, 256], P(('tower', 'group', 'blk')), may hold values from -102 to 102
- cluster_ids: int32 [128, 64], P(('tower', 'group', 'blk')), may hold values from 0 to 127, all different within a row
- positives: int32 [128, 384], P(('tower', 'group', 'blk')), may hold values from 0 to 1023
- owner_map: int32 [4, 128], P('group'), may hold values from 0 to 127, each once within a row
- panels: bfloat16 [512, 16, 256], P(('group', 'blk')), may hold values from -0.375 to 0.375
- scales: bfloat16 [512, 16], P(('group', 'blk')), may hold values from 0.5 to 2
Outputs:
- losses: bfloat16 [128, 384], P(('tower', 'group', 'blk'))
- query_grads: bfloat16 [128, 384, 256], P(('tower', 'group', 'blk'))
- panel_grads: float32 [512, 16, 256], P(('group', 'blk'), 'tower')
Inputs may be any that keep to these rules, and one draw needn't show every extreme that they name: `cluster_ids`: each row lists 64 different clusters. `owner_map`: each row is a permutation.
All inputs are finite; a program needn't handle non-finite values.
Results may differ from a plain program's by a relative error of at most 0.014.
Values may be sent and summed in bfloat16 or wider, within the bound.
No kernel may reach another device: no remote copies, remote signals or barrier semaphores. Data moves between devices by JAX's collectives and lax.ppermute only.
A program may use at most 64 MiB of HBM per device.

v0:
```python
import jax
import jax.numpy as jnp
from jax import lax
from jax.sharding import PartitionSpec as P

FLOOR_SCORE = -1e30


def score_part(flat_query, panel_part, scale_part, row_sel, first_slot):
    how_many, panel_items, feat_width = panel_part.shape
    scale_row = scale_part.reshape(how_many * panel_items).astype(jnp.float32)
    scores = (
        jnp.dot(
            flat_query,
            panel_part.reshape(how_many * panel_items, feat_width).T,
            preferred_element_type=jnp.float32,
        )
        * scale_row[None, :]
    )
    allowed = jnp.repeat(row_sel, panel_items, axis=1)
    columns = first_slot * panel_items + lax.iota(jnp.int32, how_many * panel_items)
    return (scores, allowed, columns, scale_row)


def shards(queries, cluster_ids, positives, owner_map, panels, scales):
    queries, cluster_ids, positives = (
        lax.all_to_all(queries, "group", split_axis=0, concat_axis=0, tiled=True),
        lax.all_to_all(cluster_ids, "group", split_axis=0, concat_axis=0, tiled=True),
        lax.all_to_all(positives, "group", split_axis=0, concat_axis=0, tiled=True),
    )
    block_count, block_rows, feat_width = queries.shape
    per_dev, panel_items = scales.shape
    blk_count = lax.axis_size("blk")
    group_slots = per_dev * blk_count
    flat_query = queries.reshape(block_count * block_rows, feat_width)
    slot_iota = lax.iota(jnp.int32, group_slots)
    ids_hot = cluster_ids[:, :, None] == slot_iota[None, None, :]
    listed = jnp.sum(jnp.where(ids_hot, owner_map[0][None, None, :], 0), axis=2)
    selected = jnp.any(listed[:, :, None] == slot_iota[None, None, :], axis=1)
    row_sel = jnp.repeat(selected, block_rows, axis=0)
    pos_slot = jnp.take_along_axis(listed, positives // panel_items, axis=1)
    target = (pos_slot * panel_items + positives % panel_items).reshape(block_count * block_rows)
    row_total = block_count * block_rows
    whole_panels, whole_scales = (
        lax.all_gather(panels, "blk", axis=0, tiled=True),
        lax.all_gather(scales, "blk", axis=0, tiled=True),
    )
    peak_now = jnp.full((row_total,), FLOOR_SCORE, jnp.float32)
    scores, allowed, columns, scale_row = score_part(
        flat_query, whole_panels, whole_scales, row_sel, 0
    )
    masked = jnp.where(allowed, scores, FLOOR_SCORE)
    new_peak = jnp.maximum(peak_now, jnp.max(masked, axis=1))
    new_total = jnp.sum(jnp.where(allowed, jnp.exp(masked - new_peak[:, None]), 0.0), axis=1)
    pos_score = jnp.sum(jnp.where(columns[None, :] == target[:, None], scores, 0.0), axis=1)
    peak_now, total_now, pos_score = (new_peak, new_total, pos_score)
    log_total = peak_now + jnp.log(total_now)
    scores, allowed, columns, scale_row = score_part(
        flat_query, whole_panels, whole_scales, row_sel, 0
    )
    chances = jnp.where(allowed, jnp.exp(scores - log_total[:, None]), 0.0)
    is_target = (columns[None, :] == target[:, None]).astype(jnp.float32)
    weights = ((chances - is_target) * scale_row[None, :]).astype(jnp.bfloat16)
    query_acc = jnp.dot(
        weights,
        whole_panels.reshape(group_slots * panel_items, feat_width),
        preferred_element_type=jnp.float32,
    )
    grad_accum = lax.psum_scatter(
        jnp.dot(weights.T, flat_query, preferred_element_type=jnp.float32)
        .reshape(per_dev * lax.axis_size("blk"), panel_items, feat_width)
        .astype(jnp.bfloat16),
        "blk",
        scatter_dimension=0,
        tiled=True,
    )
    panel_grads = lax.psum_scatter(grad_accum, "tower", scatter_dimension=1, tiled=True).astype(
        jnp.float32
    )
    losses = (log_total - pos_score).astype(jnp.bfloat16).reshape(block_count, block_rows)
    query_grads = query_acc.astype(jnp.bfloat16).reshape(block_count, block_rows, feat_width)
    back_grads, back_losses = (
        lax.all_to_all(query_grads, "group", split_axis=0, concat_axis=0, tiled=True),
        lax.all_to_all(losses, "group", split_axis=0, concat_axis=0, tiled=True),
    )
    return (back_losses, back_grads, panel_grads)


def solution(mesh):
    return jax.shard_map(
        shards,
        mesh=mesh,
        in_specs=(
            P(("tower", "group", "blk"), None, None),
            P(("tower", "group", "blk"), None),
            P(("tower", "group", "blk"), None),
            P("group", None),
            P(("group", "blk"), None, None),
            P(("group", "blk"), None),
        ),
        out_specs=(
            P(("tower", "group", "blk"), None),
            P(("tower", "group", "blk"), None, None),
            P(("group", "blk"), "tower", None),
        ),
        check_vma=False,
    )
```

profile of v0, /device:TPU:0, one launch (start us, length us, event | category | flops | bytes accessed | tf_op | source)
XLA Modules:
  0.0 145.0 jit_solution(3357532611632144300)
XLA Ops:
  7.2 0.7 all-gather.3.cloned.1.call-update
  7.9 5.2 %all-to-all-start = ((s32[4,1,64]{2,1,0:T(1,128)}), s32[4,1,64]{2,1,0:T(1,128)S(1)}, u32[]{:S(2)}, u32[]{:S(2)}) async-start(s32[4,1,64]{2,1,0:T(1,128)} %bitcast.60), calls=%async_computation | async-start | bytes 4096 | tf_op jit(solution)/shard_map/all_to_all | solution.py:28
  13.1 0.7 all_to_all.31
  13.8 3.9 %all-to-all-done = s32[4,1,64]{2,1,0:T(1,128)S(1)} async-done(((s32[4,1,64]{2,1,0:T(1,128)}), s32[4,1,64]{2,1,0:T(1,128)S(1)}, u32[]{:S(2)}, u32[]{:S(2)}) %all-to-all-start) | async-done | bytes 1056 | tf_op jit(solution)/shard_map/all_to_all | solution.py:28
  17.6 7.0 %all_to_all.43 = s32[4,1,384]{2,1,0:T(1,128)S(1)} all-to-all(s32[4,1,384]{2,1,0:T(1,128)S(1)} %all_to_all.31), channel_id=1, replica_groups=mesh['tower'=2,'group'=4,'blk'=4] {'group'}, dimensions={0} | all-to-all | bytes 12288 | tf_op jit(solution)/shard_map/all_to_all | solution.py:29
  24.7 4.2 %all-to-all-start.1 = ((bf16[4,384,256]{2,1,0:T(8,128)(2,1)}), bf16[4,384,256]{2,1,0:T(8,128)(2,1)}, u32[]{:S(2)}, u32[]{:S(2)}) async-start(bf16[4,384,256]{2,1,0:T(8,128)(2,1)} %param.6), calls=%async_computation.1 | async-start | bytes 1572864 | tf_op jit(solution)/shard_map/all_to_all | solution.py:27
  28.9 13.6 %all-gather = bf16[4,32,16]{1,2,0:T(8,128)(2,1)S(1)} all-gather(bf16[1,32,16]{1,2,0:T(8,128)(2,1)} %bitcast.58), channel_id=1, replica_groups=mesh['tower'=2,'group'=4,'blk'=4] {'blk'}, dimensions={0}, use_global_device_ids=true | all-gather | bytes 5120 | tf_op jit(solution)/shard_map/all_gather | solution.py:46
  42.7 0.9 select_reduce_fusion.2
  43.6 0.1 fusion.1
  43.7 0.1 copy.35
  43.9 0.2 broadcast_in_dim.51
  44.2 0.8 broadcast_in_dim.52
  45.0 6.6 %copy.37 = pred[1536,2048]{1,0:T(32,128)(4,1)S(1)} copy(pred[1536,2048]{0,1:T(8,128)(4,1)S(1)} %bitcast.47) | data formatting | bytes 6291456 | tf_op jit(solution)/shard_map/reshape | solution.py:20
  51.8 13.3 %gather_fusion = s32[1536]{0:T(1024)S(1)} fusion(s32[4,64]{1,0:T(4,128)S(1)} %select_reduce_fusion.2, s32[1536]{0:T(1024)S(1)} %reshape.255), kind=kCustom, calls=%fused_computation | custom fusion | bytes 24576 | tf_op jit(solution)/shard_map/jit(take_along_axis)/gather | solution.py:41
  65.2 4.3 %fusion = (f32[1536]{0:T(1024)S(1)}, f32[1536,2048]{1,0:T(8,128)S(1)}) fusion(pred[1536,2048]{1,0:T(32,128)(4,1)S(1)} %copy.37, f32[2048]{0:T(1024)S(1)} %reshape.254, bf16[1536,256]{1,0:T(8,128)(2,1)} %bitcast.4, bf16[2048,256]{1,0:T(8,128)(2,1)} %bitcast.49), kind=kOutput, calls=%fused_computation.6 | convolution fusion | flops 1620048384 | bytes 17577984 | tf_op jit(solution)/shard_map/dot_general | solution.py:13
  69.5 7.2 %select_reduce_fusion = (f32[1536]{0:T(1024)S(1)}, f32[1536]{0:T(1024)S(1)}) fusion(f32[1536,2048]{1,0:T(8,128)S(1)} %get-tuple-element.14, s32[1536]{0:T(1024)S(1)} %fusion.2, f32[2048]{0:T(1024)S(1)} %reshape.254, pred[1536,2048]{1,0:T(32,128)(4,1)S(1)} %copy.37, f32[1536]{0:T(1024)S(1)} %broadcast_maximum_fusion), kind=kLoop, calls=%fused_computation.2 | loop fusion | flops 25162752 | bytes 15761408 | tf_op jit(solution)/shard_map/reduce_sum | solution.py:55
  76.7 6.8 %multiply_convert_fusion = bf16[1536,2048]{1,0:T(8,128)(2,1)} fusion(pred[1536,2048]{1,0:T(32,128)(4,1)S(1)} %copy.37, f32[1536,2048]{1,0:T(8,128)S(1)} %get-tuple-element.14, f32[1536]{0:T(1024)S(1)} %get-tuple-element.12, s32[1536]{0:T(1024)S(1)} %fusion.2, f32[2048]{0:T(1024)S(1)} %reshape.254), kind=kLoop, calls=%fused_computation.1 | loop fusion | flops 25165824 | bytes 22040576 | tf_op jit(solution)/shard_map/convert_element_type | solution.py:63
  83.5 8.6 %copy.41 = bf16[2048,1536]{1,0:T(8,128)(2,1)} copy(bf16[2048,1536]{0,1:T(8,128)(2,1)} %bitcast.46) | data formatting | bytes 12582912 | tf_op jit(solution)/shard_map/dot_general | solution.py:70
  92.1 5.8 %convolution_convert_fusion.1 = bf16[128,16,256]{2,1,0:T(8,128)(2,1)} fusion(bf16[128,16,1536]{2,1,0:T(8,128)(2,1)} %bitcast.48, bf16[1536,256,1]{1,0,2:T(8,128)(2,1)} %bitcast.11), kind=kOutput, calls=%fused_computation.8 | convolution fusion | flops 1611137024 | bytes 8126464 | tf_op jit(solution)/shard_map/dot_general | solution.py:70
  98.0 0.5 broadcast.202
  98.5 0.7 reduce.3
  99.2 0.7 reshape.271
  99.8 4.0 %all-to-all-start.3 = ((bf16[4,2,192]{2,1,0:T(2,128)(2,1)}), bf16[4,2,192]{2,1,0:T(2,128)(2,1)S(1)}, u32[]{:S(2)}, u32[]{:S(2)}) async-start(bf16[4,2,192]{2,1,0:T(2,128)(2,1)} %reshape.271), calls=%async_computation.3 | async-start | bytes 8192 | tf_op jit(solution)/shard_map/all_to_all | solution.py:84
  103.8 5.7 %convolution_convert_fusion = bf16[1536,256]{1,0:T(8,128)(2,1)} fusion(bf16[1536,2048]{1,0:T(8,128)(2,1)} %multiply_convert_fusion, bf16[2048,256]{1,0:T(8,128)(2,1)S(1)} %bitcast.50), kind=kOutput, calls=%fused_computation.7 | convolution fusion | flops 1611005952 | bytes 8126464 | tf_op jit(solution)/shard_map/dot_general | solution.py:64
  109.5 4.2 %all-to-all-start.4 = ((bf16[4,384,256]{2,1,0:T(8,128)(2,1)}), bf16[4,384,256]{2,1,0:T(8,128)(2,1)S(1)}, u32[]{:S(2)}, u32[]{:S(2)}) async-start(bf16[4,384,256]{2,1,0:T(8,128)(2,1)} %bitcast.8), calls=%async_computation.4 | async-start | bytes 1572864 | tf_op jit(solution)/shard_map/all_to_all | solution.py:83
  113.7 12.9 %reduce-scatter.5.cloned.1.call-done = bf16[32,16,256]{2,1,0:T(8,128)(2,1)} async-done(((bf16[128,16,256]{2,1,0:T(8,128)(2,1)}), bf16[32,16,256]{2,1,0:T(8,128)(2,1)}) %reduce-scatter.5.cloned.1.call-update) | async-done | bytes 262160 | tf_op jit(solution)/shard_map/reduce_scatter | solution.py:69
  126.6 1.7 %copy.46 = bf16[2,8,32,256]{3,1,2,0:T(8,128)(2,1)} copy(bf16[2,8,32,256]{3,1,0,2:T(8,128)(2,1)} %bitcast.55) | data formatting | bytes 524288
  128.4 0.6 copy.53
  128.9 6.9 %reduce-scatter.7.cloned.1.call-done = bf16[8,8192]{1,0:T(8,128)(2,1)} async-done(((bf16[16,8192]{1,0:T(8,128)(2,1)}), bf16[8,8192]{1,0:T(8,128)(2,1)}) %reduce-scatter.7.cloned.1.call-update) | async-done | bytes 131088
  135.8 0.9 copy.52
  136.8 0.8 copy_convert_fusion
  137.5 0.9 copy.58
  (23 shorter events, 0.7 us)
Async XLA Ops:
  7.2 58.0 %all-gather.3.cloned.1.call-start = ((), (), s32[]{:S(2)}) async-start(), calls=%async_computation.7 | async-start | bytes 1310720 | tf_op jit(solution)/shard_map/all_gather | solution.py:45
  7.9 9.7 %all-to-all-start = ((s32[4,1,64]{2,1,0:T(1,128)}), s32[4,1,64]{2,1,0:T(1,128)S(1)}, u32[]{:S(2)}, u32[]{:S(2)}) async-start(s32[4,1,64]{2,1,0:T(1,128)} %bitcast.60), calls=%async_computation | async-start | bytes 4096 | tf_op jit(solution)/shard_map/all_to_all | solution.py:28
  24.7 40.5 %all-to-all-start.1 = ((bf16[4,384,256]{2,1,0:T(8,128)(2,1)}), bf16[4,384,256]{2,1,0:T(8,128)(2,1)}, u32[]{:S(2)}, u32[]{:S(2)}) async-start(bf16[4,384,256]{2,1,0:T(8,128)(2,1)} %param.6), calls=%async_computation.1 | async-start | bytes 1572864 | tf_op jit(solution)/shard_map/all_to_all | solution.py:27
  28.9 97.7 %reduce-scatter.5.cloned.1.call-start = ((), (), s32[]{:S(2)}) async-start(), calls=%async_computation.8 | async-start | bytes 1310720 | tf_op jit(solution)/shard_map/reduce_scatter | solution.py:69
  92.1 11.7 %copy-start = (bf16[128,16,256]{2,1,0:T(8,128)(2,1)S(1)}, bf16[128,16,256]{2,1,0:T(8,128)(2,1)}, u32[]{:S(2)}) copy-start(bf16[128,16,256]{2,1,0:T(8,128)(2,1)} %all-gather.3.cloned.1.call-done) | copy-start | bytes 3145732
  99.8 9.7 %all-to-all-start.3 = ((bf16[4,2,192]{2,1,0:T(2,128)(2,1)}), bf16[4,2,192]{2,1,0:T(2,128)(2,1)S(1)}, u32[]{:S(2)}, u32[]{:S(2)}) async-start(bf16[4,2,192]{2,1,0:T(2,128)(2,1)} %reshape.271), calls=%async_computation.3 | async-start | bytes 8192 | tf_op jit(solution)/shard_map/all_to_all | solution.py:84
  109.5 19.4 %all-to-all-start.4 = ((bf16[4,384,256]{2,1,0:T(8,128)(2,1)}), bf16[4,384,256]{2,1,0:T(8,128)(2,1)S(1)}, u32[]{:S(2)}, u32[]{:S(2)}) async-start(bf16[4,384,256]{2,1,0:T(8,128)(2,1)} %bitcast.8), calls=%async_computation.4 | async-start | bytes 1572864 | tf_op jit(solution)/shard_map/all_to_all | solution.py:83
  113.7 22.1 %reduce-scatter.7.cloned.1.call-start = ((), (), s32[]{:S(2)}) async-start(), calls=%async_computation.9 | async-start | bytes 393216
Sparse Core Ops, SparseCore 0:
  9.6 30.8 all-gather.2
  98.1 28.4 reduce-scatter.4
  129.5 6.3 reduce-scatter.6
where the time goes:
time: 146 us; the launch traced here: 145 us
  local copies, waits for them, and re-layouts  36.1 us (25%)
  waiting for transfers between devices  24.4 us (17%)
  blocking collectives  20.6 us (14%)
  starting transfers between devices  17.7 us (12%)
  other arithmetic  16.6 us (11%)
  matrix products  15.7 us (11%)
  between operations  13.9 us (10%)
    all_gather x1, blocking collectives, shards(): lax.all_gather(scales, 'blk', axis=0, tiled=True)  13.6 us
    gather x2, local copies, waits for them, and re-layouts, shards(): pos_slot = jnp.take_along_axis(listed, positives // panel_items, axis=1)  13.3 us
    reduce_scatter x1, waiting for transfers between devices, shards(): lax.psum_scatter(jnp.dot(weights.T, flat_query, preferred_element_type=jn...  12.9 us
    dot_general x1, local copies, waits for them, and re-layouts, shards(): jnp.dot(weights.T, flat_query, preferred_element_type=jnp.float32)  8.63 us
    unnamed x4, waiting for transfers between devices  7.6 us
    reduce_sum x1, other arithmetic, shards(): jnp.sum(jnp.where(columns[None, :] == target[:, None], scores, 0.0), axis=1)  7.22 us
    all_to_all x1, blocking collectives, shards(): lax.all_to_all(positives, 'group', split_axis=0, concat_axis=0, tiled=True)  7.01 us
    convert_element_type x1, other arithmetic, shards(): weights = ((chances - is_target) * scale_row[None, :]).astype(jnp.bfloat16)  6.82 us
  transfers between devices with their start and end apart: 7, of which 3 were waited for; matrix products, arithmetic and copies ran while one was open for 22% of the time, Pallas kernels for 0%

commit v1 on v0

v1 whole, which is shorter than its diff:
```python
import functools

import jax
import jax.numpy as jnp
from jax import lax
from jax.experimental import pallas as pl
from jax.experimental.pallas import tpu as pltpu
from jax.sharding import PartitionSpec as P

VMEM_LIMIT = 48 * 1024 * 1024
LANES = 128
TILE = 16


def peers(axis):
    n = lax.axis_size(axis)
    me = lax.axis_index(axis)
    if n & (n - 1) == 0:
        return [(me ^ k, me ^ k, [(i, i ^ k) for i in range(n)]) for k in range(1, n)]
    return [
        (lax.rem(me + k, n), lax.rem(me + n - k, n), [(i, (i + k) % n) for i in range(n)])
        for k in range(1, n)
    ]


def pick(array, index):
    return lax.dynamic_index_in_dim(array, index, 0, keepdims=False)


def weights_kernel(dims, *refs):
    (nq, nblk, ntow, rows, nsel, items, slots, shard) = dims
    meta, pos_ref = refs[0], refs[1]
    q_refs = refs[2 : 2 + nq]
    own_ref, own_scale = refs[2 + nq], refs[3 + nq]
    n_piece = (nblk - 1) * ntow
    pieces = refs[4 + nq : 4 + nq + n_piece]
    w_ref, sel_ref, loss_ref, grad_ref = refs[4 + nq + n_piece : 8 + nq + n_piece]
    panel, scale, wide, score, sel_wide, term = refs[8 + nq + n_piece :]
    part = shard // ntow
    cand = nsel * items
    row0 = nq * nsel

    own_start = pl.multiple_of(meta[row0] * (shard * items), TILE)
    panel[pl.ds(own_start, shard * items), :] = own_ref[...]
    scale[...] = jnp.zeros_like(scale)
    scale[pl.ds(pl.multiple_of(meta[row0] * shard, 8), shard), 0:items] = own_scale[...].astype(
        jnp.float32
    )
    for n, piece in enumerate(pieces):
        first = meta[row0 + 1 + n]
        panel[pl.ds(pl.multiple_of(first * items, TILE), part * items), :] = piece[
            0 : part * items, :
        ]
        scale[pl.ds(first, part), :] = piece[
            part * items : part * items + part, 0:LANES
        ].astype(jnp.float32)

    total = slots * items
    slot_of = lax.broadcasted_iota(jnp.int32, (total, slots), 0) // items
    spread = (slot_of == lax.broadcasted_iota(jnp.int32, (total, slots), 1)).astype(jnp.bfloat16)
    by_slot = jnp.dot(
        spread, scale[...].astype(jnp.bfloat16), preferred_element_type=jnp.float32
    )
    item_of = lax.broadcasted_iota(jnp.int32, (total, LANES), 0) % items
    own_item = item_of == lax.broadcasted_iota(jnp.int32, (total, LANES), 1)
    wide[...] = jnp.dot(
        jnp.where(own_item, by_slot, 0.0).astype(jnp.bfloat16),
        jnp.ones((LANES, LANES), jnp.bfloat16),
        preferred_element_type=jnp.float32,
    )
    grad_ref[...] = jnp.zeros_like(grad_ref)

    step = 64
    reps = rows // LANES
    for b in range(nq):
        for j in range(nsel):
            start = pl.multiple_of(meta[b * nsel + j] * items, TILE)
            sel_ref[b, j * items : (j + 1) * items, :] = panel[pl.ds(start, items), :]
            sel_wide[j * items : (j + 1) * items, :] = wide[pl.ds(start, items), :]
        query = q_refs[b][...]
        score[...] = lax.dot_general(
            sel_ref[b],
            query,
            (((1,), (1,)), ((), ())),
            preferred_element_type=jnp.float32,
        )
        pos = pos_ref[b : b + 1, :]

        def scaled(c, peak):
            at = pl.ds(pl.multiple_of(c * step, step), step)
            s = score[at, :] * jnp.tile(sel_wide[at, :], (1, reps))
            score[at, :] = s
            return jnp.maximum(peak, jnp.max(s.reshape(step // 8, 8, rows), axis=0))

        peak8 = lax.fori_loop(
            0, cand // step, scaled, jnp.full((8, rows), -jnp.inf, jnp.float32), unroll=True
        )
        peak = jnp.max(peak8, axis=0, keepdims=True)

        def exps(c, carry):
            total8, pick8 = carry
            at = pl.ds(pl.multiple_of(c * step, step), step)
            s = score[at, :]
            hot = lax.broadcasted_iota(jnp.int32, (step, rows), 0) == pos - c * step
            e = jnp.exp(s - peak)
            score[at, :] = e
            picked = jnp.where(hot, s, 0.0)
            return (
                total8 + jnp.sum(e.reshape(step // 8, 8, rows), axis=0),
                pick8 + jnp.sum(picked.reshape(step // 8, 8, rows), axis=0),
            )

        zero8 = jnp.zeros((8, rows), jnp.float32)
        total8, pick8 = lax.fori_loop(0, cand // step, exps, (zero8, zero8), unroll=True)
        total = jnp.sum(total8, axis=0, keepdims=True)
        picked = jnp.sum(pick8, axis=0, keepdims=True)
        loss_ref[b : b + 1, :] = peak + jnp.log(total) - picked
        inverse = 1.0 / total

        def weigh(c, _):
            at = pl.ds(pl.multiple_of(c * step, step), step)
            hot = lax.broadcasted_iota(jnp.int32, (step, rows), 0) == pos - c * step
            chance = score[at, :] * inverse - jnp.where(hot, 1.0, 0.0)
            w = chance * jnp.tile(sel_wide[at, :], (1, reps))
            w_ref[b, at, :] = w.astype(jnp.bfloat16)
            return 0

        lax.fori_loop(0, cand // step, weigh, 0, unroll=True)
        term[...] = jnp.dot(w_ref[b], query, preferred_element_type=jnp.float32)
        for j in range(nsel):
            start = pl.multiple_of(meta[b * nsel + j] * items, TILE)
            grad_ref[pl.ds(start, items), :] += term[j * items : (j + 1) * items, :]


def query_kernel(nq, w_ref, sel_ref, *outs):
    for b in range(nq):
        outs[b][...] = lax.dot_general(
            w_ref[b],
            sel_ref[b],
            (((0,), (0,)), ((), ())),
            preferred_element_type=jnp.float32,
        ).astype(jnp.bfloat16)


def shards(queries, cluster_ids, positives, owner_map, panels, scales):
    nq, rows, width = queries.shape
    shard, items = scales.shape
    nsel = cluster_ids.shape[1]
    nblk, ntow = lax.axis_size("blk"), lax.axis_size("tower")
    slots = shard * nblk
    part = shard // ntow
    cand = nsel * items
    mine, blk_me, tow_me = lax.axis_index("group"), lax.axis_index("blk"), lax.axis_index("tower")
    group_peers, blk_peers, tow_peers = peers("group"), peers("blk"), peers("tower")
    per = nq // lax.axis_size("group")

    flat_scales = jnp.pad(scales, ((0, 0), (0, width - items)))
    half = lax.dynamic_slice_in_dim(panels, tow_me * part, part, 0).reshape(part * items, width)
    half_scales = lax.dynamic_slice_in_dim(flat_scales, tow_me * part, part, 0)
    pad_rows = -part % TILE
    message = jnp.concatenate([half, half_scales, jnp.zeros((pad_rows, width), half.dtype)])
    pieces, firsts = [], []
    for to, source, pattern in blk_peers:
        piece = lax.ppermute(message, "blk", pattern)
        pieces.append(piece)
        firsts.append(source * shard + tow_me * part)
        for _, tow_source, tow_pattern in tow_peers:
            pieces.append(lax.ppermute(piece, "tower", tow_pattern))
            firsts.append(source * shard + tow_source * part)

    blocks = queries.reshape(nq // per, per, rows, width)
    lists = jnp.concatenate([cluster_ids, positives], axis=1).reshape(nq // per, per, nsel + rows)
    got_q, got_l = [pick(blocks, mine)], [pick(lists, mine)]
    for to, source, pattern in group_peers:
        got_l.append(lax.ppermute(pick(lists, to), "group", pattern))
        got_q.append(lax.ppermute(pick(blocks, to), "group", pattern))
    q_list = [q[i] for q in got_q for i in range(per)]
    got = jnp.concatenate(got_l, axis=0)
    ids, pos = got[:, :nsel], got[:, nsel:]
    hot = ids[:, :, None] == lax.iota(jnp.int32, slots)[None, None, :]
    listed = jnp.sum(jnp.where(hot, owner_map[0][None, None, :], 0), axis=2)
    meta = jnp.concatenate(
        [listed.reshape(-1), jnp.stack([blk_me] + firsts).astype(jnp.int32)]
    )

    vmem = pl.BlockSpec(memory_space=pltpu.VMEM)
    smem = pl.BlockSpec(memory_space=pltpu.SMEM)
    dims = (nq, nblk, ntow, rows, nsel, items, slots, shard)
    w, sel, loss, grads = pl.pallas_call(
        functools.partial(weights_kernel, dims),
        out_shape=(
            jax.ShapeDtypeStruct((nq, cand, rows), jnp.bfloat16),
            jax.ShapeDtypeStruct((nq, cand, width), jnp.bfloat16),
            jax.ShapeDtypeStruct((nq, rows), jnp.float32),
            jax.ShapeDtypeStruct((slots * items, width), jnp.float32),
        ),
        in_specs=[smem] + [vmem] * (3 + nq + len(pieces)),
        out_specs=(vmem,) * 4,
        scratch_shapes=[
            pltpu.VMEM((slots * items, width), jnp.bfloat16),
            pltpu.VMEM((slots, LANES), jnp.float32),
            pltpu.VMEM((slots * items, LANES), jnp.float32),
            pltpu.VMEM((cand, rows), jnp.float32),
            pltpu.VMEM((cand, LANES), jnp.float32),
            pltpu.VMEM((cand, width), jnp.float32),
        ],
        compiler_params=pltpu.CompilerParams(vmem_limit_bytes=VMEM_LIMIT),
        name="weights",
    )(meta, pos, *q_list, panels.reshape(shard * items, width), scales, *pieces)

    by_part = grads.reshape(slots, ntow, items // ntow, width)
    total = lax.dynamic_index_in_dim(by_part, tow_me, 1, keepdims=False)
    for to, source, pattern in tow_peers:
        sent = lax.dynamic_index_in_dim(by_part, to, 1, keepdims=False).astype(jnp.bfloat16)
        total = total + lax.ppermute(sent, "tower", pattern).astype(jnp.float32)
    by_shard = total.reshape(nblk, shard, items // ntow, width)

    query_grads = pl.pallas_call(
        functools.partial(query_kernel, nq),
        out_shape=[jax.ShapeDtypeStruct((rows, width), jnp.bfloat16)] * nq,
        in_specs=[vmem, vmem],
        out_specs=[vmem] * nq,
        compiler_params=pltpu.CompilerParams(vmem_limit_bytes=VMEM_LIMIT),
        name="query_grads",
    )(w, sel)

    panel_grads = pick(by_shard, blk_me)
    for to, source, pattern in blk_peers:
        sent = pick(by_shard, to).astype(jnp.bfloat16)
        panel_grads = panel_grads + lax.ppermute(sent, "blk", pattern).astype(jnp.float32)

    losses = loss.astype(jnp.bfloat16)
    back_l = jnp.zeros((nq // per, per, rows), jnp.bfloat16)
    back_q = jnp.zeros((nq // per, per, rows, width), jnp.bfloat16)
    back_l = lax.dynamic_update_index_in_dim(back_l, losses[:per], mine, 0)
    back_q = lax.dynamic_update_index_in_dim(back_q, jnp.stack(query_grads[:per]), mine, 0)
    for n, (to, source, pattern) in enumerate(group_peers):
        at = slice((n + 1) * per, (n + 2) * per)
        home = [(d, s) for s, d in pattern]
        back_l = lax.dynamic_update_index_in_dim(
            back_l, lax.ppermute(losses[at], "group", home), to, 0
        )
        back_q = lax.dynamic_update_index_in_dim(
            back_q, lax.ppermute(jnp.stack(query_grads[at]), "group", home), to, 0
        )
    return back_l.reshape(nq, rows), back_q.reshape(nq, rows, width), panel_grads


def solution(mesh):
    return jax.shard_map(
        shards,
        mesh=mesh,
        in_specs=(
            P(("tower", "group", "blk"), None, None),
            P(("tower", "group", "blk"), None),
            P(("tower", "group", "blk"), None),
            P("group", None),
            P(("group", "blk"), None, None),
            P(("group", "blk"), None),
        ),
        out_specs=(
            P(("tower", "group", "blk"), None),
            P(("tower", "group", "blk"), None, None),
            P(("group", "blk"), "tower", None),
        ),
        check_vma=False,
    )
```

time: 146 us -> 77.3 us (0.53)
  local copies, waits for them, and re-layouts: 36.1 us -> 14.8 us
  blocking collectives: 20.6 us -> 0 us
  matrix products: 15.7 us -> 0 us
  other arithmetic: 16.6 us -> 2.69 us
  between operations: 13.9 us -> 0.84 us
  Pallas kernels: 0 us -> 8.62 us
  starting transfers between devices: 17.7 us -> 26.2 us
    ppermute x0 -> x22, starting transfers between devices: none -> 26.2 us  [the longest x3 5.76 us: shards(): piece = lax.ppermute(message, 'blk', pattern)]
    ppermute x0 -> x22, waiting for transfers between devices: none -> 23.9 us  [the longest x3 8.38 us: shards(): got_l.append(lax.ppermute(pick(lists, to), 'group', pattern))]
    all_to_all x4 -> x0, starting transfers between devices: 17.6 us -> none  [the longest x1 5.18 us: shards(): lax.all_to_all(cluster_ids, 'group', split_axis=0, concat_axis=0, tiled=T...]
    dot_general x3 -> x0, matrix products: 15.7 us -> none  [the longest x1 5.8 us: shards(): jnp.dot(weights.T, flat_query, preferred_element_type=jnp.float32)]
    all_gather x1 -> x0, blocking collectives: 13.6 us -> none  [shards(): lax.all_gather(scales, 'blk', axis=0, tiled=True)]
    gather x2 -> x0, local copies, waits for them, and re-layouts: 13.3 us -> none  [shards(): pos_slot = jnp.take_along_axis(listed, positives // panel_items, axis=1)]
    reduce_scatter x1 -> x0, waiting for transfers between devices: 12.9 us -> none  [shards(): lax.psum_scatter(jnp.dot(weights.T, flat_query, preferred_element_type=jn...]
    dot_general x1 -> x0, local copies, waits for them, and re-layouts: 8.63 us -> none  [shards(): jnp.dot(weights.T, flat_query, preferred_element_type=jnp.float32)]
  transfers between devices with their start and end apart: 7 -> 22, of which waited for: 3 -> 9; matrix products, arithmetic and copies ran while one was open for 22% -> 10% of each run, Pallas kernels for 0% -> 0%
where the time goes in v1:
time: 77.3 us; the launch traced here: 77 us
  starting transfers between devices  26.2 us (34%)
  waiting for transfers between devices  23.9 us (31%)
  local copies, waits for them, and re-layouts  14.8 us (19%)
  Pallas kernels  8.62 us (11%)
  other arithmetic  2.69 us (3%)
  between operations  0.84 us (1%)
    pallas_call x1, Pallas kernels, shards(): pl.pallas_call(functools.partial(weights_kernel, dims), out_shape=(jax.Sh...  8.62 us
    unnamed x31, local copies, waits for them, and re-layouts  8.4 us
    ppermute x3, waiting for transfers between devices, shards(): got_l.append(lax.ppermute(pick(lists, to), 'group', pattern))  8.38 us
    ppermute x3, waiting for transfers between devices, shards(): lax.ppermute(sent, 'blk', pattern).astype(jnp.float32)  7.69 us
    ppermute x3, starting transfers between devices, shards(): piece = lax.ppermute(message, 'blk', pattern)  5.76 us
    ppermute x3, starting transfers between devices, shards(): lax.ppermute(jnp.stack(query_grads[at]), 'group', home)  4.8 us
    ppermute x3, starting transfers between devices, shards(): lax.ppermute(sent, 'blk', pattern).astype(jnp.float32)  4.45 us
    ppermute x3, waiting for transfers between devices, shards(): got_q.append(lax.ppermute(pick(blocks, to), 'group', pattern))  3.93 us
  transfers between devices with their start and end apart: 22, of which 9 were waited for; matrix products, arithmetic and copies ran while one was open for 10% of the time, Pallas kernels for 0%

profile of v1, /device:TPU:0, one launch (start us, length us, event | category | flops | bytes accessed | tf_op | source)
XLA Modules:
  0.0 77.0 jit_solution(4374073479815821973)
XLA Ops:
  0.7 0.8 %copy.12.refs_7_ = bf16[32,16]{1,0:T(8,128)(2,1)S(1)} copy(bf16[32,16]{0,1:T(8,128)(2,1)} %param.11) | data formatting | bytes 2048 | tf_op args[5]
  1.5 0.9 %constant_dynamic-slice_fusion = bf16[16,16,256]{2,1,0:T(8,128)(2,1)S(1)} fusion(bf16[32,16,256]{2,1,0:T(8,128)(2,1)} %param.10, s32[]{:T(128)S(6)} %select_n.61), kind=kLoop, calls=%fused_computation.32 | loop fusion | bytes 262148 | tf_op jit(solution)/shard_map/dynamic_slice | solution.py:158
  2.4 5.1 %collective-permute-start.10 = (bf16[272,256]{1,0:T(8,128)(2,1)S(1)}, bf16[272,256]{1,0:T(8,128)(2,1)S(1)}, u32[]{:S(2)}, u32[]{:S(2)}) collective-permute-start(bf16[272,256]{1,0:T(8,128)(2,1)S(1)} %pad_maximum_fusion), channel_id=1, source_target_pairs={{0,3},{1,2},{2,1},{3,0},{4,7},{5,6},{6,5},{7,4},{8,11},{9,10},{10,... | collective-permute-start | bytes 417800 | tf_op jit(solution)/shard_map/ppermute | solution.py:164
  8.2 1.3 %constant_dynamic-slice_fusion.1 = (bf16[1,384,256]{2,1,0:T(8,128)(2,1)S(1)}, bf16[1,384,256]{2,1,0:T(8,128)(2,1)S(1)}, bf16[384,256]{1,0:T(8,128)(2,1)S(1)}, bf16[1,384,256]{2,1,0:T(8,128)(2,1)S(1)}) fusion(bf16[4,384,256]{2,1,0:T(8,128)(2,1)} %param.6, s32[]{:T(128)S(6)} %select_n.59, s32[]{:T(128)S(6)} %select_n.57, s32[]{:T(128)S(6)} %select_n.56, ...), kind=kLoop, calls=%fused_computation.33 | loop fusion | bytes 1572880 | tf_op jit(solution)/shard_map/jit(dynamic_index_in_dim)/squeeze | solution.py:27
  9.5 1.7 %collective-permute-start.4 = (bf16[1,384,256]{2,1,0:T(8,128)(2,1)S(1)}, bf16[1,384,256]{2,1,0:T(8,128)(2,1)S(1)}, u32[]{:S(2)}, u32[]{:S(2)}) collective-permute-start(bf16[1,384,256]{2,1,0:T(8,128)(2,1)S(1)} %get-tuple-element.33), channel_id=1, source_target_pairs={{0,8},{4,12},{8,0},{12,4},{1,9},{5,13},{9,1},{13,5},{2,10},{6,14},... | collective-permute-start | bytes 589832 | tf_op jit(solution)/shard_map/ppermute | solution.py:176
  11.3 1.6 %collective-permute-start = (s32[1,448]{1,0:T(1,128)S(1)}, s32[1,448]{1,0:T(1,128)S(1)}, u32[]{:S(2)}, u32[]{:S(2)}) collective-permute-start(s32[1,448]{1,0:T(1,128)S(1)} %get-tuple-element.35), channel_id=1, source_target_pairs={{0,4},{4,0},{8,12},{12,8},{1,5},{5,1},{9,13},{13,9},{2,6},{6,2},{1... | collective-permute-start | bytes 5384 | tf_op jit(solution)/shard_map/ppermute | solution.py:175
  12.9 2.1 %collective-permute-done = s32[1,448]{1,0:T(1,128)S(1)} collective-permute-done((s32[1,448]{1,0:T(1,128)S(1)}, s32[1,448]{1,0:T(1,128)S(1)}, u32[]{:S(2)}, u32[]{:S(2)}) %collective-permute-start) | collective-permute-done | bytes 1824 | tf_op jit(solution)/shard_map/ppermute | solution.py:175
  15.3 3.2 %collective-permute-done.1 = s32[1,448]{1,0:T(1,128)S(1)} collective-permute-done((s32[1,448]{1,0:T(1,128)S(1)}, s32[1,448]{1,0:T(1,128)S(1)}, u32[]{:S(2)}, u32[]{:S(2)}) %collective-permute-start.1) | collective-permute-done | bytes 1824 | tf_op jit(solution)/shard_map/ppermute | solution.py:175
  18.5 1.4 %collective-permute-start.2 = (s32[1,448]{1,0:T(1,128)S(1)}, s32[1,448]{1,0:T(1,128)S(1)}, u32[]{:S(2)}, u32[]{:S(2)}) collective-permute-start(s32[1,448]{1,0:T(1,128)S(1)} %get-tuple-element.37), channel_id=1, source_target_pairs={{0,12},{4,8},{8,4},{12,0},{1,13},{5,9},{9,5},{13,1},{2,14},{6,10},... | collective-permute-start | bytes 5384 | tf_op jit(solution)/shard_map/ppermute | solution.py:175
  20.0 3.1 %collective-permute-done.2 = s32[1,448]{1,0:T(1,128)S(1)} collective-permute-done((s32[1,448]{1,0:T(1,128)S(1)}, s32[1,448]{1,0:T(1,128)S(1)}, u32[]{:S(2)}, u32[]{:S(2)}) %collective-permute-start.2) | collective-permute-done | bytes 1824 | tf_op jit(solution)/shard_map/ppermute | solution.py:175
  23.0 1.4 %collective-permute-start.5 = (bf16[1,384,256]{2,1,0:T(8,128)(2,1)S(1)}, bf16[1,384,256]{2,1,0:T(8,128)(2,1)S(1)}, u32[]{:S(2)}, u32[]{:S(2)}) collective-permute-start(bf16[1,384,256]{2,1,0:T(8,128)(2,1)S(1)} %get-tuple-element.30), channel_id=1, source_target_pairs={{0,12},{4,8},{8,4},{12,0},{1,13},{5,9},{9,5},{13,1},{2,14},{6,10},... | collective-permute-start | bytes 589832 | tf_op jit(solution)/shard_map/ppermute | solution.py:176
  26.7 2.9 %collective-permute-done.5 = bf16[1,384,256]{2,1,0:T(8,128)(2,1)S(1)} collective-permute-done((bf16[1,384,256]{2,1,0:T(8,128)(2,1)S(1)}, bf16[1,384,256]{2,1,0:T(8,128)(2,1)S(1)}, u32[]{:S(2)}, u32[]{:S(2)}) %collective-permute-start.5) | collective-permute-done | bytes 196640 | tf_op jit(solution)/shard_map/ppermute | solution.py:176
  29.6 1.0 %collective-permute-done.3 = bf16[1,384,256]{2,1,0:T(8,128)(2,1)S(1)} collective-permute-done((bf16[1,384,256]{2,1,0:T(8,128)(2,1)S(1)}, bf16[1,384,256]{2,1,0:T(8,128)(2,1)S(1)}, u32[]{:S(2)}, u32[]{:S(2)}) %collective-permute-start.3) | collective-permute-done | bytes 196640 | tf_op jit(solution)/shard_map/ppermute | solution.py:176
  32.6 0.9 %copy-done.3 = bf16[272,256]{1,0:T(8,128)(2,1)S(1)} copy-done((bf16[272,256]{1,0:T(8,128)(2,1)S(1)}, bf16[272,256]{1,0:T(8,128)(2,1)}, u32[]{:S(2)}) %copy-start.3) | copy-done | bytes 139288
  33.5 0.9 %copy-done.5 = bf16[272,256]{1,0:T(8,128)(2,1)S(1)} copy-done((bf16[272,256]{1,0:T(8,128)(2,1)S(1)}, bf16[272,256]{1,0:T(8,128)(2,1)}, u32[]{:S(2)}) %copy-start.5) | copy-done | bytes 139288
  34.4 0.9 %copy-done.7 = bf16[272,256]{1,0:T(8,128)(2,1)S(1)} copy-done((bf16[272,256]{1,0:T(8,128)(2,1)S(1)}, bf16[272,256]{1,0:T(8,128)(2,1)}, u32[]{:S(2)}) %copy-start.7) | copy-done | bytes 139288
  35.3 0.9 %copy-done.9 = bf16[272,256]{1,0:T(8,128)(2,1)S(1)} copy-done((bf16[272,256]{1,0:T(8,128)(2,1)S(1)}, bf16[272,256]{1,0:T(8,128)(2,1)}, u32[]{:S(2)}) %copy-start.9) | copy-done | bytes 139288
  36.2 8.6 %weights.1 = (bf16[4,1024,384]{2,1,0:T(8,128)(2,1)}, bf16[4,1024,256]{2,1,0:T(8,128)(2,1)S(1)}, f32[4,384]{1,0:T(4,128)S(1)}, f32[2048,256]{1,0:T(8,128)S(1)}) custom-call(s32[263]{0:T(512)S(1)} %concatenate.14.refs_0_, s32[4,384]{1,0:T(4,128)S(1)} %pad_add_fusion.refs_1_, bf16[384,256]{1,0:T(8,128)(2,1)S(1)} %get-tuple-element.32.refs_2_, ...), custom_call_target="tpu_custom_call" | custom-call | tf_op jit(solution)/shard_map/weights/pallas_call | solution.py:189
  44.8 1.3 %copy-done = f32[2048,256]{1,0:T(8,128)} copy-done((f32[2048,256]{1,0:T(8,128)}, f32[2048,256]{1,0:T(8,128)S(1)}, u32[]{:S(2)}) %copy-start) | copy-done | bytes 2097176
  46.4 3.6 %query_grads.1 = (bf16[4,384,256]{2,1,0:T(8,128)(2,1)S(1)}, bf16[384,256]{1,0:T(8,128)(2,1)}, bf16[384,256]{1,0:T(8,128)(2,1)}, bf16[384,256]{1,0:T(8,128)(2,1)}) fusion(bf16[4,384,256]{2,1,0:T(8,128)(2,1)S(1)} %reshape.83, s32[]{:T(128)S(6)} %select_n.56, bf16[4,1024,384]{2,1,0:T(8,128)(2,1)} %get-tuple-element.12, ...), kind=kCustom, calls=%fused_computation.9 | custom fusion | bytes 6029316 | tf_op jit(solution)/shard_map/query_grads/pallas_call | solution.py:218
  50.0 1.6 %collective-permute-start.15 = (bf16[1,384,256]{2,1,0:T(8,128)(2,1)}, bf16[1,384,256]{2,1,0:T(8,128)(2,1)S(1)}, u32[]{:S(2)}, u32[]{:S(2)}) collective-permute-start(bf16[1,384,256]{2,1,0:T(8,128)(2,1)} %bitcast.15), channel_id=1, source_target_pairs={{4,0},{0,4},{12,8},{8,12},{5,1},{1,5},{13,9},{9,13},{6,2},{2,6},{1... | collective-permute-start | bytes 589832 | tf_op jit(solution)/shard_map/ppermute | solution.py:244
  52.1 1.6 %collective-permute-start.13 = (bf16[1,384]{1,0:T(2,128)(2,1)S(1)}, bf16[1,384]{1,0:T(2,128)(2,1)S(1)}, u32[]{:S(2)}, u32[]{:S(2)}) collective-permute-start(bf16[1,384]{1,0:T(2,128)(2,1)S(1)} %get-tuple-element.39), channel_id=1, source_target_pairs={{8,0},{12,4},{0,8},{4,12},{9,1},{13,5},{1,9},{5,13},{10,2},{14,6},... | collective-permute-start | bytes 2312 | tf_op jit(solution)/shard_map/ppermute | solution.py:241
  53.8 1.5 %collective-permute-start.14 = (bf16[1,384]{1,0:T(2,128)(2,1)S(1)}, bf16[1,384]{1,0:T(2,128)(2,1)S(1)}, u32[]{:S(2)}, u32[]{:S(2)}) collective-permute-start(bf16[1,384]{1,0:T(2,128)(2,1)S(1)} %get-tuple-element.38), channel_id=1, source_target_pairs={{12,0},{8,4},{4,8},{0,12},{13,1},{9,5},{5,9},{1,13},{14,2},{10,6},... | collective-permute-start | bytes 2312 | tf_op jit(solution)/shard_map/ppermute | solution.py:241
  55.3 2.3 %collective-permute-done.12 = bf16[1,384]{1,0:T(2,128)(2,1)S(1)} collective-permute-done((bf16[1,384]{1,0:T(2,128)(2,1)S(1)}, bf16[1,384]{1,0:T(2,128)(2,1)S(1)}, u32[]{:S(2)}, u32[]{:S(2)}) %collective-permute-start.12) | collective-permute-done | bytes 800 | tf_op jit(solution)/shard_map/ppermute | solution.py:241
  57.6 1.6 %collective-permute-start.16 = (bf16[1,384,256]{2,1,0:T(8,128)(2,1)}, bf16[1,384,256]{2,1,0:T(8,128)(2,1)S(1)}, u32[]{:S(2)}, u32[]{:S(2)}) collective-permute-start(bf16[1,384,256]{2,1,0:T(8,128)(2,1)} %bitcast.48), channel_id=1, source_target_pairs={{8,0},{12,4},{0,8},{4,12},{9,1},{13,5},{1,9},{5,13},{10,2},{14,6},... | collective-permute-start | bytes 589832 | tf_op jit(solution)/shard_map/ppermute | solution.py:244
  59.3 1.5 %collective-permute-start.17 = (bf16[1,384,256]{2,1,0:T(8,128)(2,1)}, bf16[1,384,256]{2,1,0:T(8,128)(2,1)S(1)}, u32[]{:S(2)}, u32[]{:S(2)}) collective-permute-start(bf16[1,384,256]{2,1,0:T(8,128)(2,1)} %bitcast.47), channel_id=1, source_target_pairs={{12,0},{8,4},{4,8},{0,12},{13,1},{9,5},{5,9},{1,13},{14,2},{10,6},... | collective-permute-start | bytes 589832 | tf_op jit(solution)/shard_map/ppermute | solution.py:244
  60.9 1.5 %bitcast_add_fusion = f32[128,8,256]{2,1,0:T(8,128)S(1)} fusion(bf16[128,8,256]{2,1,0:T(8,128)(2,1)} %collective-permute-done.18, f32[128,2,8,256]{3,2,1,0:T(8,128)} %bitcast.39, s32[]{:T(128)S(6)} %select_n.62), kind=kLoop, calls=%fused_computation | loop fusion | flops 524288 | bytes 2621444 | tf_op jit(solution)/shard_map/add | solution.py:215
  62.5 1.3 %collective-permute-start.19 = (bf16[32,8,256]{2,1,0:T(8,128)(2,1)S(1)}, bf16[32,8,256]{2,1,0:T(8,128)(2,1)S(1)}, u32[]{:S(2)}, u32[]{:S(2)}) collective-permute-start(bf16[32,8,256]{2,1,0:T(8,128)(2,1)S(1)} %get-tuple-element.27), channel_id=1, source_target_pairs={{0,1},{1,0},{2,3},{3,2},{4,5},{5,4},{6,7},{7,6},{8,9},{9,8},{10,11... | collective-permute-start | bytes 393224 | tf_op jit(solution)/shard_map/ppermute | solution.py:230
  63.8 2.9 %collective-permute-start.20 = (bf16[32,8,256]{2,1,0:T(8,128)(2,1)S(1)}, bf16[32,8,256]{2,1,0:T(8,128)(2,1)S(1)}, u32[]{:S(2)}, u32[]{:S(2)}) collective-permute-start(bf16[32,8,256]{2,1,0:T(8,128)(2,1)S(1)} %get-tuple-element.29), channel_id=1, source_target_pairs={{0,2},{1,3},{2,0},{3,1},{4,6},{5,7},{6,4},{7,5},{8,10},{9,11},{10,... | collective-permute-start | bytes 393224 | tf_op jit(solution)/shard_map/ppermute | solution.py:230
  66.9 1.5 %collective-permute-done.16 = bf16[1,384,256]{2,1,0:T(8,128)(2,1)S(1)} collective-permute-done((bf16[1,384,256]{2,1,0:T(8,128)(2,1)}, bf16[1,384,256]{2,1,0:T(8,128)(2,1)S(1)}, u32[]{:S(2)}, u32[]{:S(2)}) %collective-permute-start.16) | collective-permute-done | bytes 196640 | tf_op jit(solution)/shard_map/ppermute | solution.py:244
  69.1 7.1 %collective-permute-done.20 = bf16[32,8,256]{2,1,0:T(8,128)(2,1)S(1)} collective-permute-done((bf16[32,8,256]{2,1,0:T(8,128)(2,1)S(1)}, bf16[32,8,256]{2,1,0:T(8,128)(2,1)S(1)}, u32[]{:S(2)}, u32[]{:S(2)}) %collective-permute-start.20) | collective-permute-done | bytes 131104 | tf_op jit(solution)/shard_map/ppermute | solution.py:230
  76.2 0.8 fusion.2
  (70 shorter events, 7.0 us)
Async XLA Ops:
  0.6 32.0 %copy-start.1 = (bf16[32,16,256]{2,1,0:T(8,128)(2,1)S(1)}, bf16[32,16,256]{2,1,0:T(8,128)(2,1)}, u32[]{:S(2)}) copy-start(bf16[32,16,256]{2,1,0:T(8,128)(2,1)} %param.10) | copy-start | bytes 786436
  0.6 10.5 %copy-start.13 = (s32[4,64]{1,0:T(4,128)S(1)}, s32[4,64]{1,0:T(4,128)}, u32[]{:S(2)}) copy-start(s32[4,64]{1,0:T(4,128)} %param.7) | copy-start | bytes 3076
  0.7 10.5 %copy-start.11 = (s32[4,384]{1,0:T(4,128)S(1)}, s32[4,384]{1,0:T(4,128)}, u32[]{:S(2)}) copy-start(s32[4,384]{1,0:T(4,128)} %param.8) | copy-start | bytes 18436
  0.7 25.5 %copy-start.14 = (s32[1,128]{1,0:T(1,128)S(1)}, s32[1,128]{1,0:T(1,128)}, u32[]{:S(2)}) copy-start(s32[1,128]{1,0:T(1,128)} %param.9) | copy-start | bytes 1540
  2.4 22.1 %collective-permute-start.10 = (bf16[272,256]{1,0:T(8,128)(2,1)S(1)}, bf16[272,256]{1,0:T(8,128)(2,1)S(1)}, u32[]{:S(2)}, u32[]{:S(2)}) collective-permute-start(bf16[272,256]{1,0:T(8,128)(2,1)S(1)} %pad_maximum_fusion), channel_id=1, source_target_pairs={{0,3},{1,2},{2,1},{3,0},{4,7},{5,6},{6,5},{7,4},{8,11},{9,10},{10,... | collective-permute-start | bytes 417800 | tf_op jit(solution)/shard_map/ppermute | solution.py:164
  7.5 17.4 %collective-permute-start.6 = (bf16[272,256]{1,0:T(8,128)(2,1)S(1)}, bf16[272,256]{1,0:T(8,128)(2,1)S(1)}, u32[]{:S(2)}, u32[]{:S(2)}) collective-permute-start(bf16[272,256]{1,0:T(8,128)(2,1)S(1)} %pad_maximum_fusion), channel_id=1, source_target_pairs={{0,1},{1,0},{2,3},{3,2},{4,5},{5,4},{6,7},{7,6},{8,9},{9,8},{10,11... | collective-permute-start | bytes 417800 | tf_op jit(solution)/shard_map/ppermute | solution.py:164
  7.5 17.4 %collective-permute-start.8 = (bf16[272,256]{1,0:T(8,128)(2,1)S(1)}, bf16[272,256]{1,0:T(8,128)(2,1)S(1)}, u32[]{:S(2)}, u32[]{:S(2)}) collective-permute-start(bf16[272,256]{1,0:T(8,128)(2,1)S(1)} %pad_maximum_fusion), channel_id=1, source_target_pairs={{0,2},{1,3},{2,0},{3,1},{4,6},{5,7},{6,4},{7,5},{8,10},{9,11},{10,... | collective-permute-start | bytes 417800 | tf_op jit(solution)/shard_map/ppermute | solution.py:164
  9.5 16.0 %collective-permute-start.4 = (bf16[1,384,256]{2,1,0:T(8,128)(2,1)S(1)}, bf16[1,384,256]{2,1,0:T(8,128)(2,1)S(1)}, u32[]{:S(2)}, u32[]{:S(2)}) collective-permute-start(bf16[1,384,256]{2,1,0:T(8,128)(2,1)S(1)} %get-tuple-element.33), channel_id=1, source_target_pairs={{0,8},{4,12},{8,0},{12,4},{1,9},{5,13},{9,1},{13,5},{2,10},{6,14},... | collective-permute-start | bytes 589832 | tf_op jit(solution)/shard_map/ppermute | solution.py:176
  11.3 3.7 %collective-permute-start = (s32[1,448]{1,0:T(1,128)S(1)}, s32[1,448]{1,0:T(1,128)S(1)}, u32[]{:S(2)}, u32[]{:S(2)}) collective-permute-start(s32[1,448]{1,0:T(1,128)S(1)} %get-tuple-element.35), channel_id=1, source_target_pairs={{0,4},{4,0},{8,12},{12,8},{1,5},{5,1},{9,13},{13,9},{2,6},{6,2},{1... | collective-permute-start | bytes 5384 | tf_op jit(solution)/shard_map/ppermute | solution.py:175
  14.9 3.6 %collective-permute-start.1 = (s32[1,448]{1,0:T(1,128)S(1)}, s32[1,448]{1,0:T(1,128)S(1)}, u32[]{:S(2)}, u32[]{:S(2)}) collective-permute-start(s32[1,448]{1,0:T(1,128)S(1)} %get-tuple-element.36), channel_id=1, source_target_pairs={{0,8},{4,12},{8,0},{12,4},{1,9},{5,13},{9,1},{13,5},{2,10},{6,14},... | collective-permute-start | bytes 5384 | tf_op jit(solution)/shard_map/ppermute | solution.py:175
  18.5 4.5 %collective-permute-start.2 = (s32[1,448]{1,0:T(1,128)S(1)}, s32[1,448]{1,0:T(1,128)S(1)}, u32[]{:S(2)}, u32[]{:S(2)}) collective-permute-start(s32[1,448]{1,0:T(1,128)S(1)} %get-tuple-element.37), channel_id=1, source_target_pairs={{0,12},{4,8},{8,4},{12,0},{1,13},{5,9},{9,5},{13,1},{2,14},{6,10},... | collective-permute-start | bytes 5384 | tf_op jit(solution)/shard_map/ppermute | solution.py:175
  23.0 6.6 %collective-permute-start.5 = (bf16[1,384,256]{2,1,0:T(8,128)(2,1)S(1)}, bf16[1,384,256]{2,1,0:T(8,128)(2,1)S(1)}, u32[]{:S(2)}, u32[]{:S(2)}) collective-permute-start(bf16[1,384,256]{2,1,0:T(8,128)(2,1)S(1)} %get-tuple-element.30), channel_id=1, source_target_pairs={{0,12},{4,8},{8,4},{12,0},{1,13},{5,9},{9,5},{13,1},{2,14},{6,10},... | collective-permute-start | bytes 589832 | tf_op jit(solution)/shard_map/ppermute | solution.py:176
  24.5 6.1 %collective-permute-start.3 = (bf16[1,384,256]{2,1,0:T(8,128)(2,1)S(1)}, bf16[1,384,256]{2,1,0:T(8,128)(2,1)S(1)}, u32[]{:S(2)}, u32[]{:S(2)}) collective-permute-start(bf16[1,384,256]{2,1,0:T(8,128)(2,1)S(1)} %get-tuple-element.31), channel_id=1, source_target_pairs={{0,4},{4,0},{8,12},{12,8},{1,5},{5,1},{9,13},{13,9},{2,6},{6,2},{1... | collective-permute-start | bytes 589832 | tf_op jit(solution)/shard_map/ppermute | solution.py:176
  24.9 5.7 %collective-permute-start.11 = (bf16[272,256]{1,0:T(8,128)(2,1)S(1)}, bf16[272,256]{1,0:T(8,128)(2,1)S(1)}, u32[]{:S(2)}, u32[]{:S(2)}) collective-permute-start(bf16[272,256]{1,0:T(8,128)(2,1)S(1)} %collective-permute-done.10.refs_12_), channel_id=1, source_target_pairs={{0,16},{16,0},{1,17},{17,1},{2,18},{18,2},{3,19},{19,3},{4,20},{20... | collective-permute-start | bytes 417800 | tf_op jit(solution)/shard_map/ppermute | solution.py:168
  24.9 6.3 %collective-permute-start.7 = (bf16[272,256]{1,0:T(8,128)(2,1)S(1)}, bf16[272,256]{1,0:T(8,128)(2,1)S(1)}, u32[]{:S(2)}, u32[]{:S(2)}) collective-permute-start(bf16[272,256]{1,0:T(8,128)(2,1)S(1)} %collective-permute-done.6.refs_8_), channel_id=1, source_target_pairs={{0,16},{16,0},{1,17},{17,1},{2,18},{18,2},{3,19},{19,3},{4,20},{20... | collective-permute-start | bytes 417800 | tf_op jit(solution)/shard_map/ppermute | solution.py:168
  25.5 6.5 %collective-permute-start.9 = (bf16[272,256]{1,0:T(8,128)(2,1)S(1)}, bf16[272,256]{1,0:T(8,128)(2,1)S(1)}, u32[]{:S(2)}, u32[]{:S(2)}) collective-permute-start(bf16[272,256]{1,0:T(8,128)(2,1)S(1)} %collective-permute-done.8.refs_10_), channel_id=1, source_target_pairs={{0,16},{16,0},{1,17},{17,1},{2,18},{18,2},{3,19},{19,3},{4,20},{20... | collective-permute-start | bytes 417800 | tf_op jit(solution)/shard_map/ppermute | solution.py:168
  32.6 0.9 %copy-start.3 = (bf16[272,256]{1,0:T(8,128)(2,1)S(1)}, bf16[272,256]{1,0:T(8,128)(2,1)}, u32[]{:S(2)}) copy-start(bf16[272,256]{1,0:T(8,128)(2,1)} %copy-done.2) | copy-start | bytes 417796
  33.5 0.9 %copy-start.5 = (bf16[272,256]{1,0:T(8,128)(2,1)S(1)}, bf16[272,256]{1,0:T(8,128)(2,1)}, u32[]{:S(2)}) copy-start(bf16[272,256]{1,0:T(8,128)(2,1)} %copy-done.4) | copy-start | bytes 417796
  35.3 0.9 %copy-start.9 = (bf16[272,256]{1,0:T(8,128)(2,1)S(1)}, bf16[272,256]{1,0:T(8,128)(2,1)}, u32[]{:S(2)}) copy-start(bf16[272,256]{1,0:T(8,128)(2,1)} %copy-done.8) | copy-start | bytes 417796
  44.8 1.3 %copy-start = (f32[2048,256]{1,0:T(8,128)}, f32[2048,256]{1,0:T(8,128)S(1)}, u32[]{:S(2)}) copy-start(f32[2048,256]{1,0:T(8,128)S(1)} %get-tuple-element.18) | copy-start | bytes 6291460
  46.2 14.7 %collective-permute-start.18 = (bf16[128,8,256]{2,1,0:T(8,128)(2,1)S(1)}, bf16[128,8,256]{2,1,0:T(8,128)(2,1)}, u32[]{:S(2)}, u32[]{:S(2)}) collective-permute-start(bf16[128,8,256]{2,1,0:T(8,128)(2,1)S(1)} %fusion), channel_id=1, source_target_pairs={{0,16},{16,0},{1,17},{17,1},{2,18},{18,2},{3,19},{19,3},{4,20},{20... | collective-permute-start | bytes 1572872 | tf_op jit(solution)/shard_map/ppermute | solution.py:215
  50.0 10.9 %collective-permute-start.15 = (bf16[1,384,256]{2,1,0:T(8,128)(2,1)}, bf16[1,384,256]{2,1,0:T(8,128)(2,1)S(1)}, u32[]{:S(2)}, u32[]{:S(2)}) collective-permute-start(bf16[1,384,256]{2,1,0:T(8,128)(2,1)} %bitcast.15), channel_id=1, source_target_pairs={{4,0},{0,4},{12,8},{8,12},{5,1},{1,5},{13,9},{9,13},{6,2},{2,6},{1... | collective-permute-start | bytes 589832 | tf_op jit(solution)/shard_map/ppermute | solution.py:244
  51.7 5.9 %collective-permute-start.12 = (bf16[1,384]{1,0:T(2,128)(2,1)S(1)}, bf16[1,384]{1,0:T(2,128)(2,1)S(1)}, u32[]{:S(2)}, u32[]{:S(2)}) collective-permute-start(bf16[1,384]{1,0:T(2,128)(2,1)S(1)} %get-tuple-element.40), channel_id=1, source_target_pairs={{4,0},{0,4},{12,8},{8,12},{5,1},{1,5},{13,9},{9,13},{6,2},{2,6},{1... | collective-permute-start | bytes 2312 | tf_op jit(solution)/shard_map/ppermute | solution.py:241
  52.1 7.1 %collective-permute-start.13 = (bf16[1,384]{1,0:T(2,128)(2,1)S(1)}, bf16[1,384]{1,0:T(2,128)(2,1)S(1)}, u32[]{:S(2)}, u32[]{:S(2)}) collective-permute-start(bf16[1,384]{1,0:T(2,128)(2,1)S(1)} %get-tuple-element.39), channel_id=1, source_target_pairs={{8,0},{12,4},{0,8},{4,12},{9,1},{13,5},{1,9},{5,13},{10,2},{14,6},... | collective-permute-start | bytes 2312 | tf_op jit(solution)/shard_map/ppermute | solution.py:241
  53.8 7.1 %collective-permute-start.14 = (bf16[1,384]{1,0:T(2,128)(2,1)S(1)}, bf16[1,384]{1,0:T(2,128)(2,1)S(1)}, u32[]{:S(2)}, u32[]{:S(2)}) collective-permute-start(bf16[1,384]{1,0:T(2,128)(2,1)S(1)} %get-tuple-element.38), channel_id=1, source_target_pairs={{12,0},{8,4},{4,8},{0,12},{13,1},{9,5},{5,9},{1,13},{14,2},{10,6},... | collective-permute-start | bytes 2312 | tf_op jit(solution)/shard_map/ppermute | solution.py:241
  57.6 10.9 %collective-permute-start.16 = (bf16[1,384,256]{2,1,0:T(8,128)(2,1)}, bf16[1,384,256]{2,1,0:T(8,128)(2,1)S(1)}, u32[]{:S(2)}, u32[]{:S(2)}) collective-permute-start(bf16[1,384,256]{2,1,0:T(8,128)(2,1)} %bitcast.48), channel_id=1, source_target_pairs={{8,0},{12,4},{0,8},{4,12},{9,1},{13,5},{1,9},{5,13},{10,2},{14,6},... | collective-permute-start | bytes 589832 | tf_op jit(solution)/shard_map/ppermute | solution.py:244
  59.3 9.2 %collective-permute-start.17 = (bf16[1,384,256]{2,1,0:T(8,128)(2,1)}, bf16[1,384,256]{2,1,0:T(8,128)(2,1)S(1)}, u32[]{:S(2)}, u32[]{:S(2)}) collective-permute-start(bf16[1,384,256]{2,1,0:T(8,128)(2,1)} %bitcast.47), channel_id=1, source_target_pairs={{12,0},{8,4},{4,8},{0,12},{13,1},{9,5},{5,9},{1,13},{14,2},{10,6},... | collective-permute-start | bytes 589832 | tf_op jit(solution)/shard_map/ppermute | solution.py:244
  60.9 7.6 %copy-start.12 = (bf16[4,384]{1,0:T(4,128)(2,1)}, bf16[4,384]{1,0:T(4,128)(2,1)S(1)}, u32[]{:S(2)}) copy-start(bf16[4,384]{1,0:T(4,128)(2,1)S(1)} %dynamic_update_slice.37) | copy-start | bytes 9220
  62.5 6.6 %collective-permute-start.19 = (bf16[32,8,256]{2,1,0:T(8,128)(2,1)S(1)}, bf16[32,8,256]{2,1,0:T(8,128)(2,1)S(1)}, u32[]{:S(2)}, u32[]{:S(2)}) collective-permute-start(bf16[32,8,256]{2,1,0:T(8,128)(2,1)S(1)} %get-tuple-element.27), channel_id=1, source_target_pairs={{0,1},{1,0},{2,3},{3,2},{4,5},{5,4},{6,7},{7,6},{8,9},{9,8},{10,11... | collective-permute-start | bytes 393224 | tf_op jit(solution)/shard_map/ppermute | solution.py:230
  63.8 12.4 %collective-permute-start.20 = (bf16[32,8,256]{2,1,0:T(8,128)(2,1)S(1)}, bf16[32,8,256]{2,1,0:T(8,128)(2,1)S(1)}, u32[]{:S(2)}, u32[]{:S(2)}) collective-permute-start(bf16[32,8,256]{2,1,0:T(8,128)(2,1)S(1)} %get-tuple-element.29), channel_id=1, source_target_pairs={{0,2},{1,3},{2,0},{3,1},{4,6},{5,7},{6,4},{7,5},{8,10},{9,11},{10,... | collective-permute-start | bytes 393224 | tf_op jit(solution)/shard_map/ppermute | solution.py:230
  66.7 9.5 %collective-permute-start.21 = (bf16[32,8,256]{2,1,0:T(8,128)(2,1)S(1)}, bf16[32,8,256]{2,1,0:T(8,128)(2,1)S(1)}, u32[]{:S(2)}, u32[]{:S(2)}) collective-permute-start(bf16[32,8,256]{2,1,0:T(8,128)(2,1)S(1)} %get-tuple-element.28), channel_id=1, source_target_pairs={{0,3},{1,2},{2,1},{3,0},{4,7},{5,6},{6,5},{7,4},{8,11},{9,10},{10,... | collective-permute-start | bytes 393224 | tf_op jit(solution)/shard_map/ppermute | solution.py:230
  68.5 8.5 %copy-start.10 = (bf16[4,384,256]{2,1,0:T(8,128)(2,1)}, bf16[4,384,256]{2,1,0:T(8,128)(2,1)S(1)}, u32[]{:S(2)}) copy-start(bf16[4,384,256]{2,1,0:T(8,128)(2,1)S(1)} %constant_dynamic-update-slice_fusion) | copy-start | bytes 2359300
  (5 other events, 3.5 us)

commit v2 on v0

v2 whole, which is shorter than its diff:
```python
import functools

import jax
import jax.numpy as jnp
from jax import lax
from jax.experimental import pallas as pl
from jax.experimental.pallas import tpu as pltpu
from jax.sharding import PartitionSpec as P

VMEM_LIMIT = 40 * 1024 * 1024
LANES = 128
TILE = 16
STEP = 64


def peers(axis):
    n = lax.axis_size(axis)
    me = lax.axis_index(axis)
    if n & (n - 1) == 0:
        return [(me ^ k, me ^ k, [(i, i ^ k) for i in range(n)]) for k in range(1, n)]
    return [
        (lax.rem(me + k, n), lax.rem(me + n - k, n), [(i, (i + k) % n) for i in range(n)])
        for k in range(1, n)
    ]


def pick(array, index):
    return lax.dynamic_index_in_dim(array, index, 0, keepdims=False)


def panel_message_kernel(part_rows, panels, scales, out, sem):
    start = pl.multiple_of(lax.axis_index("tower") * part_rows, TILE)
    copy = pltpu.make_async_copy(
        panels.at[pl.ds(start, part_rows), :], out.at[0:part_rows, :], sem
    )
    copy.start()
    items, shard = scales.shape
    out[part_rows : part_rows + items, :] = jnp.zeros((items, out.shape[1]), out.dtype)
    out[part_rows : part_rows + items, 0:shard] = scales[...]
    copy.wait()


def query_message_kernel(per, items, targets, queries, ids, positives, *refs):
    outs, (marks, sems) = refs[:-2], refs[-2:]
    rows = queries.shape[1]
    nsel = ids.shape[1]
    reps = rows // LANES
    goal = targets()
    copies = []
    for n, out in enumerate(outs):
        block = goal[n // per] * per + n % per
        copies.append(
            pltpu.make_async_copy(queries.at[block], out.at[0:rows, :], sems.at[n])
        )
        copies[-1].start()
    for n, out in enumerate(outs):
        block = goal[n // per] * per + n % per
        place = positives[pl.ds(block, 1), :]
        marks[...] = jnp.zeros_like(marks)
        for c in range(reps):
            chunk = place[:, c * LANES : (c + 1) * LANES]
            marks[c : c + 1, 0:LANES] = (chunk // items).astype(jnp.float32)
            marks[c : c + 1, LANES : 2 * LANES] = (chunk % items).astype(jnp.float32)
        marks[reps : reps + 1, 0:nsel] = ids[pl.ds(block, 1), :].astype(jnp.float32)
        out[rows : rows + TILE, :] = marks[...].astype(out.dtype)
    for copy in copies:
        copy.wait()


def score_kernel(dims, *refs):
    nq, nlocal, ntow, n_piece, rows, nsel, items, slots, shard, split = dims
    refs = list(refs)

    def take(n):
        out, refs[:] = refs[:n], refs[n:]
        return out

    meta, pos_local, scale_own, queries, own = take(5)
    messages = take(nq - nlocal)
    pieces = take(n_piece)
    outs = take(nq)
    (keep,) = take(1)
    sends = take(ntow - 1 if split else 0)
    panel, scale, wide, query, score, sel, sel_wide, weight, term, grad, sems = refs
    part = shard // ntow
    cand = nsel * items
    base = nq * nsel
    width = panel.shape[1]
    copies = []

    def fetch(source, target):
        copies.append(pltpu.make_async_copy(source, target, sems.at[len(copies)]))
        copies[-1].start()

    def row(n):
        return pl.multiple_of(meta[base + n] * items, TILE)

    fetch(own, panel.at[pl.ds(row(0), shard * items), :])
    for n, piece in enumerate(pieces):
        fetch(piece.at[0 : part * items, :], panel.at[pl.ds(row(n + 1), part * items), :])
        if n % ntow == 0:
            fetch(
                piece.at[part * items : part * items + items, 0:LANES], scale.at[n // ntow]
            )
    for n, message in enumerate(messages):
        fetch(message, query.at[nlocal + n])
    for n in range(nlocal):
        fetch(queries.at[meta[base + 1 + n_piece] * nlocal + n], query.at[n, 0:rows, :])
    grad[...] = jnp.zeros_like(grad)
    for copy in copies:
        copy.wait()

    item_of = lax.broadcasted_iota(jnp.int32, (shard * items, items), 0) % items
    spread = item_of == lax.broadcasted_iota(jnp.int32, (shard * items, items), 1)
    spread = spread.astype(jnp.bfloat16)

    def widen(values, first):
        lanes = values.shape[1]
        of_item = jnp.dot(spread, values, preferred_element_type=jnp.float32)
        slot_of = lax.broadcasted_iota(jnp.int32, (shard * items, lanes), 0) // items
        mine = slot_of == lax.broadcasted_iota(jnp.int32, (shard * items, lanes), 1)
        wide[pl.ds(first, shard * items), :] = jnp.dot(
            jnp.where(mine, of_item, 0.0).astype(jnp.bfloat16),
            jnp.ones((lanes, LANES), jnp.bfloat16),
            preferred_element_type=jnp.float32,
        )

    widen(scale_own[...], row(0))
    for n in range(n_piece // ntow):
        first = meta[base + 2 + n_piece + n] * (shard * items)
        widen(scale[n], pl.multiple_of(first, TILE))

    reps = rows // LANES
    chunks = cand // STEP

    def gather(b):
        two = b % 2
        for j in range(nsel):
            start = pl.multiple_of(meta[b * nsel + j] * items, TILE)
            at = slice(j * items, (j + 1) * items)
            sel[two, at, :] = panel[pl.ds(start, items), :]
            sel_wide[two, at, :] = wide[pl.ds(start, items), :]
        score[two] = lax.dot_general(
            sel[two],
            query[b, 0:rows, :],
            (((1,), (1,)), ((), ())),
            preferred_element_type=jnp.float32,
        )

    def positions(b):
        if b < nlocal:
            return pos_local[b : b + 1, :]
        marks = query[b, rows : rows + TILE, :].astype(jnp.float32)
        found = [
            marks[n : n + 1, 0:LANES] * items + marks[n : n + 1, LANES : 2 * LANES]
            for n in range(reps)
        ]
        return jnp.concatenate(found, axis=1).astype(jnp.int32)

    gather(0)
    for b in range(nq):
        two = b % 2
        pos = positions(b)
        if b + 1 < nq:
            gather(b + 1)
        peak8 = jnp.full((8, rows), -jnp.inf, jnp.float32)
        for c in range(chunks):
            at = slice(c * STEP, (c + 1) * STEP)
            s = score[two, at, :] * jnp.tile(sel_wide[two, at, :], (1, reps))
            score[two, at, :] = s
            peak8 = jnp.maximum(peak8, jnp.max(s.reshape(STEP // 8, 8, rows), axis=0))
        peak = jnp.max(peak8, axis=0, keepdims=True)
        total8 = jnp.zeros((8, rows), jnp.float32)
        pick8 = jnp.zeros((8, rows), jnp.float32)
        for c in range(chunks):
            at = slice(c * STEP, (c + 1) * STEP)
            s = score[two, at, :]
            hot = lax.broadcasted_iota(jnp.int32, (STEP, rows), 0) == pos - c * STEP
            e = jnp.exp(s - peak)
            score[two, at, :] = e
            total8 = total8 + jnp.sum(e.reshape(STEP // 8, 8, rows), axis=0)
            picked = jnp.where(hot, s, 0.0)
            pick8 = pick8 + jnp.sum(picked.reshape(STEP // 8, 8, rows), axis=0)
        total = jnp.sum(total8, axis=0, keepdims=True)
        loss = peak + jnp.log(total) - jnp.sum(pick8, axis=0, keepdims=True)
        inverse = 1.0 / total
        for c in range(chunks):
            at = slice(c * STEP, (c + 1) * STEP)
            hot = lax.broadcasted_iota(jnp.int32, (STEP, rows), 0) == pos - c * STEP
            chance = score[two, at, :] * inverse - jnp.where(hot, 1.0, 0.0)
            w = chance * jnp.tile(sel_wide[two, at, :], (1, reps))
            weight[two, at, :] = w.astype(jnp.bfloat16)
        term[two] = jnp.dot(
            weight[two], query[b, 0:rows, :], preferred_element_type=jnp.float32
        )
        outs[b][0:rows, :] = lax.dot_general(
            weight[two],
            sel[two],
            (((0,), (0,)), ((), ())),
            preferred_element_type=jnp.float32,
        ).astype(jnp.bfloat16)
        line = lax.broadcasted_iota(jnp.int32, (TILE, LANES), 0)
        below = jnp.zeros((TILE, LANES), jnp.float32)
        for n in range(reps):
            below = jnp.where(line == n, loss[:, n * LANES : (n + 1) * LANES], below)
        outs[b][rows : rows + TILE, :] = jnp.zeros((TILE, width), jnp.bfloat16)
        outs[b][rows : rows + TILE, 0:LANES] = below.astype(jnp.bfloat16)
        for j in range(nsel):
            slot = meta[b * nsel + j]
            add = term[two, j * items : (j + 1) * items, :]
            if split:
                grad[slot] += add.reshape(ntow, items // ntow, width)
            else:
                start = pl.multiple_of(slot * items, TILE)
                grad[pl.ds(start, items), :] += add
    if split:
        own_at = base + 2 + n_piece + n_piece // ntow
        keep[...] = grad[:, meta[own_at]].reshape(keep.shape)
        for n, send in enumerate(sends):
            send[...] = grad[:, meta[own_at + 1 + n]].reshape(send.shape).astype(send.dtype)
    else:
        keep[...] = grad[...]


def shards(queries, cluster_ids, positives, owner_map, panels, scales):
    nq, rows, width = queries.shape
    shard, items = scales.shape
    nsel = cluster_ids.shape[1]
    nblk, ntow = lax.axis_size("blk"), lax.axis_size("tower")
    slots = shard * nblk
    part = shard // ntow
    cand = nsel * items
    ngroup = lax.axis_size("group")
    mine, blk_me, tow_me = lax.axis_index("group"), lax.axis_index("blk"), lax.axis_index("tower")
    group_peers, blk_peers, tow_peers = peers("group"), peers("blk"), peers("tower")
    per = nq // ngroup
    split = (items // ntow) % 8 == 0
    vmem = pl.BlockSpec(memory_space=pltpu.VMEM)
    smem = pl.BlockSpec(memory_space=pltpu.SMEM)
    hbm = pl.BlockSpec(memory_space=pl.ANY)
    params = pltpu.CompilerParams(vmem_limit_bytes=VMEM_LIMIT)
    flat_panels = panels.reshape(shard * items, width)
    flat_scales = scales.T

    message = pl.pallas_call(
        functools.partial(panel_message_kernel, part * items),
        out_shape=jax.ShapeDtypeStruct((part * items + items, width), panels.dtype),
        in_specs=[hbm, vmem],
        out_specs=vmem,
        scratch_shapes=[pltpu.SemaphoreType.DMA],
        compiler_params=params,
        name="panel_message",
    )(flat_panels, flat_scales)
    pieces, firsts, sources = [], [], []
    for to, source, pattern in blk_peers:
        piece = lax.ppermute(message, "blk", pattern)
        pieces.append(piece)
        firsts.append(source * shard + tow_me * part)
        sources.append(source)
        for _, tow_source, tow_pattern in tow_peers:
            pieces.append(lax.ppermute(piece, "tower", tow_pattern))
            firsts.append(source * shard + tow_source * part)

    def targets():
        return [to for to, _, _ in peers("group")]

    leaving = pl.pallas_call(
        functools.partial(query_message_kernel, per, items, targets),
        out_shape=[jax.ShapeDtypeStruct((rows + TILE, width), queries.dtype)] * (nq - per),
        in_specs=[hbm, vmem, vmem],
        out_specs=[vmem] * (nq - per),
        scratch_shapes=[
            pltpu.VMEM((TILE, width), jnp.float32),
            pltpu.SemaphoreType.DMA((nq - per,)),
        ],
        compiler_params=params,
        name="query_message",
    )(queries, cluster_ids, positives)
    arrived = [
        lax.ppermute(leaving[n * per + i], "group", pattern)
        for n, (_, _, pattern) in enumerate(group_peers)
        for i in range(per)
    ]
    reps = rows // LANES
    ids = [pick(cluster_ids.reshape(ngroup, per, nsel), mine)]
    ids += [got[rows + reps : rows + reps + 1, :nsel].astype(jnp.int32) for got in arrived]
    ids = jnp.concatenate(ids, axis=0)
    hot = ids[:, :, None] == lax.iota(jnp.int32, slots)[None, None, :]
    listed = jnp.sum(jnp.where(hot, owner_map[0][None, None, :], 0), axis=2)
    places = [blk_me * shard] + firsts + [mine] + sources
    places += [tow_me] + [to for to, _, _ in tow_peers]
    meta = jnp.concatenate([listed.reshape(-1), jnp.stack(places).astype(jnp.int32)])
    pos_local = pick(positives.reshape(ngroup, per, rows), mine)

    dims = (nq, per, ntow, len(pieces), rows, nsel, items, slots, shard, split)
    sent_rows = slots * items // ntow
    keep_rows = sent_rows if split else slots * items
    n_send = ntow - 1 if split else 0
    grad_shape = (slots, ntow, items // ntow, width) if split else (slots * items, width)
    results = pl.pallas_call(
        functools.partial(score_kernel, dims),
        out_shape=[jax.ShapeDtypeStruct((rows + TILE, width), jnp.bfloat16)] * nq
        + [jax.ShapeDtypeStruct((keep_rows, width), jnp.float32)]
        + [jax.ShapeDtypeStruct((sent_rows, width), jnp.bfloat16)] * n_send,
        in_specs=[smem, vmem, vmem] + [hbm] * (2 + nq - per + len(pieces)),
        out_specs=[vmem] * (nq + 1 + n_send),
        scratch_shapes=[
            pltpu.VMEM((slots * items, width), jnp.bfloat16),
            pltpu.VMEM((max(nblk - 1, 1), items, LANES), jnp.bfloat16),
            pltpu.VMEM((slots * items, LANES), jnp.float32),
            pltpu.VMEM((nq, rows + TILE, width), jnp.bfloat16),
            pltpu.VMEM((2, cand, rows), jnp.float32),
            pltpu.VMEM((2, cand, width), jnp.bfloat16),
            pltpu.VMEM((2, cand, LANES), jnp.float32),
            pltpu.VMEM((2, cand, rows), jnp.bfloat16),
            pltpu.VMEM((2, cand, width), jnp.float32),
            pltpu.VMEM(grad_shape, jnp.float32),
            pltpu.SemaphoreType.DMA((1 + len(pieces) + (nblk - 1) + nq,)),
        ],
        compiler_params=params,
        name="score",
    )(meta, pos_local, flat_scales, queries, flat_panels, *arrived, *pieces)
    query_grads, keep, sends = results[:nq], results[nq], results[nq + 1 :]

    if split:
        total = keep
        for sent, (_, _, pattern) in zip(sends, tow_peers):
            total = total + lax.ppermute(sent, "tower", pattern).astype(jnp.float32)
    else:
        by_part = keep.reshape(slots, ntow, items // ntow, width)
        total = lax.dynamic_index_in_dim(by_part, tow_me, 1, keepdims=False)
        for to, _, pattern in tow_peers:
            sent = lax.dynamic_index_in_dim(by_part, to, 1, keepdims=False)
            sent = sent.astype(jnp.bfloat16)
            total = total + lax.ppermute(sent, "tower", pattern).astype(jnp.float32)
    total, *query_grads = lax.optimization_barrier((total, *query_grads))
    by_shard = total.reshape(nblk, shard, items // ntow, width)
    panel_grads = pick(by_shard, blk_me)
    for to, _, pattern in blk_peers:
        sent = pick(by_shard, to).astype(jnp.bfloat16)
        panel_grads = panel_grads + lax.ppermute(sent, "blk", pattern).astype(jnp.float32)

    back = [(mine, query_grads[:per])]
    for n, (to, _, pattern) in enumerate(group_peers):
        home = [(d, s) for s, d in pattern]
        blocks = query_grads[(n + 1) * per : (n + 2) * per]
        back.append((to, [lax.ppermute(block, "group", home) for block in blocks]))
    back_q = jnp.zeros((nq, rows, width), jnp.bfloat16)
    back_l = jnp.zeros((nq, rows), jnp.bfloat16)
    for to, blocks in back:
        for i, block in enumerate(blocks):
            back_q = lax.dynamic_update_index_in_dim(back_q, block[:rows], to * per + i, 0)
            line = block[rows : rows + reps, :LANES].reshape(rows)
            back_l = lax.dynamic_update_index_in_dim(back_l, line, to * per + i, 0)
    return back_l, back_q, panel_grads


def solution(mesh):
    return jax.shard_map(
        shards,
        mesh=mesh,
        in_specs=(
            P(("tower", "group", "blk"), None, None),
            P(("tower", "group", "blk"), None),
            P(("tower", "group", "blk"), None),
            P("group", None),
            P(("group", "blk"), None, None),
            P(("group", "blk"), None),
        ),
        out_specs=(
            P(("tower", "group", "blk"), None),
            P(("tower", "group", "blk"), None, None),
            P(("group", "blk"), "tower", None),
        ),
        check_vma=False,
    )
```

time: 146 us -> 62.1 us (0.43)
  local copies, waits for them, and re-layouts: 36.1 us -> 11.7 us
  blocking collectives: 20.6 us -> 0 us
  matrix products: 15.7 us -> 0 us
  other arithmetic: 16.6 us -> 3.05 us
  between operations: 13.9 us -> 0.84 us
  Pallas kernels: 0 us -> 12.3 us
  waiting for transfers between devices: 24.4 us -> 15.7 us
    ppermute x0 -> x16, starting transfers between devices: none -> 18.2 us  [the longest x3 5.68 us: shards(): piece = lax.ppermute(message, 'blk', pattern)]
    all_to_all x4 -> x0, starting transfers between devices: 17.6 us -> none  [the longest x1 5.18 us: shards(): lax.all_to_all(cluster_ids, 'group', split_axis=0, concat_axis=0, tiled=T...]
    dot_general x3 -> x0, matrix products: 15.7 us -> none  [the longest x1 5.8 us: shards(): jnp.dot(weights.T, flat_query, preferred_element_type=jnp.float32)]
    ppermute x0 -> x16, waiting for transfers between devices: none -> 15.7 us  [the longest x3 5.62 us: shards(): lax.ppermute(sent, 'blk', pattern).astype(jnp.float32)]
    all_gather x1 -> x0, blocking collectives: 13.6 us -> none  [shards(): lax.all_gather(scales, 'blk', axis=0, tiled=True)]
    gather x2 -> x0, local copies, waits for them, and re-layouts: 13.3 us -> none  [shards(): pos_slot = jnp.take_along_axis(listed, positives // panel_items, axis=1)]
    reduce_scatter x1 -> x0, waiting for transfers between devices: 12.9 us -> none  [shards(): lax.psum_scatter(jnp.dot(weights.T, flat_query, preferred_element_type=jn...]
    pallas_call x0 -> x3, Pallas kernels: none -> 12.3 us  [the longest x1 11.3 us: shards(): pl.pallas_call(functools.partial(score_kernel, dims), out_shape=[jax.Shap...]
  transfers between devices with their start and end apart: 7 -> 16, of which waited for: 3 -> 7; matrix products, arithmetic and copies ran while one was open for 22% -> 4% of each run, Pallas kernels for 0% -> 1%
where the time goes in v2:
time: 62.1 us; the launch traced here: 61.8 us
  starting transfers between devices  18.2 us (29%)
  waiting for transfers between devices  15.7 us (25%)
  Pallas kernels  12.3 us (20%)
  local copies, waits for them, and re-layouts  11.7 us (19%)
  other arithmetic  3.05 us (5%)
  between operations  0.84 us (1%)
    pallas_call x1, Pallas kernels, shards(): pl.pallas_call(functools.partial(score_kernel, dims), out_shape=[jax.Shap...  11.3 us
    unnamed x50, local copies, waits for them, and re-layouts  10.1 us
    ppermute x3, starting transfers between devices, shards(): piece = lax.ppermute(message, 'blk', pattern)  5.68 us
    ppermute x3, waiting for transfers between devices, shards(): lax.ppermute(sent, 'blk', pattern).astype(jnp.float32)  5.62 us
    ppermute x3, waiting for transfers between devices, shards(): piece = lax.ppermute(message, 'blk', pattern)  5.27 us
    ppermute x3, starting transfers between devices, shards(): lax.ppermute(sent, 'blk', pattern).astype(jnp.float32)  4.45 us
    ppermute x3, starting transfers between devices, shards(): back.append((to, [lax.ppermute(block, 'group', home) for block in blocks]))  3.88 us
    ppermute x3, starting transfers between devices, shards(): lax.ppermute(leaving[n * per + i], 'group', pattern)  3.62 us
  transfers between devices with their start and end apart: 16, of which 7 were waited for; matrix products, arithmetic and copies ran while one was open for 4% of the time, Pallas kernels for 1%

profile of v2, /device:TPU:0, one launch (start us, length us, event | category | flops | bytes accessed | tf_op | source)
XLA Modules:
  0.0 61.8 jit_solution(13986114695336685018)
XLA Ops:
  0.6 0.9 %copy-done.2 = bf16[32,16,256]{2,1,0:T(8,128)(2,1)S(1)} copy-done((bf16[32,16,256]{2,1,0:T(8,128)(2,1)S(1)}, bf16[32,16,256]{2,1,0:T(8,128)(2,1)}, u32[]{:S(2)}) %copy-start.2) | copy-done | bytes 262168
  1.6 0.7 %copy-done.8 = bf16[32,16]{0,1:T(8,128)(2,1)S(1)} copy-done((bf16[32,16]{0,1:T(8,128)(2,1)S(1)}, bf16[32,16]{0,1:T(8,128)(2,1)}, u32[]{:S(2)}) %copy-start.8) | copy-done | bytes 1048
  2.5 3.1 %collective-permute-start.3 = (bf16[272,256]{1,0:T(8,128)(2,1)S(1)}, bf16[272,256]{1,0:T(8,128)(2,1)S(1)}, u32[]{:S(2)}, u32[]{:S(2)}) collective-permute-start(bf16[272,256]{1,0:T(8,128)(2,1)S(1)} %panel_message.1), channel_id=1, source_target_pairs={{0,1},{1,0},{2,3},{3,2},{4,5},{5,4},{6,7},{7,6},{8,9},{9,8},{10,11... | collective-permute-start | bytes 417800 | tf_op jit(solution)/shard_map/ppermute | solution.py:256
  5.5 2.6 %collective-permute-start.5 = (bf16[272,256]{1,0:T(8,128)(2,1)S(1)}, bf16[272,256]{1,0:T(8,128)(2,1)S(1)}, u32[]{:S(2)}, u32[]{:S(2)}) collective-permute-start(bf16[272,256]{1,0:T(8,128)(2,1)S(1)} %panel_message.1), channel_id=1, source_target_pairs={{0,2},{1,3},{2,0},{3,1},{4,6},{5,7},{6,4},{7,5},{8,10},{9,11},{10,... | collective-permute-start | bytes 417800 | tf_op jit(solution)/shard_map/ppermute | solution.py:256
  8.2 1.1 %copy-done = bf16[4,384,256]{2,1,0:T(8,128)(2,1)S(1)} copy-done((bf16[4,384,256]{2,1,0:T(8,128)(2,1)S(1)}, bf16[4,384,256]{2,1,0:T(8,128)(2,1)}, u32[]{:S(2)}) %copy-start) | copy-done | bytes 786456
  9.3 0.8 %query_message.1 = (bf16[400,256]{1,0:T(8,128)(2,1)S(1)}, bf16[400,256]{1,0:T(8,128)(2,1)S(1)}, bf16[400,256]{1,0:T(8,128)(2,1)S(1)}) custom-call(bf16[4,384,256]{2,1,0:T(8,128)(2,1)S(1)} %copy-done, s32[4,64]{1,0:T(4,128)S(1)} %copy-done.11, s32[4,384]{1,0:T(4,128)S(1)} %copy-done.10), custom_call_target="tpu_custom_call" | custom-call | tf_op jit(solution)/shard_map/query_message/pallas_call | solution.py:267
  10.1 2.7 %collective-permute-start.2 = (bf16[400,256]{1,0:T(8,128)(2,1)S(1)}, bf16[400,256]{1,0:T(8,128)(2,1)S(1)}, u32[]{:S(2)}, u32[]{:S(2)}) collective-permute-start(bf16[400,256]{1,0:T(8,128)(2,1)S(1)} %get-tuple-element.19), channel_id=1, source_target_pairs={{0,12},{4,8},{8,4},{12,0},{1,13},{5,9},{9,5},{13,1},{2,14},{6,10},... | collective-permute-start | bytes 614408 | tf_op jit(solution)/shard_map/ppermute | solution.py:280
  13.7 5.3 %collective-permute-done.5.refs_10_ = bf16[272,256]{1,0:T(8,128)(2,1)S(1)} collective-permute-done((bf16[272,256]{1,0:T(8,128)(2,1)S(1)}, bf16[272,256]{1,0:T(8,128)(2,1)S(1)}, u32[]{:S(2)}, u32[]{:S(2)}) %collective-permute-start.5) | collective-permute-done | bytes 139296 | tf_op jit(solution)/shard_map/ppermute | solution.py:256
  19.0 0.5 collective-permute-start.6
  19.6 2.1 %collective-permute-done.1.refs_6_ = bf16[400,256]{1,0:T(8,128)(2,1)S(1)} collective-permute-done((bf16[400,256]{1,0:T(8,128)(2,1)S(1)}, bf16[400,256]{1,0:T(8,128)(2,1)S(1)}, u32[]{:S(2)}, u32[]{:S(2)}) %collective-permute-start.1) | collective-permute-done | bytes 204832 | tf_op jit(solution)/shard_map/ppermute | solution.py:280
  21.8 0.6 %copy-done.20 = s32[1,128]{1,0:T(1,128)S(1)} copy-done((s32[1,128]{1,0:T(1,128)S(1)}, s32[1,128]{1,0:T(1,128)}, u32[]{:S(2)}) %copy-start.20) | copy-done | bytes 536
  22.9 0.6 %copy-done.4 = bf16[272,256]{1,0:T(8,128)(2,1)} copy-done((bf16[272,256]{1,0:T(8,128)(2,1)}, bf16[272,256]{1,0:T(8,128)(2,1)S(1)}, u32[]{:S(2)}) %copy-start.4) | copy-done | bytes 139288
  23.6 0.7 %copy-done.6 = bf16[272,256]{1,0:T(8,128)(2,1)} copy-done((bf16[272,256]{1,0:T(8,128)(2,1)}, bf16[272,256]{1,0:T(8,128)(2,1)S(1)}, u32[]{:S(2)}) %copy-start.6) | copy-done | bytes 139288
  24.3 0.9 %copy-done.5 = bf16[272,256]{1,0:T(8,128)(2,1)S(1)} copy-done((bf16[272,256]{1,0:T(8,128)(2,1)S(1)}, bf16[272,256]{1,0:T(8,128)(2,1)}, u32[]{:S(2)}) %copy-start.5) | copy-done | bytes 139288
  25.2 0.9 %copy-done.7 = bf16[272,256]{1,0:T(8,128)(2,1)S(1)} copy-done((bf16[272,256]{1,0:T(8,128)(2,1)S(1)}, bf16[272,256]{1,0:T(8,128)(2,1)}, u32[]{:S(2)}) %copy-start.7) | copy-done | bytes 139288
  26.1 11.3 %score.1 = (bf16[400,256]{1,0:T(8,128)(2,1)S(1)}, bf16[400,256]{1,0:T(8,128)(2,1)S(1)}, bf16[400,256]{1,0:T(8,128)(2,1)S(1)}, bf16[400,256]{1,0:T(8,128)(2,1)S(1...) custom-call(s32[269]{0:T(512)S(1)} %concatenate.7.refs_0_, s32[1,384]{1,0:T(1,128)S(1)} %constant_dynamic-slice_fusion.refs_1_, ...), custom_call_target="tpu_custom_call" | custom-call | tf_op jit(solution)/shard_map/score/pallas_call | solution.py:300
  37.4 0.7 %copy-done.12 = bf16[400,256]{1,0:T(8,128)(2,1)} copy-done((bf16[400,256]{1,0:T(8,128)(2,1)}, bf16[400,256]{1,0:T(8,128)(2,1)S(1)}, u32[]{:S(2)}) %copy-start.12) | copy-done | bytes 204824
  38.1 0.7 %copy-done.14 = bf16[400,256]{1,0:T(8,128)(2,1)} copy-done((bf16[400,256]{1,0:T(8,128)(2,1)}, bf16[400,256]{1,0:T(8,128)(2,1)S(1)}, u32[]{:S(2)}) %copy-start.14) | copy-done | bytes 204824
  38.8 0.7 %copy-done.16 = bf16[400,256]{1,0:T(8,128)(2,1)} copy-done((bf16[400,256]{1,0:T(8,128)(2,1)}, bf16[400,256]{1,0:T(8,128)(2,1)S(1)}, u32[]{:S(2)}) %copy-start.16) | copy-done | bytes 204824
  39.4 2.1 %collective-permute-done.9 = bf16[1024,256]{1,0:T(8,128)(2,1)S(1)} collective-permute-done((bf16[1024,256]{1,0:T(8,128)(2,1)}, bf16[1024,256]{1,0:T(8,128)(2,1)S(1)}, u32[]{:S(2)}, u32[]{:S(2)}) %collective-permute-start.9) | collective-permute-done | bytes 524320 | tf_op jit(solution)/shard_map/ppermute | solution.py:328
  41.6 1.1 %convert_add_fusion = f32[1024,256]{1,0:T(8,128)} fusion(f32[1024,256]{1,0:T(8,128)S(1)} %get-tuple-element.20, bf16[1024,256]{1,0:T(8,128)(2,1)S(1)} %collective-permute-done.9), kind=kLoop, calls=%fused_computation | loop fusion | flops 524288 | bytes 2621440 | tf_op jit(solution)/shard_map/add | solution.py:328
  42.6 1.2 %fusion.5 = (bf16[32,8,256]{2,1,0:T(8,128)(2,1)S(1)}, bf16[32,8,256]{2,1,0:T(8,128)(2,1)S(1)}, bf16[32,8,256]{2,1,0:T(8,128)(2,1)S(1)}) fusion(f32[4,32,8,256]{3,2,1,0:T(8,128)} %bitcast.20, s32[]{:T(128)S(6)} %select_n.45, s32[]{:T(128)S(6)} %select_n.47, s32[]{:T(128)S(6)} %select_n.46), kind=kLoop, calls=%fused_computation.14 | loop fusion | bytes 786444 | tf_op jit(solution)/shard_map/convert_element_type | solution.py:340
  43.8 0.7 %collective-permute-start.13 = (bf16[32,8,256]{2,1,0:T(8,128)(2,1)S(1)}, bf16[32,8,256]{2,1,0:T(8,128)(2,1)S(1)}, u32[]{:S(2)}, u32[]{:S(2)}) collective-permute-start(bf16[32,8,256]{2,1,0:T(8,128)(2,1)S(1)} %get-tuple-element.31), channel_id=1, source_target_pairs={{0,1},{1,0},{2,3},{3,2},{4,5},{5,4},{6,7},{7,6},{8,9},{9,8},{10,11... | collective-permute-start | bytes 393224 | tf_op jit(solution)/shard_map/ppermute | solution.py:341
  44.5 3.5 %collective-permute-start.14 = (bf16[32,8,256]{2,1,0:T(8,128)(2,1)S(1)}, bf16[32,8,256]{2,1,0:T(8,128)(2,1)S(1)}, u32[]{:S(2)}, u32[]{:S(2)}) collective-permute-start(bf16[32,8,256]{2,1,0:T(8,128)(2,1)S(1)} %get-tuple-element.33), channel_id=1, source_target_pairs={{0,2},{1,3},{2,0},{3,1},{4,6},{5,7},{6,4},{7,5},{8,10},{9,11},{10,... | collective-permute-start | bytes 393224 | tf_op jit(solution)/shard_map/ppermute | solution.py:341
  48.3 1.4 %collective-permute-start.10 = (bf16[400,256]{1,0:T(8,128)(2,1)S(1)}, bf16[400,256]{1,0:T(8,128)(2,1)S(1)}, u32[]{:S(2)}, u32[]{:S(2)}) collective-permute-start(bf16[400,256]{1,0:T(8,128)(2,1)S(1)} %copy-done.17), channel_id=1, source_target_pairs={{4,0},{0,4},{12,8},{8,12},{5,1},{1,5},{13,9},{9,13},{6,2},{2,6},{1... | collective-permute-start | bytes 614408 | tf_op jit(solution)/shard_map/ppermute | solution.py:347
  49.7 0.8 %collective-permute-start.11 = (bf16[400,256]{1,0:T(8,128)(2,1)S(1)}, bf16[400,256]{1,0:T(8,128)(2,1)S(1)}, u32[]{:S(2)}, u32[]{:S(2)}) collective-permute-start(bf16[400,256]{1,0:T(8,128)(2,1)S(1)} %copy-done.15), channel_id=1, source_target_pairs={{8,0},{12,4},{0,8},{4,12},{9,1},{13,5},{1,9},{5,13},{10,2},{14,6},... | collective-permute-start | bytes 614408 | tf_op jit(solution)/shard_map/ppermute | solution.py:347
  50.7 1.0 %collective-permute-done.13 = bf16[32,8,256]{2,1,0:T(8,128)(2,1)S(1)} collective-permute-done((bf16[32,8,256]{2,1,0:T(8,128)(2,1)S(1)}, bf16[32,8,256]{2,1,0:T(8,128)(2,1)S(1)}, u32[]{:S(2)}, u32[]{:S(2)}) %collective-permute-start.13) | collective-permute-done | bytes 131104 | tf_op jit(solution)/shard_map/ppermute | solution.py:341
  51.7 1.7 %collective-permute-start.12 = (bf16[400,256]{1,0:T(8,128)(2,1)S(1)}, bf16[400,256]{1,0:T(8,128)(2,1)S(1)}, u32[]{:S(2)}, u32[]{:S(2)}) collective-permute-start(bf16[400,256]{1,0:T(8,128)(2,1)S(1)} %copy-done.13), channel_id=1, source_target_pairs={{12,0},{8,4},{4,8},{0,12},{13,1},{9,5},{5,9},{1,13},{14,2},{10,6},... | collective-permute-start | bytes 614408 | tf_op jit(solution)/shard_map/ppermute | solution.py:347
  53.3 4.6 %collective-permute-done.14 = bf16[32,8,256]{2,1,0:T(8,128)(2,1)S(1)} collective-permute-done((bf16[32,8,256]{2,1,0:T(8,128)(2,1)S(1)}, bf16[32,8,256]{2,1,0:T(8,128)(2,1)S(1)}, u32[]{:S(2)}, u32[]{:S(2)}) %collective-permute-start.14) | collective-permute-done | bytes 131104 | tf_op jit(solution)/shard_map/ppermute | solution.py:341
  57.9 1.7 %fusion.1 = f32[32,8,256]{2,1,0:T(8,128)} fusion(bf16[32,8,256]{2,1,0:T(8,128)(2,1)S(1)} %collective-permute-done.15, bf16[32,8,256]{2,1,0:T(8,128)(2,1)S(1)} %collective-permute-done.14, bf16[32,8,256]{2,1,0:T(8,128)(2,1)S(1)} %collective-permute-done.13, f32[4,32,8,256]{3,2,1,0:T(8,128)} %bitcast.20, s32[]{:T(128)S(6)} %select_n.44), kind=kLoop, calls=%fused_computation.3 | loop fusion | flops 393216 | bytes 917508 | tf_op jit(solution)/shard_map/add | solution.py:341
  60.3 0.5 copy-done.19
  60.9 0.9 %copy-done.18 = bf16[4,384,256]{2,1,0:T(8,128)(2,1)} copy-done((bf16[4,384,256]{2,1,0:T(8,128)(2,1)}, bf16[4,384,256]{2,1,0:T(8,128)(2,1)S(1)}, u32[]{:S(2)}) %copy-start.18) | copy-done | bytes 786456
  (75 shorter events, 2.9 us)
Async XLA Ops:
  0.6 1.0 %copy-start.2 = (bf16[32,16,256]{2,1,0:T(8,128)(2,1)S(1)}, bf16[32,16,256]{2,1,0:T(8,128)(2,1)}, u32[]{:S(2)}) copy-start(bf16[32,16,256]{2,1,0:T(8,128)(2,1)} %param.10) | copy-start | bytes 786436
  1.6 0.7 %copy-start.8 = (bf16[32,16]{0,1:T(8,128)(2,1)S(1)}, bf16[32,16]{0,1:T(8,128)(2,1)}, u32[]{:S(2)}) copy-start(bf16[32,16]{0,1:T(8,128)(2,1)} %param.11) | copy-start | bytes 3076
  2.3 5.9 %copy-start.10 = (s32[4,384]{1,0:T(4,128)S(1)}, s32[4,384]{1,0:T(4,128)}, u32[]{:S(2)}) copy-start(s32[4,384]{1,0:T(4,128)} %positives.1) | copy-start | bytes 18436
  2.3 5.9 %copy-start.11 = (s32[4,64]{1,0:T(4,128)S(1)}, s32[4,64]{1,0:T(4,128)}, u32[]{:S(2)}) copy-start(s32[4,64]{1,0:T(4,128)} %ids.1) | copy-start | bytes 3076
  2.3 22.0 %copy-start.3 = (bf16[32,16,256]{2,1,0:T(8,128)(2,1)S(1)}, bf16[32,16,256]{2,1,0:T(8,128)(2,1)}, u32[]{:S(2)}) copy-start(bf16[32,16,256]{2,1,0:T(8,128)(2,1)} %param.10) | copy-start | bytes 786436
  2.5 10.9 %collective-permute-start.3 = (bf16[272,256]{1,0:T(8,128)(2,1)S(1)}, bf16[272,256]{1,0:T(8,128)(2,1)S(1)}, u32[]{:S(2)}, u32[]{:S(2)}) collective-permute-start(bf16[272,256]{1,0:T(8,128)(2,1)S(1)} %panel_message.1), channel_id=1, source_target_pairs={{0,1},{1,0},{2,3},{3,2},{4,5},{5,4},{6,7},{7,6},{8,9},{9,8},{10,11... | collective-permute-start | bytes 417800 | tf_op jit(solution)/shard_map/ppermute | solution.py:256
  5.5 13.5 %collective-permute-start.5 = (bf16[272,256]{1,0:T(8,128)(2,1)S(1)}, bf16[272,256]{1,0:T(8,128)(2,1)S(1)}, u32[]{:S(2)}, u32[]{:S(2)}) collective-permute-start(bf16[272,256]{1,0:T(8,128)(2,1)S(1)} %panel_message.1), channel_id=1, source_target_pairs={{0,2},{1,3},{2,0},{3,1},{4,6},{5,7},{6,4},{7,5},{8,10},{9,11},{10,... | collective-permute-start | bytes 417800 | tf_op jit(solution)/shard_map/ppermute | solution.py:256
  8.1 10.9 %collective-permute-start.7 = (bf16[272,256]{1,0:T(8,128)(2,1)S(1)}, bf16[272,256]{1,0:T(8,128)(2,1)S(1)}, u32[]{:S(2)}, u32[]{:S(2)}) collective-permute-start(bf16[272,256]{1,0:T(8,128)(2,1)S(1)} %panel_message.1), channel_id=1, source_target_pairs={{0,3},{1,2},{2,1},{3,0},{4,7},{5,6},{6,5},{7,4},{8,11},{9,10},{10,... | collective-permute-start | bytes 417800 | tf_op jit(solution)/shard_map/ppermute | solution.py:256
  8.1 1.1 %copy-start = (bf16[4,384,256]{2,1,0:T(8,128)(2,1)S(1)}, bf16[4,384,256]{2,1,0:T(8,128)(2,1)}, u32[]{:S(2)}) copy-start(bf16[4,384,256]{2,1,0:T(8,128)(2,1)} %refs_3_.1) | copy-start | bytes 2359300
  9.3 15.0 %copy-start.1 = (bf16[4,384,256]{2,1,0:T(8,128)(2,1)S(1)}, bf16[4,384,256]{2,1,0:T(8,128)(2,1)}, u32[]{:S(2)}) copy-start(bf16[4,384,256]{2,1,0:T(8,128)(2,1)} %refs_3_.1) | copy-start | bytes 2359300
  10.1 9.4 %collective-permute-start.2 = (bf16[400,256]{1,0:T(8,128)(2,1)S(1)}, bf16[400,256]{1,0:T(8,128)(2,1)S(1)}, u32[]{:S(2)}, u32[]{:S(2)}) collective-permute-start(bf16[400,256]{1,0:T(8,128)(2,1)S(1)} %get-tuple-element.19), channel_id=1, source_target_pairs={{0,12},{4,8},{8,4},{12,0},{1,13},{5,9},{9,5},{13,1},{2,14},{6,10},... | collective-permute-start | bytes 614408 | tf_op jit(solution)/shard_map/ppermute | solution.py:280
  12.8 8.9 %collective-permute-start.1 = (bf16[400,256]{1,0:T(8,128)(2,1)S(1)}, bf16[400,256]{1,0:T(8,128)(2,1)S(1)}, u32[]{:S(2)}, u32[]{:S(2)}) collective-permute-start(bf16[400,256]{1,0:T(8,128)(2,1)S(1)} %get-tuple-element.18), channel_id=1, source_target_pairs={{0,8},{4,12},{8,0},{12,4},{1,9},{5,13},{9,1},{13,5},{2,10},{6,14},... | collective-permute-start | bytes 614408 | tf_op jit(solution)/shard_map/ppermute | solution.py:280
  13.4 8.5 %collective-permute-start = (bf16[400,256]{1,0:T(8,128)(2,1)S(1)}, bf16[400,256]{1,0:T(8,128)(2,1)S(1)}, u32[]{:S(2)}, u32[]{:S(2)}) collective-permute-start(bf16[400,256]{1,0:T(8,128)(2,1)S(1)} %get-tuple-element.17), channel_id=1, source_target_pairs={{0,4},{4,0},{8,12},{12,8},{1,5},{5,1},{9,13},{13,9},{2,6},{6,2},{1... | collective-permute-start | bytes 614408 | tf_op jit(solution)/shard_map/ppermute | solution.py:280
  19.0 3.9 %collective-permute-start.4 = (bf16[272,256]{1,0:T(8,128)(2,1)S(1)}, bf16[272,256]{1,0:T(8,128)(2,1)S(1)}, u32[]{:S(2)}, u32[]{:S(2)}) collective-permute-start(bf16[272,256]{1,0:T(8,128)(2,1)S(1)} %collective-permute-done.3.refs_8_), channel_id=1, source_target_pairs={{0,16},{16,0},{1,17},{17,1},{2,18},{18,2},{3,19},{19,3},{4,20},{20... | collective-permute-start | bytes 417800 | tf_op jit(solution)/shard_map/ppermute | solution.py:261
  19.0 3.9 %collective-permute-start.6 = (bf16[272,256]{1,0:T(8,128)(2,1)S(1)}, bf16[272,256]{1,0:T(8,128)(2,1)S(1)}, u32[]{:S(2)}, u32[]{:S(2)}) collective-permute-start(bf16[272,256]{1,0:T(8,128)(2,1)S(1)} %collective-permute-done.5.refs_10_), channel_id=1, source_target_pairs={{0,16},{16,0},{1,17},{17,1},{2,18},{18,2},{3,19},{19,3},{4,20},{20... | collective-permute-start | bytes 417800 | tf_op jit(solution)/shard_map/ppermute | solution.py:261
  19.5 4.0 %collective-permute-start.8 = (bf16[272,256]{1,0:T(8,128)(2,1)S(1)}, bf16[272,256]{1,0:T(8,128)(2,1)S(1)}, u32[]{:S(2)}, u32[]{:S(2)}) collective-permute-start(bf16[272,256]{1,0:T(8,128)(2,1)S(1)} %collective-permute-done.7.refs_12_), channel_id=1, source_target_pairs={{0,16},{16,0},{1,17},{17,1},{2,18},{18,2},{3,19},{19,3},{4,20},{20... | collective-permute-start | bytes 417800 | tf_op jit(solution)/shard_map/ppermute | solution.py:261
  22.8 1.5 %copy-start.9 = (bf16[32,16]{0,1:T(8,128)(2,1)S(1)}, bf16[32,16]{0,1:T(8,128)(2,1)}, u32[]{:S(2)}) copy-start(bf16[32,16]{0,1:T(8,128)(2,1)} %param.11) | copy-start | bytes 3076
  24.2 0.9 %copy-start.5 = (bf16[272,256]{1,0:T(8,128)(2,1)S(1)}, bf16[272,256]{1,0:T(8,128)(2,1)}, u32[]{:S(2)}) copy-start(bf16[272,256]{1,0:T(8,128)(2,1)} %copy-done.4) | copy-start | bytes 417796
  25.2 0.9 %copy-start.7 = (bf16[272,256]{1,0:T(8,128)(2,1)S(1)}, bf16[272,256]{1,0:T(8,128)(2,1)}, u32[]{:S(2)}) copy-start(bf16[272,256]{1,0:T(8,128)(2,1)} %copy-done.6) | copy-start | bytes 417796
  37.4 0.7 %copy-start.12 = (bf16[400,256]{1,0:T(8,128)(2,1)}, bf16[400,256]{1,0:T(8,128)(2,1)S(1)}, u32[]{:S(2)}) copy-start(bf16[400,256]{1,0:T(8,128)(2,1)S(1)} %get-tuple-element.29) | copy-start | bytes 614404
  38.1 0.7 %copy-start.14 = (bf16[400,256]{1,0:T(8,128)(2,1)}, bf16[400,256]{1,0:T(8,128)(2,1)S(1)}, u32[]{:S(2)}) copy-start(bf16[400,256]{1,0:T(8,128)(2,1)S(1)} %get-tuple-element.28) | copy-start | bytes 614404
  39.4 2.1 %collective-permute-start.9 = (bf16[1024,256]{1,0:T(8,128)(2,1)}, bf16[1024,256]{1,0:T(8,128)(2,1)S(1)}, u32[]{:S(2)}, u32[]{:S(2)}) collective-permute-start(bf16[1024,256]{1,0:T(8,128)(2,1)} %get-tuple-element.21), channel_id=1, source_target_pairs={{0,16},{16,0},{1,17},{17,1},{2,18},{18,2},{3,19},{19,3},{4,20},{20... | collective-permute-start | bytes 1572872 | tf_op jit(solution)/shard_map/ppermute | solution.py:328
  42.6 5.7 %copy-start.17 = (bf16[400,256]{1,0:T(8,128)(2,1)S(1)}, bf16[400,256]{1,0:T(8,128)(2,1)}, u32[]{:S(2)}) copy-start(bf16[400,256]{1,0:T(8,128)(2,1)} %copy-done.16) | copy-start | bytes 614404
  42.6 7.1 %copy-start.15 = (bf16[400,256]{1,0:T(8,128)(2,1)S(1)}, bf16[400,256]{1,0:T(8,128)(2,1)}, u32[]{:S(2)}) copy-start(bf16[400,256]{1,0:T(8,128)(2,1)} %copy-done.14) | copy-start | bytes 614404
  43.8 7.8 %collective-permute-start.13 = (bf16[32,8,256]{2,1,0:T(8,128)(2,1)S(1)}, bf16[32,8,256]{2,1,0:T(8,128)(2,1)S(1)}, u32[]{:S(2)}, u32[]{:S(2)}) collective-permute-start(bf16[32,8,256]{2,1,0:T(8,128)(2,1)S(1)} %get-tuple-element.31), channel_id=1, source_target_pairs={{0,1},{1,0},{2,3},{3,2},{4,5},{5,4},{6,7},{7,6},{8,9},{9,8},{10,11... | collective-permute-start | bytes 393224 | tf_op jit(solution)/shard_map/ppermute | solution.py:341
  44.5 13.5 %collective-permute-start.14 = (bf16[32,8,256]{2,1,0:T(8,128)(2,1)S(1)}, bf16[32,8,256]{2,1,0:T(8,128)(2,1)S(1)}, u32[]{:S(2)}, u32[]{:S(2)}) collective-permute-start(bf16[32,8,256]{2,1,0:T(8,128)(2,1)S(1)} %get-tuple-element.33), channel_id=1, source_target_pairs={{0,2},{1,3},{2,0},{3,1},{4,6},{5,7},{6,4},{7,5},{8,10},{9,11},{10,... | collective-permute-start | bytes 393224 | tf_op jit(solution)/shard_map/ppermute | solution.py:341
  48.0 10.0 %collective-permute-start.15 = (bf16[32,8,256]{2,1,0:T(8,128)(2,1)S(1)}, bf16[32,8,256]{2,1,0:T(8,128)(2,1)S(1)}, u32[]{:S(2)}, u32[]{:S(2)}) collective-permute-start(bf16[32,8,256]{2,1,0:T(8,128)(2,1)S(1)} %get-tuple-element.32), channel_id=1, source_target_pairs={{0,3},{1,2},{2,1},{3,0},{4,7},{5,6},{6,5},{7,4},{8,11},{9,10},{10,... | collective-permute-start | bytes 393224 | tf_op jit(solution)/shard_map/ppermute | solution.py:341
  48.3 11.4 %collective-permute-start.10 = (bf16[400,256]{1,0:T(8,128)(2,1)S(1)}, bf16[400,256]{1,0:T(8,128)(2,1)S(1)}, u32[]{:S(2)}, u32[]{:S(2)}) collective-permute-start(bf16[400,256]{1,0:T(8,128)(2,1)S(1)} %copy-done.17), channel_id=1, source_target_pairs={{4,0},{0,4},{12,8},{8,12},{5,1},{1,5},{13,9},{9,13},{6,2},{2,6},{1... | collective-permute-start | bytes 614408 | tf_op jit(solution)/shard_map/ppermute | solution.py:347
  49.7 10.4 %collective-permute-start.11 = (bf16[400,256]{1,0:T(8,128)(2,1)S(1)}, bf16[400,256]{1,0:T(8,128)(2,1)S(1)}, u32[]{:S(2)}, u32[]{:S(2)}) collective-permute-start(bf16[400,256]{1,0:T(8,128)(2,1)S(1)} %copy-done.15), channel_id=1, source_target_pairs={{8,0},{12,4},{0,8},{4,12},{9,1},{13,5},{1,9},{5,13},{10,2},{14,6},... | collective-permute-start | bytes 614408 | tf_op jit(solution)/shard_map/ppermute | solution.py:347
  50.6 1.1 %copy-start.13 = (bf16[400,256]{1,0:T(8,128)(2,1)S(1)}, bf16[400,256]{1,0:T(8,128)(2,1)}, u32[]{:S(2)}) copy-start(bf16[400,256]{1,0:T(8,128)(2,1)} %copy-done.12) | copy-start | bytes 614404
  51.7 8.5 %collective-permute-start.12 = (bf16[400,256]{1,0:T(8,128)(2,1)S(1)}, bf16[400,256]{1,0:T(8,128)(2,1)S(1)}, u32[]{:S(2)}, u32[]{:S(2)}) collective-permute-start(bf16[400,256]{1,0:T(8,128)(2,1)S(1)} %copy-done.13), channel_id=1, source_target_pairs={{12,0},{8,4},{4,8},{0,12},{13,1},{9,5},{5,9},{1,13},{14,2},{10,6},... | collective-permute-start | bytes 614408 | tf_op jit(solution)/shard_map/ppermute | solution.py:347
  60.9 0.9 %copy-start.18 = (bf16[4,384,256]{2,1,0:T(8,128)(2,1)}, bf16[4,384,256]{2,1,0:T(8,128)(2,1)S(1)}, u32[]{:S(2)}) copy-start(bf16[4,384,256]{2,1,0:T(8,128)(2,1)S(1)} %fusion.2) | copy-start | bytes 2359300
  (5 other events, 3.2 us)

commit v3 on v2

v3 whole, which is shorter than its diff:
```python
import functools
import math

import jax
import jax.numpy as jnp
from jax import lax
from jax.experimental import pallas as pl
from jax.experimental.pallas import tpu as pltpu
from jax.sharding import PartitionSpec as P

VMEM_LIMIT = 40 * 1024 * 1024
LANES = 128
TILE = 16
ORDER = (
    (("r", 0), ("g", 0), ("s", 0), ("p", 0), ("r", 1)),
    (("g", 1), ("s", 1), ("e", 0), ("w", 0), ("t", 0), ("p", 1), ("q", 0), ("a", 0)),
    (),
)
LN2 = math.log(2.0)


def peers(axis):
    n = lax.axis_size(axis)
    me = lax.axis_index(axis)
    if n & (n - 1) == 0:
        return [(me ^ k, me ^ k, [(i, i ^ k) for i in range(n)]) for k in range(1, n)]
    return [
        (lax.rem(me + k, n), lax.rem(me + n - k, n), [(i, (i + k) % n) for i in range(n)])
        for k in range(1, n)
    ]


def pick(array, index):
    return lax.dynamic_index_in_dim(array, index, 0, keepdims=False)


def panel_message_kernel(part_rows, panels, scales, out, held, sems):
    start = pl.multiple_of(lax.axis_index("tower") * part_rows, TILE)
    copy = pltpu.make_async_copy(
        panels.at[pl.ds(start, part_rows), :], out.at[0:part_rows, :], sems.at[0]
    )
    copy.start()
    fetch = pltpu.make_async_copy(scales, held, sems.at[1])
    fetch.start()
    items, shard = scales.shape
    out[part_rows : part_rows + items, :] = jnp.zeros((items, out.shape[1]), out.dtype)
    fetch.wait()
    out[part_rows : part_rows + items, 0:shard] = held[...]
    copy.wait()


def query_message_kernel(per, items, targets, queries, ids_far, positives_far, *refs):
    (*outs, ids, positives, marks, sems) = refs
    rows = queries.shape[1]
    nsel = ids.shape[1]
    reps = rows // LANES
    goal = targets()
    lists = [
        pltpu.make_async_copy(ids_far, ids, sems.at[len(outs)]),
        pltpu.make_async_copy(positives_far, positives, sems.at[len(outs) + 1]),
    ]
    for copy in lists:
        copy.start()
    copies = []
    for n, out in enumerate(outs):
        block = goal[n // per] * per + n % per
        copies.append(
            pltpu.make_async_copy(queries.at[block], out.at[0:rows, :], sems.at[n])
        )
        copies[-1].start()
    for copy in lists:
        copy.wait()
    for n, out in enumerate(outs):
        block = goal[n // per] * per + n % per
        place = positives[pl.ds(block, 1), :]
        marks[...] = jnp.zeros_like(marks)
        for c in range(reps):
            chunk = place[:, c * LANES : (c + 1) * LANES]
            marks[c : c + 1, 0:LANES] = (chunk // items).astype(jnp.float32)
            marks[c : c + 1, LANES : 2 * LANES] = (chunk % items).astype(jnp.float32)
        marks[reps : reps + 1, 0:nsel] = ids[pl.ds(block, 1), :].astype(jnp.float32)
        out[rows : rows + TILE, :] = marks[...].astype(out.dtype)
    for copy in copies:
        copy.wait()


def score_kernel(dims, *refs):
    nq, nlocal, ntow, n_piece, rows, nsel, items, slots, shard, split = dims
    refs = list(refs)

    def take(n):
        out, refs[:] = refs[:n], refs[n:]
        return out

    owner_far, ids_far, pos_far, scale_far, queries, own = take(6)
    messages = take(nq - nlocal)
    pieces = take(n_piece)
    outs = take(nq)
    (keep,) = take(1)
    sends = take(ntow - 1 if split else 0)
    (panel, scale, wide, query, score, sel, sel_wide, weight, term, back, grad, place) = refs[:12]
    (owner, ids, far_ids, moved_ids, pos_own, scale_own, sems) = refs[12:]
    part = shard // ntow
    cand = nsel * items
    width = panel.shape[1]
    mine, blk_me, tow_me = lax.axis_index("group"), lax.axis_index("blk"), lax.axis_index("tower")
    blk_to = [to for _, to, _ in peers("blk")]
    tow_to = [to for _, to, _ in peers("tower")]
    copies = []

    def fetch(source, target):
        copies.append(pltpu.make_async_copy(source, target, sems.at[len(copies)]))
        copies[-1].start()
        return copies[-1]

    def rows_at(slot, count):
        return pl.ds(pl.multiple_of(slot * items, TILE), count * items)

    early = [fetch(ids_far, ids), fetch(owner_far, owner)]
    early.append(fetch(scale_far, scale_own))
    early.append(fetch(pos_far, pos_own))
    early.append(fetch(own, panel.at[rows_at(blk_me * shard, shard), :]))
    for n, piece in enumerate(pieces):
        first = blk_to[n // ntow] * shard + ([tow_me] + tow_to)[n % ntow] * part
        held = piece.at[0 : part * items, :]
        early.append(fetch(held, panel.at[rows_at(first, part), :]))
        if n % ntow == 0:
            held = piece.at[part * items : part * items + items, 0:LANES]
            early.append(fetch(held, scale.at[n // ntow]))
    blocks = []
    for n in range(nlocal):
        blocks.append(fetch(queries.at[mine * nlocal + n], query.at[n, 0:rows, :]))
    for n, message in enumerate(messages):
        blocks.append(fetch(message, query.at[nlocal + n]))
    grad[...] = jnp.zeros_like(grad)
    for copy in early:
        copy.wait()

    reps = rows // LANES
    moved = []

    def arrive(b):
        blocks[b].wait()
        if b < nlocal:
            place[b] = jnp.broadcast_to(pos_own[pl.ds(mine * nlocal + b, 1), :], (8, rows))
            return
        marks = query[b, rows : rows + TILE, :].astype(jnp.float32)
        found = [
            marks[n : n + 1, 0:LANES] * items + marks[n : n + 1, LANES : 2 * LANES]
            for n in range(reps)
        ]
        found = jnp.concatenate(found, axis=1).astype(jnp.int32)
        place[b] = jnp.broadcast_to(found, (8, rows))
        moved_ids[b] = jnp.broadcast_to(marks[reps : reps + 1, 0:LANES], (8, LANES)).astype(
            jnp.int32
        )
        moved.append(fetch(moved_ids.at[b], far_ids.at[b]))

    def slot_of(b, j):
        if b < nlocal:
            return owner[0, ids[mine * nlocal + b, j]]
        return owner[0, far_ids[b, 0, j]]

    item_of = lax.broadcasted_iota(jnp.int32, (shard * items, items), 0) % items
    spread = item_of == lax.broadcasted_iota(jnp.int32, (shard * items, items), 1)
    spread = spread.astype(jnp.bfloat16)

    def widen(values, at):
        lanes = values.shape[1]
        of_item = jnp.dot(spread, values, preferred_element_type=jnp.float32)
        slot_of = lax.broadcasted_iota(jnp.int32, (shard * items, lanes), 0) // items
        mine = slot_of == lax.broadcasted_iota(jnp.int32, (shard * items, lanes), 1)
        wide[at, :] = jnp.dot(
            jnp.where(mine, of_item, 0.0).astype(jnp.bfloat16),
            jnp.ones((lanes, LANES), jnp.bfloat16),
            preferred_element_type=jnp.float32,
        ) * (1.0 / LN2)

    widen(scale_own[...], rows_at(blk_me * shard, shard))
    for n, to in enumerate(blk_to):
        widen(scale[n], rows_at(to * shard, shard))

    line = lax.broadcasted_iota(jnp.int32, (8, rows), 0)
    state = [{} for _ in range(nq)]

    def gather(b):
        two = b % 2
        for j in range(nsel):
            at = slice(j * items, (j + 1) * items)
            slot = rows_at(slot_of(b, j), 1)
            sel[two, at, :] = panel[slot, :]
            sel_wide[two, at, :] = wide[slot, :]

    def scores(b):
        score[b % 2] = lax.dot_general(
            sel[b % 2],
            query[b, 0:rows, :],
            (((1,), (1,)), ((), ())),
            preferred_element_type=jnp.float32,
        )

    def spread_scale(two, first):
        return jnp.tile(sel_wide[two, first : first + 8, :], (1, reps))

    def peaks(b):
        two = b % 2
        peak = jnp.full((8, rows), -jnp.inf, jnp.float32)
        for first in range(0, cand, 8):
            s = score[two, first : first + 8, :] * spread_scale(two, first)
            score[two, first : first + 8, :] = s
            peak = jnp.maximum(peak, s)
        state[b]["top"] = jnp.max(peak, axis=0, keepdims=True)

    def exps(b):
        two, top, pos = b % 2, state[b]["top"], place[b]
        total = jnp.zeros((8, rows), jnp.float32)
        pick = jnp.zeros((8, rows), jnp.float32)
        for first in range(0, cand, 8):
            s = score[two, first : first + 8, :]
            e = jnp.exp2(s - top)
            score[two, first : first + 8, :] = e
            total = total + e
            pick = jnp.where(line == pos - first, s, pick)
        total = jnp.sum(total, axis=0, keepdims=True)
        picked = jnp.sum(pick, axis=0, keepdims=True)
        loss = (top - picked) * LN2 + jnp.log(total)
        state[b]["inverse"] = LN2 / total
        row_of = lax.broadcasted_iota(jnp.int32, (TILE, LANES), 0)
        below = jnp.zeros((TILE, LANES), jnp.float32)
        for n in range(reps):
            below = jnp.where(row_of == n, loss[:, n * LANES : (n + 1) * LANES], below)
        back[b, rows : rows + TILE, :] = jnp.zeros((TILE, width), jnp.bfloat16)
        back[b, rows : rows + TILE, 0:LANES] = below.astype(jnp.bfloat16)

    def weigh(b):
        two, inverse, pos = b % 2, state[b]["inverse"], place[b]
        for start in range(0, cand, TILE):
            halves = []
            for first in range(start, start + TILE, 8):
                chance = score[two, first : first + 8, :] * inverse
                chance = jnp.where(line == pos - first, chance - LN2, chance)
                halves.append(chance * spread_scale(two, first))
            weight[two, start : start + TILE, :] = jnp.concatenate(halves, axis=0).astype(
                jnp.bfloat16
            )

    def panel_terms(b):
        term[b % 2] = jnp.dot(
            weight[b % 2], query[b, 0:rows, :], preferred_element_type=jnp.float32
        )

    def scatter(b):
        for j in range(nsel):
            slot = slot_of(b, j)
            add = term[b % 2, j * items : (j + 1) * items, :]
            if split:
                grad[slot] += add.reshape(ntow, items // ntow, width)
            else:
                grad[rows_at(slot, 1), :] += add

    def query_terms(b):
        back[b, 0:rows, :] = lax.dot_general(
            weight[b % 2],
            sel[b % 2],
            (((0,), (0,)), ((), ())),
            preferred_element_type=jnp.float32,
        ).astype(jnp.bfloat16)
        leaves.append(pltpu.make_async_copy(back.at[b], outs[b], sems.at[sems.shape[0] - nq + b]))
        leaves[-1].start()

    leaves = []
    def ready(b):
        if b == 0:
            arrive(0)
        if b == 1:
            for n in range(1, nq):
                arrive(n)
            for copy in moved:
                copy.wait()

    jobs = dict(r=ready, g=gather, s=scores, p=peaks, e=exps, w=weigh, t=panel_terms, a=scatter, q=query_terms)
    for name, shift in ORDER[0]:
        if shift < nq:
            jobs[name](shift)
    for b in range(nq):
        for name, shift in ORDER[1]:
            if 0 <= b + shift < nq:
                jobs[name](b + shift)
    for name, shift in ORDER[2]:
        jobs[name](nq - 1 + shift)
    if split:
        keep[...] = grad[:, tow_me].reshape(keep.shape)
        for to, send in zip([to for to, _, _ in peers("tower")], sends):
            send[...] = grad[:, to].reshape(send.shape).astype(send.dtype)
    else:
        keep[...] = grad[...]
    for copy in leaves:
        copy.wait()


def tower_sum_kernel(nblk, partners, keep, *refs):
    got, outs = refs[: len(refs) - nblk], refs[len(refs) - nblk :]
    me, to = partners()
    rows = keep.shape[0] // nblk
    for owner, out in zip([me] + to, outs):
        at = pl.ds(pl.multiple_of(owner * rows, TILE), rows)
        total = keep[at, :]
        for term in got:
            total = total + term[at, :].astype(jnp.float32)
        out[...] = total.astype(out.dtype)


def shard_sum_kernel(own, *refs):
    total = own[...]
    for term in refs[:-1]:
        total = total + term[...].astype(jnp.float32)
    refs[-1][...] = total


def home_kernel(per, partners, *refs):
    (*blocks, grads, losses, sems) = refs
    nq, rows, _ = grads.shape
    me, to = partners()
    copies = []
    lines = lax.broadcasted_iota(jnp.int32, (nq, LANES), 0)
    parts = [jnp.zeros((nq, LANES), jnp.float32)] * (rows // LANES)
    for n, block in enumerate(blocks):
        place = ([me] + to)[n // per] * per + n % per
        copies.append(
            pltpu.make_async_copy(block.at[0:rows, :], grads.at[place], sems.at[n])
        )
        copies[-1].start()
    for n, block in enumerate(blocks):
        place = ([me] + to)[n // per] * per + n % per
        tile = block[rows : rows + TILE, 0:LANES].astype(jnp.float32)
        parts = [jnp.where(lines == place, tile[c : c + 1, :], p) for c, p in enumerate(parts)]
    losses[...] = jnp.concatenate(parts, axis=1).astype(losses.dtype)
    for copy in copies:
        copy.wait()


def shards(queries, cluster_ids, positives, owner_map, panels, scales):
    nq, rows, width = queries.shape
    shard, items = scales.shape
    nsel = cluster_ids.shape[1]
    nblk, ntow = lax.axis_size("blk"), lax.axis_size("tower")
    slots = shard * nblk
    part = shard // ntow
    cand = nsel * items
    ngroup = lax.axis_size("group")
    mine, blk_me, tow_me = lax.axis_index("group"), lax.axis_index("blk"), lax.axis_index("tower")
    group_peers, blk_peers, tow_peers = peers("group"), peers("blk"), peers("tower")
    per = nq // ngroup
    split = (items // ntow) % 8 == 0
    vmem = pl.BlockSpec(memory_space=pltpu.VMEM)
    hbm = pl.BlockSpec(memory_space=pltpu.HBM)
    where = pl.BlockSpec(memory_space=pl.ANY)
    pin = functools.partial(pltpu.with_memory_space_constraint, memory_space=pltpu.HBM)
    params = pltpu.CompilerParams(vmem_limit_bytes=VMEM_LIMIT)
    flat_panels = panels.reshape(shard * items, width)
    flat_scales = scales.T

    message = pl.pallas_call(
        functools.partial(panel_message_kernel, part * items),
        out_shape=jax.ShapeDtypeStruct((part * items + items, width), panels.dtype),
        in_specs=[hbm, hbm],
        out_specs=vmem,
        scratch_shapes=[
            pltpu.VMEM((items, shard), scales.dtype),
            pltpu.SemaphoreType.DMA((2,)),
        ],
        compiler_params=params,
        name="panel_message",
    )(pin(flat_panels), pin(flat_scales))
    pieces = []
    for to, source, pattern in blk_peers:
        piece = lax.ppermute(message, "blk", pattern)
        pieces.append(piece)
        for _, tow_source, tow_pattern in tow_peers:
            pieces.append(lax.ppermute(piece, "tower", tow_pattern))

    def targets():
        return [to for to, _, _ in peers("group")]

    leaving = pl.pallas_call(
        functools.partial(query_message_kernel, per, items, targets),
        out_shape=[jax.ShapeDtypeStruct((rows + TILE, width), queries.dtype)] * (nq - per),
        in_specs=[hbm, hbm, hbm],
        out_specs=[vmem] * (nq - per),
        scratch_shapes=[
            pltpu.VMEM(cluster_ids.shape, jnp.int32),
            pltpu.VMEM(positives.shape, jnp.int32),
            pltpu.VMEM((TILE, width), jnp.float32),
            pltpu.SemaphoreType.DMA((nq - per + 2,)),
        ],
        compiler_params=params,
        name="query_message",
    )(pin(queries), pin(cluster_ids), pin(positives))
    arrived = [
        lax.ppermute(leaving[n * per + i], "group", pattern)
        for n, (_, _, pattern) in enumerate(group_peers)
        for i in range(per)
    ]
    dims = (nq, per, ntow, len(pieces), rows, nsel, items, slots, shard, split)
    sent_rows = slots * items // ntow
    keep_rows = sent_rows if split else slots * items
    n_send = ntow - 1 if split else 0
    grad_shape = (slots, ntow, items // ntow, width) if split else (slots * items, width)
    results = pl.pallas_call(
        functools.partial(score_kernel, dims),
        out_shape=[pltpu.HBM((rows + TILE, width), jnp.bfloat16)] * nq
        + [pltpu.VMEM((keep_rows, width), jnp.float32)]
        + [pltpu.VMEM((sent_rows, width), jnp.bfloat16)] * n_send,
        in_specs=[hbm] * 6 + [where] * (nq - per + len(pieces)),
        out_specs=[hbm] * nq + [vmem] * (1 + n_send),
        scratch_shapes=[
            pltpu.VMEM((slots * items, width), jnp.bfloat16),
            pltpu.VMEM((max(nblk - 1, 1), items, LANES), jnp.bfloat16),
            pltpu.VMEM((slots * items, LANES), jnp.float32),
            pltpu.VMEM((nq, rows + TILE, width), jnp.bfloat16),
            pltpu.VMEM((2, cand, rows), jnp.float32),
            pltpu.VMEM((2, cand, width), jnp.bfloat16),
            pltpu.VMEM((2, cand, LANES), jnp.float32),
            pltpu.VMEM((2, cand, rows), jnp.bfloat16),
            pltpu.VMEM((2, cand, width), jnp.float32),
            pltpu.VMEM((nq, rows + TILE, width), jnp.bfloat16),
            pltpu.VMEM(grad_shape, jnp.float32),
            pltpu.VMEM((nq, 8, rows), jnp.int32),
            pltpu.SMEM(owner_map.shape, jnp.int32),
            pltpu.SMEM(cluster_ids.shape, jnp.int32),
            pltpu.SMEM((nq, 8, LANES), jnp.int32),
            pltpu.VMEM((nq, 8, LANES), jnp.int32),
            pltpu.VMEM(positives.shape, jnp.int32),
            pltpu.VMEM(flat_scales.shape, flat_scales.dtype),
            pltpu.SemaphoreType.DMA((5 + len(pieces) + (nblk - 1) + 3 * nq,)),
        ],
        compiler_params=params,
        name="score",
    )(
        pin(owner_map),
        pin(cluster_ids),
        pin(positives),
        pin(flat_scales),
        pin(queries),
        pin(flat_panels),
        *arrived,
        *pieces,
    )
    query_grads, keep, sends = results[:nq], results[nq], results[nq + 1 :]

    def partners(axis):
        return lax.axis_index(axis), [to for to, _, _ in peers(axis)]

    shard_rows = shard * items // ntow
    if split:
        got = [lax.ppermute(sent, "tower", p) for sent, (_, _, p) in zip(sends, tow_peers)]
        own, *leaving = pl.pallas_call(
            functools.partial(tower_sum_kernel, nblk, functools.partial(partners, "blk")),
            out_shape=[pltpu.VMEM((shard_rows, width), jnp.float32)]
            + [pltpu.VMEM((shard_rows, width), jnp.bfloat16)] * (nblk - 1),
            in_specs=[vmem] * (1 + len(got)),
            out_specs=[vmem] * nblk,
            compiler_params=params,
            name="tower_sum",
        )(keep, *got)
    else:
        by_part = keep.reshape(slots, ntow, items // ntow, width)
        total = lax.dynamic_index_in_dim(by_part, tow_me, 1, keepdims=False)
        for to, _, pattern in tow_peers:
            sent = lax.dynamic_index_in_dim(by_part, to, 1, keepdims=False)
            sent = sent.astype(jnp.bfloat16)
            total = total + lax.ppermute(sent, "tower", pattern).astype(jnp.float32)
        total = total.reshape(nblk, shard_rows, width)
        own = pick(total, blk_me)
        leaving = [pick(total, to).astype(jnp.bfloat16) for to, _, _ in blk_peers]
    own, *rest = lax.optimization_barrier((own, *leaving, *query_grads))
    leaving, query_grads = rest[: nblk - 1], rest[nblk - 1 :]
    terms = [lax.ppermute(sent, "blk", p) for sent, (_, _, p) in zip(leaving, blk_peers)]
    panel_grads = pl.pallas_call(
        shard_sum_kernel,
        out_shape=jax.ShapeDtypeStruct((shard_rows, width), jnp.float32),
        in_specs=[vmem] * nblk,
        out_specs=vmem,
        compiler_params=params,
        cost_estimate=pl.CostEstimate(flops=10**9, bytes_accessed=10**7, transcendentals=0),
        name="shard_sum",
    )(own, *terms).reshape(shard, items // ntow, width)

    blocks = list(query_grads[:per])
    for n, (to, _, pattern) in enumerate(group_peers):
        home = [(d, s) for s, d in pattern]
        for block in query_grads[(n + 1) * per : (n + 2) * per]:
            blocks.append(lax.ppermute(block, "group", home))
    back_q, back_l = pl.pallas_call(
        functools.partial(home_kernel, per, functools.partial(partners, "group")),
        out_shape=[
            pltpu.HBM((nq, rows, width), jnp.bfloat16),
            jax.ShapeDtypeStruct((nq, rows), jnp.bfloat16),
        ],
        in_specs=[vmem] * nq,
        out_specs=[hbm, vmem],
        scratch_shapes=[pltpu.SemaphoreType.DMA((nq,))],
        compiler_params=params,
        name="home",
    )(*blocks)
    return back_l, back_q, panel_grads


def solution(mesh):
    return jax.shard_map(
        shards,
        mesh=mesh,
        in_specs=(
            P(("tower", "group", "blk"), None, None),
            P(("tower", "group", "blk"), None),
            P(("tower", "group", "blk"), None),
            P("group", None),
            P(("group", "blk"), None, None),
            P(("group", "blk"), None),
        ),
        out_specs=(
            P(("tower", "group", "blk"), None),
            P(("tower", "group", "blk"), None, None),
            P(("group", "blk"), "tower", None),
        ),
        check_vma=False,
    )
```

time: 62.1 us -> 53.1 us (0.86)
  local copies, waits for them, and re-layouts: 11.7 us -> 0.02 us
  starting transfers between devices: 18.2 us -> 22.4 us
  Pallas kernels: 12.3 us -> 15.5 us
  other arithmetic: 3.05 us -> 0 us
  waiting for transfers between devices: 15.7 us -> 14.4 us
    unnamed x50 -> x8, local copies, waits for them, and re-layouts: 10.1 us -> 0.02 us
    ppermute x7, starting transfers between devices: 8.34 us -> 11.4 us  [the longest x3 5.77 us: shards(): lax.ppermute(sent, 'blk', p)]
    add x2 -> x0, other arithmetic: 2.8 us -> none  [the longest x1 1.72 us: shards(): panel_grads + lax.ppermute(sent, 'blk', pattern).astype(jnp.float32)]
    pallas_call x1 -> x4, Pallas kernels: 11.3 us -> 13.3 us  [the longest x1 11 us: shards(): pl.pallas_call(functools.partial(score_kernel, dims), out_shape=[pltpu.HB...]
    convert_element_type x1 -> x0, local copies, waits for them, and re-layouts: 1.2 us -> none  [shards(): sent = pick(by_shard, to).astype(jnp.bfloat16)]
    ppermute x3, starting transfers between devices: 3.62 us -> 4.54 us  [shards(): lax.ppermute(leaving[n * per + i], 'group', pattern)]
    ppermute x3, waiting for transfers between devices: 2.2 us -> 1.34 us  [shards(): lax.ppermute(leaving[n * per + i], 'group', pattern)]
    pallas_call x1, Pallas kernels: 0.17 us -> 0.93 us  [shards(): pl.pallas_call(functools.partial(panel_message_kernel, part * items), out...]
  transfers between devices with their start and end apart: 16 -> 16, of which waited for: 7 -> 6; matrix products, arithmetic and copies ran while one was open for 4% -> 0% of each run, Pallas kernels for 1% -> 4%
where the time goes in v3:
time: 53.1 us; the launch traced here: 53 us
  starting transfers between devices  22.4 us (42%)
  Pallas kernels  15.5 us (29%)
  waiting for transfers between devices  14.4 us (27%)
  between operations  0.7 us (1%)
    pallas_call x1, Pallas kernels, shards(): pl.pallas_call(functools.partial(score_kernel, dims), out_shape=[pltpu.HB...  11 us
    ppermute x3, starting transfers between devices, shards(): piece = lax.ppermute(message, 'blk', pattern)  5.9 us
    ppermute x3, starting transfers between devices, shards(): lax.ppermute(sent, 'blk', p)  5.77 us
    ppermute x3, starting transfers between devices, shards(): blocks.append(lax.ppermute(block, 'group', home))  5.47 us
    ppermute x3, waiting for transfers between devices, shards(): piece = lax.ppermute(message, 'blk', pattern)  5.25 us
    ppermute x3, waiting for transfers between devices, shards(): lax.ppermute(sent, 'blk', p)  4.98 us
    ppermute x3, starting transfers between devices, shards(): lax.ppermute(leaving[n * per + i], 'group', pattern)  4.54 us
    ppermute x1, waiting for transfers between devices, shards(): lax.ppermute(sent, 'tower', p)  1.84 us
  transfers between devices with their start and end apart: 16, of which 6 were waited for; matrix products, arithmetic and copies ran while one was open for 0% of the time, Pallas kernels for 4%

profile of v3, /device:TPU:0, one launch (start us, length us, event | category | flops | bytes accessed | tf_op | source)
XLA Modules:
  0.0 53.0 jit_solution(10986781127889210080)
XLA Ops:
  0.6 0.9 %panel_message.1 = bf16[272,256]{1,0:T(8,128)(2,1)S(1)} custom-call(bf16[512,256]{1,0:T(8,128)(2,1)} %bitcast.3, bf16[16,32]{1,0:T(8,128)(2,1)} %bitcast.5), custom_call_target="tpu_custom_call" | custom-call | tf_op jit(solution)/shard_map/panel_message/pallas_call | solution.py:363
  1.6 5.1 %collective-permute-start.7 = (bf16[272,256]{1,0:T(8,128)(2,1)S(1)}, bf16[272,256]{1,0:T(8,128)(2,1)S(1)}, u32[]{:S(2)}, u32[]{:S(2)}) collective-permute-start(bf16[272,256]{1,0:T(8,128)(2,1)S(1)} %panel_message.1), channel_id=1, source_target_pairs={{0,3},{1,2},{2,1},{3,0},{4,7},{5,6},{6,5},{7,4},{8,11},{9,10},{10,... | collective-permute-start | bytes 417800 | tf_op jit(solution)/shard_map/ppermute | solution.py:377
  6.7 1.2 %query_message.1 = (bf16[400,256]{1,0:T(8,128)(2,1)S(1)}, bf16[400,256]{1,0:T(8,128)(2,1)S(1)}, bf16[400,256]{1,0:T(8,128)(2,1)S(1)}) custom-call(bf16[4,384,256]{2,1,0:T(8,128)(2,1)} %refs_4_.1, s32[4,64]{1,0:T(4,128)} %refs_1_.1, s32[4,384]{1,0:T(4,128)} %refs_2_.1), custom_call_target="tpu_custom_call" | custom-call | tf_op jit(solution)/shard_map/query_message/pallas_call | solution.py:385
  7.9 1.6 %collective-permute-start = (bf16[400,256]{1,0:T(8,128)(2,1)S(1)}, bf16[400,256]{1,0:T(8,128)(2,1)S(1)}, u32[]{:S(2)}, u32[]{:S(2)}) collective-permute-start(bf16[400,256]{1,0:T(8,128)(2,1)S(1)} %get-tuple-element.26), channel_id=1, source_target_pairs={{0,4},{4,0},{8,12},{12,8},{1,5},{5,1},{9,13},{13,9},{2,6},{6,2},{1... | collective-permute-start | bytes 614408 | tf_op jit(solution)/shard_map/ppermute | solution.py:400
  9.4 0.0 collective-permute-start.5
  9.4 0.8 %collective-permute-start.3 = (bf16[272,256]{1,0:T(8,128)(2,1)S(1)}, bf16[272,256]{1,0:T(8,128)(2,1)S(1)}, u32[]{:S(2)}, u32[]{:S(2)}) collective-permute-start(bf16[272,256]{1,0:T(8,128)(2,1)S(1)} %panel_message.1), channel_id=1, source_target_pairs={{0,1},{1,0},{2,3},{3,2},{4,5},{5,4},{6,7},{7,6},{8,9},{9,8},{10,11... | collective-permute-start | bytes 417800 | tf_op jit(solution)/shard_map/ppermute | solution.py:377
  10.2 1.5 %collective-permute-start.1 = (bf16[400,256]{1,0:T(8,128)(2,1)S(1)}, bf16[400,256]{1,0:T(8,128)(2,1)S(1)}, u32[]{:S(2)}, u32[]{:S(2)}) collective-permute-start(bf16[400,256]{1,0:T(8,128)(2,1)S(1)} %get-tuple-element.27), channel_id=1, source_target_pairs={{0,8},{4,12},{8,0},{12,4},{1,9},{5,13},{9,1},{13,5},{2,10},{6,14},... | collective-permute-start | bytes 614408 | tf_op jit(solution)/shard_map/ppermute | solution.py:400
  11.7 0.0 collective-permute-done.7.refs_13_
  11.7 1.5 %collective-permute-start.2 = (bf16[400,256]{1,0:T(8,128)(2,1)S(1)}, bf16[400,256]{1,0:T(8,128)(2,1)S(1)}, u32[]{:S(2)}, u32[]{:S(2)}) collective-permute-start(bf16[400,256]{1,0:T(8,128)(2,1)S(1)} %get-tuple-element.28), channel_id=1, source_target_pairs={{0,12},{4,8},{8,4},{12,0},{1,13},{5,9},{9,5},{13,1},{2,14},{6,10},... | collective-permute-start | bytes 614408 | tf_op jit(solution)/shard_map/ppermute | solution.py:400
  13.2 5.2 %collective-permute-done.5.refs_11_ = bf16[272,256]{1,0:T(8,128)(2,1)S(1)} collective-permute-done((bf16[272,256]{1,0:T(8,128)(2,1)S(1)}, bf16[272,256]{1,0:T(8,128)(2,1)S(1)}, u32[]{:S(2)}, u32[]{:S(2)}) %collective-permute-start.5) | collective-permute-done | bytes 139296 | tf_op jit(solution)/shard_map/ppermute | solution.py:377
  18.5 0.5 collective-permute-start.6
  19.0 0.1 collective-permute-start.4
  19.1 1.3 %collective-permute-done.1.refs_7_ = bf16[400,256]{1,0:T(8,128)(2,1)S(1)} collective-permute-done((bf16[400,256]{1,0:T(8,128)(2,1)S(1)}, bf16[400,256]{1,0:T(8,128)(2,1)S(1)}, u32[]{:S(2)}, u32[]{:S(2)}) %collective-permute-start.1) | collective-permute-done | bytes 204832 | tf_op jit(solution)/shard_map/ppermute | solution.py:400
  20.4 0.0 collective-permute-done.8.refs_14_
  20.4 0.0 collective-permute-done.6.refs_12_
  20.4 0.0 collective-permute-done.4.refs_10_
  20.4 11.0 %score.1 = (bf16[400,256]{1,0:T(8,128)(2,1)}, bf16[400,256]{1,0:T(8,128)(2,1)}, bf16[400,256]{1,0:T(8,128)(2,1)}, bf16[400,256]{1,0:T(8,128)(2,1)}, f32[1024,256...) custom-call(s32[1,128]{1,0:T(1,128)} %refs_0_.1, s32[4,64]{1,0:T(4,128)} %refs_1_.1, s32[4,384]{1,0:T(4,128)} %refs_2_.1, ...), custom_call_target="tpu_custom_call" | custom-call | tf_op jit(solution)/shard_map/score/pallas_call | solution.py:409
  31.4 0.1 collective-permute-start.9
  31.5 1.8 %collective-permute-done.9.refs_0_ = bf16[1024,256]{1,0:T(8,128)(2,1)S(1)} collective-permute-done((bf16[1024,256]{1,0:T(8,128)(2,1)S(1)}, bf16[1024,256]{1,0:T(8,128)(2,1)S(1)}, u32[]{:S(2)}, u32[]{:S(2)}) %collective-permute-start.9) | collective-permute-done | bytes 524320 | tf_op jit(solution)/shard_map/ppermute | solution.py:456
  33.4 0.1 tower_sum.1
  33.5 0.0 copy-start
  33.5 3.3 %collective-permute-start.13 = (bf16[256,256]{1,0:T(8,128)(2,1)S(1)}, bf16[256,256]{1,0:T(8,128)(2,1)S(1)}, u32[]{:S(2)}, u32[]{:S(2)}) collective-permute-start(bf16[256,256]{1,0:T(8,128)(2,1)S(1)} %get-tuple-element.46), channel_id=1, source_target_pairs={{0,1},{1,0},{2,3},{3,2},{4,5},{5,4},{6,7},{7,6},{8,9},{9,8},{10,11... | collective-permute-start | bytes 393224 | tf_op jit(solution)/shard_map/ppermute | solution.py:478
  36.9 1.0 %collective-permute-start.14 = (bf16[256,256]{1,0:T(8,128)(2,1)S(1)}, bf16[256,256]{1,0:T(8,128)(2,1)S(1)}, u32[]{:S(2)}, u32[]{:S(2)}) collective-permute-start(bf16[256,256]{1,0:T(8,128)(2,1)S(1)} %get-tuple-element.47), channel_id=1, source_target_pairs={{0,2},{1,3},{2,0},{3,1},{4,6},{5,7},{6,4},{7,5},{8,10},{9,11},{10,... | collective-permute-start | bytes 393224 | tf_op jit(solution)/shard_map/ppermute | solution.py:478
  37.9 1.4 %collective-permute-start.15 = (bf16[256,256]{1,0:T(8,128)(2,1)S(1)}, bf16[256,256]{1,0:T(8,128)(2,1)S(1)}, u32[]{:S(2)}, u32[]{:S(2)}) collective-permute-start(bf16[256,256]{1,0:T(8,128)(2,1)S(1)} %get-tuple-element.48), channel_id=1, source_target_pairs={{0,3},{1,2},{2,1},{3,0},{4,7},{5,6},{6,5},{7,4},{8,11},{9,10},{10,... | collective-permute-start | bytes 393224 | tf_op jit(solution)/shard_map/ppermute | solution.py:478
  39.3 1.5 %collective-permute-start.10 = (bf16[400,256]{1,0:T(8,128)(2,1)S(1)}, bf16[400,256]{1,0:T(8,128)(2,1)S(1)}, u32[]{:S(2)}, u32[]{:S(2)}) collective-permute-start(bf16[400,256]{1,0:T(8,128)(2,1)S(1)} %copy-done.3), channel_id=1, source_target_pairs={{4,0},{0,4},{12,8},{8,12},{5,1},{1,5},{13,9},{9,13},{6,2},{2,6},{1... | collective-permute-start | bytes 614408 | tf_op jit(solution)/shard_map/ppermute | solution.py:493
  40.8 1.5 %collective-permute-start.11 = (bf16[400,256]{1,0:T(8,128)(2,1)S(1)}, bf16[400,256]{1,0:T(8,128)(2,1)S(1)}, u32[]{:S(2)}, u32[]{:S(2)}) collective-permute-start(bf16[400,256]{1,0:T(8,128)(2,1)S(1)} %copy-done.2), channel_id=1, source_target_pairs={{8,0},{12,4},{0,8},{4,12},{9,1},{13,5},{1,9},{5,13},{10,2},{14,6},... | collective-permute-start | bytes 614408 | tf_op jit(solution)/shard_map/ppermute | solution.py:493
  42.3 0.2 collective-permute-done.13.refs_0_
  42.5 2.5 %collective-permute-start.12 = (bf16[400,256]{1,0:T(8,128)(2,1)S(1)}, bf16[400,256]{1,0:T(8,128)(2,1)S(1)}, u32[]{:S(2)}, u32[]{:S(2)}) collective-permute-start(bf16[400,256]{1,0:T(8,128)(2,1)S(1)} %copy-done.1), channel_id=1, source_target_pairs={{12,0},{8,4},{4,8},{0,12},{13,1},{9,5},{5,9},{1,13},{14,2},{10,6},... | collective-permute-start | bytes 614408 | tf_op jit(solution)/shard_map/ppermute | solution.py:493
  45.0 4.8 %collective-permute-done.14.refs_1_ = bf16[256,256]{1,0:T(8,128)(2,1)S(1)} collective-permute-done((bf16[256,256]{1,0:T(8,128)(2,1)S(1)}, bf16[256,256]{1,0:T(8,128)(2,1)S(1)}, u32[]{:S(2)}, u32[]{:S(2)}) %collective-permute-start.14) | collective-permute-done | bytes 131104 | tf_op jit(solution)/shard_map/ppermute | solution.py:478
  49.8 0.8 %shard_sum.1 = f32[256,256]{1,0:T(8,128)} custom-call(f32[256,256]{1,0:T(8,128)S(1)} %get-tuple-element.45.own, bf16[256,256]{1,0:T(8,128)(2,1)S(1)} %collective-permute-done.13.refs_0_, bf16[256,256]{1,0:T(8,128)(2,1)S(1)} %collective-permute-done.14.refs_1_, bf16[256,256]{1,0:T(8,128)(2,1)S(1)} %collective-permute-done.15.refs_2_), custom_call_target="tpu_custom_call" | custom-call | flops 1000000000 | bytes 10000000 | tf_op jit(solution)/shard_map/shard_sum/pallas_call | solution.py:479
  50.5 0.9 %collective-permute-done.11.refs_2_ = bf16[400,256]{1,0:T(8,128)(2,1)S(1)} collective-permute-done((bf16[400,256]{1,0:T(8,128)(2,1)S(1)}, bf16[400,256]{1,0:T(8,128)(2,1)S(1)}, u32[]{:S(2)}, u32[]{:S(2)}) %collective-permute-start.11) | collective-permute-done | bytes 204832 | tf_op jit(solution)/shard_map/ppermute | solution.py:493
  51.5 1.5 %home.1 = (bf16[4,384,256]{2,1,0:T(8,128)(2,1)}, bf16[4,384]{1,0:T(4,128)(2,1)}) custom-call(bf16[400,256]{1,0:T(8,128)(2,1)S(1)} %copy-done, bf16[400,256]{1,0:T(8,128)(2,1)S(1)} %collective-permute-done.10.refs_1_, bf16[400,256]{1,0:T(8,128)(2,1)S(1)} %collective-permute-done.11.refs_2_, bf16[400,256]{1,0:T(8,128)(2,1)S(1)} %collective-permute-done.12.refs_3_), custom_call_target="tpu_custom_call" | custom-call | tf_op jit(solution)/shard_map/home/pallas_call | solution.py:494
  (14 shorter events, 0.0 us)
Async XLA Ops:
  1.6 10.2 %collective-permute-start.7 = (bf16[272,256]{1,0:T(8,128)(2,1)S(1)}, bf16[272,256]{1,0:T(8,128)(2,1)S(1)}, u32[]{:S(2)}, u32[]{:S(2)}) collective-permute-start(bf16[272,256]{1,0:T(8,128)(2,1)S(1)} %panel_message.1), channel_id=1, source_target_pairs={{0,3},{1,2},{2,1},{3,0},{4,7},{5,6},{6,5},{7,4},{8,11},{9,10},{10,... | collective-permute-start | bytes 417800 | tf_op jit(solution)/shard_map/ppermute | solution.py:377
  7.9 11.1 %collective-permute-start = (bf16[400,256]{1,0:T(8,128)(2,1)S(1)}, bf16[400,256]{1,0:T(8,128)(2,1)S(1)}, u32[]{:S(2)}, u32[]{:S(2)}) collective-permute-start(bf16[400,256]{1,0:T(8,128)(2,1)S(1)} %get-tuple-element.26), channel_id=1, source_target_pairs={{0,4},{4,0},{8,12},{12,8},{1,5},{5,1},{9,13},{13,9},{2,6},{6,2},{1... | collective-permute-start | bytes 614408 | tf_op jit(solution)/shard_map/ppermute | solution.py:400
  9.4 9.0 %collective-permute-start.5 = (bf16[272,256]{1,0:T(8,128)(2,1)S(1)}, bf16[272,256]{1,0:T(8,128)(2,1)S(1)}, u32[]{:S(2)}, u32[]{:S(2)}) collective-permute-start(bf16[272,256]{1,0:T(8,128)(2,1)S(1)} %panel_message.1), channel_id=1, source_target_pairs={{0,2},{1,3},{2,0},{3,1},{4,6},{5,7},{6,4},{7,5},{8,10},{9,11},{10,... | collective-permute-start | bytes 417800 | tf_op jit(solution)/shard_map/ppermute | solution.py:377
  9.4 9.0 %collective-permute-start.3 = (bf16[272,256]{1,0:T(8,128)(2,1)S(1)}, bf16[272,256]{1,0:T(8,128)(2,1)S(1)}, u32[]{:S(2)}, u32[]{:S(2)}) collective-permute-start(bf16[272,256]{1,0:T(8,128)(2,1)S(1)} %panel_message.1), channel_id=1, source_target_pairs={{0,1},{1,0},{2,3},{3,2},{4,5},{5,4},{6,7},{7,6},{8,9},{9,8},{10,11... | collective-permute-start | bytes 417800 | tf_op jit(solution)/shard_map/ppermute | solution.py:377
  10.2 10.2 %collective-permute-start.1 = (bf16[400,256]{1,0:T(8,128)(2,1)S(1)}, bf16[400,256]{1,0:T(8,128)(2,1)S(1)}, u32[]{:S(2)}, u32[]{:S(2)}) collective-permute-start(bf16[400,256]{1,0:T(8,128)(2,1)S(1)} %get-tuple-element.27), channel_id=1, source_target_pairs={{0,8},{4,12},{8,0},{12,4},{1,9},{5,13},{9,1},{13,5},{2,10},{6,14},... | collective-permute-start | bytes 614408 | tf_op jit(solution)/shard_map/ppermute | solution.py:400
  11.7 8.6 %collective-permute-start.2 = (bf16[400,256]{1,0:T(8,128)(2,1)S(1)}, bf16[400,256]{1,0:T(8,128)(2,1)S(1)}, u32[]{:S(2)}, u32[]{:S(2)}) collective-permute-start(bf16[400,256]{1,0:T(8,128)(2,1)S(1)} %get-tuple-element.28), channel_id=1, source_target_pairs={{0,12},{4,8},{8,4},{12,0},{1,13},{5,9},{9,5},{13,1},{2,14},{6,10},... | collective-permute-start | bytes 614408 | tf_op jit(solution)/shard_map/ppermute | solution.py:400
  18.5 1.9 %collective-permute-start.8 = (bf16[272,256]{1,0:T(8,128)(2,1)S(1)}, bf16[272,256]{1,0:T(8,128)(2,1)S(1)}, u32[]{:S(2)}, u32[]{:S(2)}) collective-permute-start(bf16[272,256]{1,0:T(8,128)(2,1)S(1)} %collective-permute-done.7.refs_13_), channel_id=1, source_target_pairs={{0,16},{16,0},{1,17},{17,1},{2,18},{18,2},{3,19},{19,3},{4,20},{20... | collective-permute-start | bytes 417800 | tf_op jit(solution)/shard_map/ppermute | solution.py:380
  18.5 1.9 %collective-permute-start.6 = (bf16[272,256]{1,0:T(8,128)(2,1)S(1)}, bf16[272,256]{1,0:T(8,128)(2,1)S(1)}, u32[]{:S(2)}, u32[]{:S(2)}) collective-permute-start(bf16[272,256]{1,0:T(8,128)(2,1)S(1)} %collective-permute-done.5.refs_11_), channel_id=1, source_target_pairs={{0,16},{16,0},{1,17},{17,1},{2,18},{18,2},{3,19},{19,3},{4,20},{20... | collective-permute-start | bytes 417800 | tf_op jit(solution)/shard_map/ppermute | solution.py:380
  19.0 1.4 %collective-permute-start.4 = (bf16[272,256]{1,0:T(8,128)(2,1)S(1)}, bf16[272,256]{1,0:T(8,128)(2,1)S(1)}, u32[]{:S(2)}, u32[]{:S(2)}) collective-permute-start(bf16[272,256]{1,0:T(8,128)(2,1)S(1)} %collective-permute-done.3.refs_9_), channel_id=1, source_target_pairs={{0,16},{16,0},{1,17},{17,1},{2,18},{18,2},{3,19},{19,3},{4,20},{20... | collective-permute-start | bytes 417800 | tf_op jit(solution)/shard_map/ppermute | solution.py:380
  31.4 2.0 %collective-permute-start.9 = (bf16[1024,256]{1,0:T(8,128)(2,1)S(1)}, bf16[1024,256]{1,0:T(8,128)(2,1)S(1)}, u32[]{:S(2)}, u32[]{:S(2)}) collective-permute-start(bf16[1024,256]{1,0:T(8,128)(2,1)S(1)} %get-tuple-element.30), channel_id=1, source_target_pairs={{0,16},{16,0},{1,17},{17,1},{2,18},{18,2},{3,19},{19,3},{4,20},{20... | collective-permute-start | bytes 1572872 | tf_op jit(solution)/shard_map/ppermute | solution.py:456
  33.4 5.9 %copy-start.3 = (bf16[400,256]{1,0:T(8,128)(2,1)S(1)}, bf16[400,256]{1,0:T(8,128)(2,1)}, u32[]{:S(2)}) copy-start(bf16[400,256]{1,0:T(8,128)(2,1)} %get-tuple-element.40) | copy-start | bytes 614404
  33.4 7.4 %copy-start.2 = (bf16[400,256]{1,0:T(8,128)(2,1)S(1)}, bf16[400,256]{1,0:T(8,128)(2,1)}, u32[]{:S(2)}) copy-start(bf16[400,256]{1,0:T(8,128)(2,1)} %get-tuple-element.41) | copy-start | bytes 614404
  33.4 9.1 %copy-start.1 = (bf16[400,256]{1,0:T(8,128)(2,1)S(1)}, bf16[400,256]{1,0:T(8,128)(2,1)}, u32[]{:S(2)}) copy-start(bf16[400,256]{1,0:T(8,128)(2,1)} %get-tuple-element.42) | copy-start | bytes 614404
  33.5 18.0 %copy-start = (bf16[400,256]{1,0:T(8,128)(2,1)S(1)}, bf16[400,256]{1,0:T(8,128)(2,1)}, u32[]{:S(2)}) copy-start(bf16[400,256]{1,0:T(8,128)(2,1)} %get-tuple-element.39.refs_0_) | copy-start | bytes 614404
  33.5 9.0 %collective-permute-start.13 = (bf16[256,256]{1,0:T(8,128)(2,1)S(1)}, bf16[256,256]{1,0:T(8,128)(2,1)S(1)}, u32[]{:S(2)}, u32[]{:S(2)}) collective-permute-start(bf16[256,256]{1,0:T(8,128)(2,1)S(1)} %get-tuple-element.46), channel_id=1, source_target_pairs={{0,1},{1,0},{2,3},{3,2},{4,5},{5,4},{6,7},{7,6},{8,9},{9,8},{10,11... | collective-permute-start | bytes 393224 | tf_op jit(solution)/shard_map/ppermute | solution.py:478
  36.9 12.9 %collective-permute-start.14 = (bf16[256,256]{1,0:T(8,128)(2,1)S(1)}, bf16[256,256]{1,0:T(8,128)(2,1)S(1)}, u32[]{:S(2)}, u32[]{:S(2)}) collective-permute-start(bf16[256,256]{1,0:T(8,128)(2,1)S(1)} %get-tuple-element.47), channel_id=1, source_target_pairs={{0,2},{1,3},{2,0},{3,1},{4,6},{5,7},{6,4},{7,5},{8,10},{9,11},{10,... | collective-permute-start | bytes 393224 | tf_op jit(solution)/shard_map/ppermute | solution.py:478
  37.9 11.9 %collective-permute-start.15 = (bf16[256,256]{1,0:T(8,128)(2,1)S(1)}, bf16[256,256]{1,0:T(8,128)(2,1)S(1)}, u32[]{:S(2)}, u32[]{:S(2)}) collective-permute-start(bf16[256,256]{1,0:T(8,128)(2,1)S(1)} %get-tuple-element.48), channel_id=1, source_target_pairs={{0,3},{1,2},{2,1},{3,0},{4,7},{5,6},{6,5},{7,4},{8,11},{9,10},{10,... | collective-permute-start | bytes 393224 | tf_op jit(solution)/shard_map/ppermute | solution.py:478
  39.3 11.2 %collective-permute-start.10 = (bf16[400,256]{1,0:T(8,128)(2,1)S(1)}, bf16[400,256]{1,0:T(8,128)(2,1)S(1)}, u32[]{:S(2)}, u32[]{:S(2)}) collective-permute-start(bf16[400,256]{1,0:T(8,128)(2,1)S(1)} %copy-done.3), channel_id=1, source_target_pairs={{4,0},{0,4},{12,8},{8,12},{5,1},{1,5},{13,9},{9,13},{6,2},{2,6},{1... | collective-permute-start | bytes 614408 | tf_op jit(solution)/shard_map/ppermute | solution.py:493
  40.8 10.7 %collective-permute-start.11 = (bf16[400,256]{1,0:T(8,128)(2,1)S(1)}, bf16[400,256]{1,0:T(8,128)(2,1)S(1)}, u32[]{:S(2)}, u32[]{:S(2)}) collective-permute-start(bf16[400,256]{1,0:T(8,128)(2,1)S(1)} %copy-done.2), channel_id=1, source_target_pairs={{8,0},{12,4},{0,8},{4,12},{9,1},{13,5},{1,9},{5,13},{10,2},{14,6},... | collective-permute-start | bytes 614408 | tf_op jit(solution)/shard_map/ppermute | solution.py:493
  42.5 8.9 %collective-permute-start.12 = (bf16[400,256]{1,0:T(8,128)(2,1)S(1)}, bf16[400,256]{1,0:T(8,128)(2,1)S(1)}, u32[]{:S(2)}, u32[]{:S(2)}) collective-permute-start(bf16[400,256]{1,0:T(8,128)(2,1)S(1)} %copy-done.1), channel_id=1, source_target_pairs={{12,0},{8,4},{4,8},{0,12},{13,1},{9,5},{5,9},{1,13},{14,2},{10,6},... | collective-permute-start | bytes 614408 | tf_op jit(solution)/shard_map/ppermute | solution.py:493

commit v4 on v3

--- a/solution.py
+++ b/solution.py
@@ -12,7 +12,7 @@
 LANES = 128
 TILE = 16
 ORDER = (
-    (("r", 0), ("g", 0), ("s", 0), ("p", 0), ("r", 1)),
+    (("g", 0), ("s", 0), ("p", 0)),
     (("g", 1), ("s", 1), ("e", 0), ("w", 0), ("t", 0), ("p", 1), ("q", 0), ("a", 0)),
     (),
 )
@@ -98,8 +98,8 @@
     outs = take(nq)
     (keep,) = take(1)
     sends = take(ntow - 1 if split else 0)
-    (panel, scale, wide, query, score, sel, sel_wide, weight, term, back, grad, place) = refs[:12]
-    (owner, ids, far_ids, moved_ids, pos_own, scale_own, sems) = refs[12:]
+    (panel, wide, query, score, sel, sel_wide, weight, term, grad, place) = refs[:10]
+    (owner, ids, far_ids, moved_ids, pos_own, scale_own, sems) = refs[10:]
     part = shard // ntow
     cand = nsel * items
     width = panel.shape[1]
@@ -120,41 +120,33 @@
     early.append(fetch(scale_far, scale_own))
     early.append(fetch(pos_far, pos_own))
     early.append(fetch(own, panel.at[rows_at(blk_me * shard, shard), :]))
+    local = [fetch(queries.at[mine * nlocal + n], query.at[n]) for n in range(nlocal)]
     for n, piece in enumerate(pieces):
         first = blk_to[n // ntow] * shard + ([tow_me] + tow_to)[n % ntow] * part
-        held = piece.at[0 : part * items, :]
-        early.append(fetch(held, panel.at[rows_at(first, part), :]))
-        if n % ntow == 0:
-            held = piece.at[part * items : part * items + items, 0:LANES]
-            early.append(fetch(held, scale.at[n // ntow]))
-    blocks = []
-    for n in range(nlocal):
-        blocks.append(fetch(queries.at[mine * nlocal + n], query.at[n, 0:rows, :]))
-    for n, message in enumerate(messages):
-        blocks.append(fetch(message, query.at[nlocal + n]))
+        panel[rows_at(first, part), :] = piece[0 : part * items, :]
     grad[...] = jnp.zeros_like(grad)
-    for copy in early:
-        copy.wait()
+
+    def block_rows(b):
+        return query[b] if b < nlocal else messages[b - nlocal][0:rows, :]
 
     reps = rows // LANES
     moved = []
 
-    def arrive(b):
-        blocks[b].wait()
-        if b < nlocal:
-            place[b] = jnp.broadcast_to(pos_own[pl.ds(mine * nlocal + b, 1), :], (8, rows))
-            return
-        marks = query[b, rows : rows + TILE, :].astype(jnp.float32)
+    for b in range(nlocal, nq):
+        marks = messages[b - nlocal][rows : rows + TILE, :].astype(jnp.float32)
         found = [
             marks[n : n + 1, 0:LANES] * items + marks[n : n + 1, LANES : 2 * LANES]
             for n in range(reps)
         ]
         found = jnp.concatenate(found, axis=1).astype(jnp.int32)
         place[b] = jnp.broadcast_to(found, (8, rows))
-        moved_ids[b] = jnp.broadcast_to(marks[reps : reps + 1, 0:LANES], (8, LANES)).astype(
-            jnp.int32
-        )
+        far = jnp.broadcast_to(marks[reps : reps + 1, 0:LANES], (8, LANES))
+        moved_ids[b] = far.astype(jnp.int32)
         moved.append(fetch(moved_ids.at[b], far_ids.at[b]))
+    for copy in early + local + moved:
+        copy.wait()
+    for b in range(nlocal):
+        place[b] = jnp.broadcast_to(pos_own[pl.ds(mine * nlocal + b, 1), :], (8, rows))
 
     def slot_of(b, j):
         if b < nlocal:
@@ -178,7 +170,7 @@
 
     widen(scale_own[...], rows_at(blk_me * shard, shard))
     for n, to in enumerate(blk_to):
-        widen(scale[n], rows_at(to * shard, shard))
+        widen(pieces[n * ntow][part * items : part * items + items, 0:LANES], rows_at(to * shard, shard))
 
     line = lax.broadcasted_iota(jnp.int32, (8, rows), 0)
     state = [{} for _ in range(nq)]
@@ -194,7 +186,7 @@
     def scores(b):
         score[b % 2] = lax.dot_general(
             sel[b % 2],
-            query[b, 0:rows, :],
+            block_rows(b),
             (((1,), (1,)), ((), ())),
             preferred_element_type=jnp.float32,
         )
@@ -229,8 +221,8 @@
         below = jnp.zeros((TILE, LANES), jnp.float32)
         for n in range(reps):
             below = jnp.where(row_of == n, loss[:, n * LANES : (n + 1) * LANES], below)
-        back[b, rows : rows + TILE, :] = jnp.zeros((TILE, width), jnp.bfloat16)
-        back[b, rows : rows + TILE, 0:LANES] = below.astype(jnp.bfloat16)
+        outs[b][rows : rows + TILE, :] = jnp.zeros((TILE, width), jnp.bfloat16)
+        outs[b][rows : rows + TILE, 0:LANES] = below.astype(jnp.bfloat16)
 
     def weigh(b):
         two, inverse, pos = b % 2, state[b]["inverse"], place[b]
@@ -246,7 +238,7 @@
 
     def panel_terms(b):
         term[b % 2] = jnp.dot(
-            weight[b % 2], query[b, 0:rows, :], preferred_element_type=jnp.float32
+            weight[b % 2], block_rows(b), preferred_element_type=jnp.float32
         )
 
     def scatter(b):
@@ -259,26 +251,14 @@
                 grad[rows_at(slot, 1), :] += add
 
     def query_terms(b):
-        back[b, 0:rows, :] = lax.dot_general(
+        outs[b][0:rows, :] = lax.dot_general(
             weight[b % 2],
             sel[b % 2],
             (((0,), (0,)), ((), ())),
             preferred_element_type=jnp.float32,
         ).astype(jnp.bfloat16)
-        leaves.append(pltpu.make_async_copy(back.at[b], outs[b], sems.at[sems.shape[0] - nq + b]))
-        leaves[-1].start()
-
-    leaves = []
-    def ready(b):
-        if b == 0:
-            arrive(0)
-        if b == 1:
-            for n in range(1, nq):
-                arrive(n)
-            for copy in moved:
-                copy.wait()
-
-    jobs = dict(r=ready, g=gather, s=scores, p=peaks, e=exps, w=weigh, t=panel_terms, a=scatter, q=query_terms)
+
+    jobs = dict(g=gather, s=scores, p=peaks, e=exps, w=weigh, t=panel_terms, a=scatter, q=query_terms)
     for name, shift in ORDER[0]:
         if shift < nq:
             jobs[name](shift)
@@ -294,8 +274,6 @@
             send[...] = grad[:, to].reshape(send.shape).astype(send.dtype)
     else:
         keep[...] = grad[...]
-    for copy in leaves:
-        copy.wait()
 
 
 def tower_sum_kernel(nblk, partners, keep, *refs):
@@ -354,7 +332,6 @@
     split = (items // ntow) % 8 == 0
     vmem = pl.BlockSpec(memory_space=pltpu.VMEM)
     hbm = pl.BlockSpec(memory_space=pltpu.HBM)
-    where = pl.BlockSpec(memory_space=pl.ANY)
     pin = functools.partial(pltpu.with_memory_space_constraint, memory_space=pltpu.HBM)
     params = pltpu.CompilerParams(vmem_limit_bytes=VMEM_LIMIT)
     flat_panels = panels.reshape(shard * items, width)
@@ -408,22 +385,20 @@
     grad_shape = (slots, ntow, items // ntow, width) if split else (slots * items, width)
     results = pl.pallas_call(
         functools.partial(score_kernel, dims),
-        out_shape=[pltpu.HBM((rows + TILE, width), jnp.bfloat16)] * nq
+        out_shape=[pltpu.VMEM((rows + TILE, width), jnp.bfloat16)] * nq
         + [pltpu.VMEM((keep_rows, width), jnp.float32)]
         + [pltpu.VMEM((sent_rows, width), jnp.bfloat16)] * n_send,
-        in_specs=[hbm] * 6 + [where] * (nq - per + len(pieces)),
-        out_specs=[hbm] * nq + [vmem] * (1 + n_send),
+        in_specs=[hbm] * 6 + [vmem] * (nq - per + len(pieces)),
+        out_specs=[vmem] * (nq + 1 + n_send),
         scratch_shapes=[
             pltpu.VMEM((slots * items, width), jnp.bfloat16),
-            pltpu.VMEM((max(nblk - 1, 1), items, LANES), jnp.bfloat16),
             pltpu.VMEM((slots * items, LANES), jnp.float32),
-            pltpu.VMEM((nq, rows + TILE, width), jnp.bfloat16),
+            pltpu.VMEM((per, rows, width), jnp.bfloat16),
             pltpu.VMEM((2, cand, rows), jnp.float32),
             pltpu.VMEM((2, cand, width), jnp.bfloat16),
             pltpu.VMEM((2, cand, LANES), jnp.float32),
             pltpu.VMEM((2, cand, rows), jnp.bfloat16),
             pltpu.VMEM((2, cand, width), jnp.float32),
-            pltpu.VMEM((nq, rows + TILE, width), jnp.bfloat16),
             pltpu.VMEM(grad_shape, jnp.float32),
             pltpu.VMEM((nq, 8, rows), jnp.int32),
             pltpu.SMEM(owner_map.shape, jnp.int32),
@@ -432,7 +407,7 @@
             pltpu.VMEM((nq, 8, LANES), jnp.int32),
             pltpu.VMEM(positives.shape, jnp.int32),
             pltpu.VMEM(flat_scales.shape, flat_scales.dtype),
-            pltpu.SemaphoreType.DMA((5 + len(pieces) + (nblk - 1) + 3 * nq,)),
+            pltpu.SemaphoreType.DMA((5 + nq,)),
         ],
         compiler_params=params,
         name="score",
@@ -473,7 +448,7 @@
         total = total.reshape(nblk, shard_rows, width)
         own = pick(total, blk_me)
         leaving = [pick(total, to).astype(jnp.bfloat16) for to, _, _ in blk_peers]
-    own, *rest = lax.optimization_barrier((own, *leaving, *query_grads))
+    own, *rest = (own, *leaving, *query_grads)
     leaving, query_grads = rest[: nblk - 1], rest[nblk - 1 :]
     terms = [lax.ppermute(sent, "blk", p) for sent, (_, _, p) in zip(leaving, blk_peers)]
     panel_grads = pl.pallas_call(

time: 53.1 us -> 49.2 us (0.927)
  Pallas kernels: 15.5 us -> 13 us
  waiting for transfers between devices: 14.4 us -> 12.9 us
    pallas_call x1, Pallas kernels: 11 us -> 8.47 us  [shards(): pl.pallas_call(functools.partial(score_kernel, dims), out_shape=[pltpu.VM...]
    ppermute x3, starting transfers between devices: 5.77 us -> 7.76 us  [shards(): lax.ppermute(sent, 'blk', p)]
    ppermute x3, starting transfers between devices: 5.47 us -> 3.49 us  [shards(): blocks.append(lax.ppermute(block, 'group', home))]
    ppermute x1, waiting for transfers between devices: 1.84 us -> 0.01 us  [shards(): lax.ppermute(sent, 'tower', p)]
    ppermute x3, waiting for transfers between devices: 0.95 us -> 1.53 us  [shards(): blocks.append(lax.ppermute(block, 'group', home))]
  transfers between devices with their start and end apart: 16 -> 16, of which waited for: 6 -> 4; matrix products, arithmetic and copies ran while one was open for 0% -> 0% of each run, Pallas kernels for 4% -> 6%
where the time goes in v4:
time: 49.2 us; the launch traced here: 49 us
  starting transfers between devices  22.4 us (46%)
  Pallas kernels  13 us (26%)
  waiting for transfers between devices  12.9 us (26%)
  between operations  0.7 us (1%)
    pallas_call x1, Pallas kernels, shards(): pl.pallas_call(functools.partial(score_kernel, dims), out_shape=[pltpu.VM...  8.47 us
    ppermute x3, starting transfers between devices, shards(): lax.ppermute(sent, 'blk', p)  7.76 us
    ppermute x3, starting transfers between devices, shards(): piece = lax.ppermute(message, 'blk', pattern)  5.9 us
    ppermute x3, waiting for transfers between devices, shards(): piece = lax.ppermute(message, 'blk', pattern)  5.25 us
    ppermute x3, waiting for transfers between devices, shards(): lax.ppermute(sent, 'blk', p)  4.79 us
    ppermute x3, starting transfers between devices, shards(): lax.ppermute(leaving[n * per + i], 'group', pattern)  4.54 us
    ppermute x3, starting transfers between devices, shards(): blocks.append(lax.ppermute(block, 'group', home))  3.49 us
    ppermute x3, waiting for transfers between devices, shards(): blocks.append(lax.ppermute(block, 'group', home))  1.53 us
  transfers between devices with their start and end apart: 16, of which 4 were waited for; matrix products, arithmetic and copies ran while one was open for 0% of the time, Pallas kernels for 6%

profile of v4, /device:TPU:0, one launch (start us, length us, event | category | flops | bytes accessed | tf_op | source)
XLA Modules:
  0.0 49.0 jit_solution(809247928375941)
XLA Ops:
  0.6 0.9 %panel_message.1 = bf16[272,256]{1,0:T(8,128)(2,1)S(1)} custom-call(bf16[512,256]{1,0:T(8,128)(2,1)} %bitcast.3, bf16[16,32]{1,0:T(8,128)(2,1)} %bitcast.5), custom_call_target="tpu_custom_call" | custom-call | tf_op jit(solution)/shard_map/panel_message/pallas_call | solution.py:340
  1.6 5.1 %collective-permute-start.7 = (bf16[272,256]{1,0:T(8,128)(2,1)S(1)}, bf16[272,256]{1,0:T(8,128)(2,1)S(1)}, u32[]{:S(2)}, u32[]{:S(2)}) collective-permute-start(bf16[272,256]{1,0:T(8,128)(2,1)S(1)} %panel_message.1), channel_id=1, source_target_pairs={{0,3},{1,2},{2,1},{3,0},{4,7},{5,6},{6,5},{7,4},{8,11},{9,10},{10,... | collective-permute-start | bytes 417800 | tf_op jit(solution)/shard_map/ppermute | solution.py:354
  6.7 1.2 %query_message.1 = (bf16[400,256]{1,0:T(8,128)(2,1)S(1)}, bf16[400,256]{1,0:T(8,128)(2,1)S(1)}, bf16[400,256]{1,0:T(8,128)(2,1)S(1)}) custom-call(bf16[4,384,256]{2,1,0:T(8,128)(2,1)} %refs_4_.1, s32[4,64]{1,0:T(4,128)} %refs_1_.1, s32[4,384]{1,0:T(4,128)} %refs_2_.1), custom_call_target="tpu_custom_call" | custom-call | tf_op jit(solution)/shard_map/query_message/pallas_call | solution.py:362
  7.9 1.6 %collective-permute-start = (bf16[400,256]{1,0:T(8,128)(2,1)S(1)}, bf16[400,256]{1,0:T(8,128)(2,1)S(1)}, u32[]{:S(2)}, u32[]{:S(2)}) collective-permute-start(bf16[400,256]{1,0:T(8,128)(2,1)S(1)} %get-tuple-element.18), channel_id=1, source_target_pairs={{0,4},{4,0},{8,12},{12,8},{1,5},{5,1},{9,13},{13,9},{2,6},{6,2},{1... | collective-permute-start | bytes 614408 | tf_op jit(solution)/shard_map/ppermute | solution.py:377
  9.4 0.0 collective-permute-start.5
  9.4 0.8 %collective-permute-start.3 = (bf16[272,256]{1,0:T(8,128)(2,1)S(1)}, bf16[272,256]{1,0:T(8,128)(2,1)S(1)}, u32[]{:S(2)}, u32[]{:S(2)}) collective-permute-start(bf16[272,256]{1,0:T(8,128)(2,1)S(1)} %panel_message.1), channel_id=1, source_target_pairs={{0,1},{1,0},{2,3},{3,2},{4,5},{5,4},{6,7},{7,6},{8,9},{9,8},{10,11... | collective-permute-start | bytes 417800 | tf_op jit(solution)/shard_map/ppermute | solution.py:354
  10.2 1.5 %collective-permute-start.1 = (bf16[400,256]{1,0:T(8,128)(2,1)S(1)}, bf16[400,256]{1,0:T(8,128)(2,1)S(1)}, u32[]{:S(2)}, u32[]{:S(2)}) collective-permute-start(bf16[400,256]{1,0:T(8,128)(2,1)S(1)} %get-tuple-element.19), channel_id=1, source_target_pairs={{0,8},{4,12},{8,0},{12,4},{1,9},{5,13},{9,1},{13,5},{2,10},{6,14},... | collective-permute-start | bytes 614408 | tf_op jit(solution)/shard_map/ppermute | solution.py:377
  11.7 1.5 %collective-permute-start.2 = (bf16[400,256]{1,0:T(8,128)(2,1)S(1)}, bf16[400,256]{1,0:T(8,128)(2,1)S(1)}, u32[]{:S(2)}, u32[]{:S(2)}) collective-permute-start(bf16[400,256]{1,0:T(8,128)(2,1)S(1)} %get-tuple-element.20), channel_id=1, source_target_pairs={{0,12},{4,8},{8,4},{12,0},{1,13},{5,9},{9,5},{13,1},{2,14},{6,10},... | collective-permute-start | bytes 614408 | tf_op jit(solution)/shard_map/ppermute | solution.py:377
  13.2 5.2 %collective-permute-done.5.refs_11_ = bf16[272,256]{1,0:T(8,128)(2,1)S(1)} collective-permute-done((bf16[272,256]{1,0:T(8,128)(2,1)S(1)}, bf16[272,256]{1,0:T(8,128)(2,1)S(1)}, u32[]{:S(2)}, u32[]{:S(2)}) %collective-permute-start.5) | collective-permute-done | bytes 139296 | tf_op jit(solution)/shard_map/ppermute | solution.py:354
  18.5 0.0 collective-permute-start.8
  18.5 0.5 %collective-permute-start.6 = (bf16[272,256]{1,0:T(8,128)(2,1)S(1)}, bf16[272,256]{1,0:T(8,128)(2,1)S(1)}, u32[]{:S(2)}, u32[]{:S(2)}) collective-permute-start(bf16[272,256]{1,0:T(8,128)(2,1)S(1)} %collective-permute-done.5.refs_11_), channel_id=1, source_target_pairs={{0,16},{16,0},{1,17},{17,1},{2,18},{18,2},{3,19},{19,3},{4,20},{20... | collective-permute-start | bytes 417800 | tf_op jit(solution)/shard_map/ppermute | solution.py:357
  19.0 0.1 collective-permute-start.4
  19.1 1.3 %collective-permute-done.1.refs_7_ = bf16[400,256]{1,0:T(8,128)(2,1)S(1)} collective-permute-done((bf16[400,256]{1,0:T(8,128)(2,1)S(1)}, bf16[400,256]{1,0:T(8,128)(2,1)S(1)}, u32[]{:S(2)}, u32[]{:S(2)}) %collective-permute-start.1) | collective-permute-done | bytes 204832 | tf_op jit(solution)/shard_map/ppermute | solution.py:377
  20.4 0.0 collective-permute-done.4.refs_10_
  20.4 8.5 %score.1 = (bf16[400,256]{1,0:T(8,128)(2,1)S(1)}, bf16[400,256]{1,0:T(8,128)(2,1)S(1)}, bf16[400,256]{1,0:T(8,128)(2,1)S(1)}, bf16[400,256]{1,0:T(8,128)(2,1)S(1...) custom-call(s32[1,128]{1,0:T(1,128)} %refs_0_.1, s32[4,64]{1,0:T(4,128)} %refs_1_.1, s32[4,384]{1,0:T(4,128)} %refs_2_.1, ...), custom_call_target="tpu_custom_call" | custom-call | tf_op jit(solution)/shard_map/score/pallas_call | solution.py:386
  28.9 0.1 collective-permute-start.12
  29.0 1.5 %collective-permute-start.9 = (bf16[400,256]{1,0:T(8,128)(2,1)S(1)}, bf16[400,256]{1,0:T(8,128)(2,1)S(1)}, u32[]{:S(2)}, u32[]{:S(2)}) collective-permute-start(bf16[400,256]{1,0:T(8,128)(2,1)S(1)} %get-tuple-element.22), channel_id=1, source_target_pairs={{4,0},{0,4},{12,8},{8,12},{5,1},{1,5},{13,9},{9,13},{6,2},{2,6},{1... | collective-permute-start | bytes 614408 | tf_op jit(solution)/shard_map/ppermute | solution.py:468
  30.5 1.5 %collective-permute-start.10 = (bf16[400,256]{1,0:T(8,128)(2,1)S(1)}, bf16[400,256]{1,0:T(8,128)(2,1)S(1)}, u32[]{:S(2)}, u32[]{:S(2)}) collective-permute-start(bf16[400,256]{1,0:T(8,128)(2,1)S(1)} %get-tuple-element.23), channel_id=1, source_target_pairs={{8,0},{12,4},{0,8},{4,12},{9,1},{13,5},{1,9},{5,13},{10,2},{14,6},... | collective-permute-start | bytes 614408 | tf_op jit(solution)/shard_map/ppermute | solution.py:468
  32.1 0.4 collective-permute-start.11
  32.5 0.0 collective-permute-done.12.refs_0_
  32.5 0.1 tower_sum.1
  32.7 3.3 %collective-permute-start.13 = (bf16[256,256]{1,0:T(8,128)(2,1)S(1)}, bf16[256,256]{1,0:T(8,128)(2,1)S(1)}, u32[]{:S(2)}, u32[]{:S(2)}) collective-permute-start(bf16[256,256]{1,0:T(8,128)(2,1)S(1)} %get-tuple-element.30), channel_id=1, source_target_pairs={{0,1},{1,0},{2,3},{3,2},{4,5},{5,4},{6,7},{7,6},{8,9},{9,8},{10,11... | collective-permute-start | bytes 393224 | tf_op jit(solution)/shard_map/ppermute | solution.py:453
  36.0 1.0 %collective-permute-start.14 = (bf16[256,256]{1,0:T(8,128)(2,1)S(1)}, bf16[256,256]{1,0:T(8,128)(2,1)S(1)}, u32[]{:S(2)}, u32[]{:S(2)}) collective-permute-start(bf16[256,256]{1,0:T(8,128)(2,1)S(1)} %get-tuple-element.31), channel_id=1, source_target_pairs={{0,2},{1,3},{2,0},{3,1},{4,6},{5,7},{6,4},{7,5},{8,10},{9,11},{10,... | collective-permute-start | bytes 393224 | tf_op jit(solution)/shard_map/ppermute | solution.py:453
  37.0 0.0 collective-permute-done.9.refs_1_
  37.0 3.4 %collective-permute-start.15 = (bf16[256,256]{1,0:T(8,128)(2,1)S(1)}, bf16[256,256]{1,0:T(8,128)(2,1)S(1)}, u32[]{:S(2)}, u32[]{:S(2)}) collective-permute-start(bf16[256,256]{1,0:T(8,128)(2,1)S(1)} %get-tuple-element.32), channel_id=1, source_target_pairs={{0,3},{1,2},{2,1},{3,0},{4,7},{5,6},{6,5},{7,4},{8,11},{9,10},{10,... | collective-permute-start | bytes 393224 | tf_op jit(solution)/shard_map/ppermute | solution.py:453
  40.4 1.5 %collective-permute-done.10.refs_2_ = bf16[400,256]{1,0:T(8,128)(2,1)S(1)} collective-permute-done((bf16[400,256]{1,0:T(8,128)(2,1)S(1)}, bf16[400,256]{1,0:T(8,128)(2,1)S(1)}, u32[]{:S(2)}, u32[]{:S(2)}) %collective-permute-start.10) | collective-permute-done | bytes 204832 | tf_op jit(solution)/shard_map/ppermute | solution.py:468
  41.9 0.0 collective-permute-done.11.refs_3_
  41.9 1.5 %home.1 = (bf16[4,384,256]{2,1,0:T(8,128)(2,1)}, bf16[4,384]{1,0:T(4,128)(2,1)}) custom-call(bf16[400,256]{1,0:T(8,128)(2,1)S(1)} %get-tuple-element.21.refs_0_, bf16[400,256]{1,0:T(8,128)(2,1)S(1)} %collective-permute-done.9.refs_1_, bf16[400,256]{1,0:T(8,128)(2,1)S(1)} %collective-permute-done.10.refs_2_, bf16[400,256]{1,0:T(8,128)(2,1)S(1)} %collective-permute-done.11.refs_3_), custom_call_target="tpu_custom_call" | custom-call | tf_op jit(solution)/shard_map/home/pallas_call | solution.py:469
  43.4 0.0 collective-permute-done.13.refs_0_
  43.4 4.8 %collective-permute-done.14.refs_1_ = bf16[256,256]{1,0:T(8,128)(2,1)S(1)} collective-permute-done((bf16[256,256]{1,0:T(8,128)(2,1)S(1)}, bf16[256,256]{1,0:T(8,128)(2,1)S(1)}, u32[]{:S(2)}, u32[]{:S(2)}) %collective-permute-start.14) | collective-permute-done | bytes 131104 | tf_op jit(solution)/shard_map/ppermute | solution.py:453
  48.2 0.0 collective-permute-done.15.refs_2_
  48.2 0.8 %shard_sum.1 = f32[256,256]{1,0:T(8,128)} custom-call(f32[256,256]{1,0:T(8,128)S(1)} %get-tuple-element.29.own, bf16[256,256]{1,0:T(8,128)(2,1)S(1)} %collective-permute-done.13.refs_0_, bf16[256,256]{1,0:T(8,128)(2,1)S(1)} %collective-permute-done.14.refs_1_, bf16[256,256]{1,0:T(8,128)(2,1)S(1)} %collective-permute-done.15.refs_2_), custom_call_target="tpu_custom_call" | custom-call | flops 1000000000 | bytes 10000000 | tf_op jit(solution)/shard_map/shard_sum/pallas_call | solution.py:454
  (6 shorter events, 0.0 us)
Async XLA Ops:
  1.6 10.2 %collective-permute-start.7 = (bf16[272,256]{1,0:T(8,128)(2,1)S(1)}, bf16[272,256]{1,0:T(8,128)(2,1)S(1)}, u32[]{:S(2)}, u32[]{:S(2)}) collective-permute-start(bf16[272,256]{1,0:T(8,128)(2,1)S(1)} %panel_message.1), channel_id=1, source_target_pairs={{0,3},{1,2},{2,1},{3,0},{4,7},{5,6},{6,5},{7,4},{8,11},{9,10},{10,... | collective-permute-start | bytes 417800 | tf_op jit(solution)/shard_map/ppermute | solution.py:354
  7.9 11.1 %collective-permute-start = (bf16[400,256]{1,0:T(8,128)(2,1)S(1)}, bf16[400,256]{1,0:T(8,128)(2,1)S(1)}, u32[]{:S(2)}, u32[]{:S(2)}) collective-permute-start(bf16[400,256]{1,0:T(8,128)(2,1)S(1)} %get-tuple-element.18), channel_id=1, source_target_pairs={{0,4},{4,0},{8,12},{12,8},{1,5},{5,1},{9,13},{13,9},{2,6},{6,2},{1... | collective-permute-start | bytes 614408 | tf_op jit(solution)/shard_map/ppermute | solution.py:377
  9.4 9.0 %collective-permute-start.5 = (bf16[272,256]{1,0:T(8,128)(2,1)S(1)}, bf16[272,256]{1,0:T(8,128)(2,1)S(1)}, u32[]{:S(2)}, u32[]{:S(2)}) collective-permute-start(bf16[272,256]{1,0:T(8,128)(2,1)S(1)} %panel_message.1), channel_id=1, source_target_pairs={{0,2},{1,3},{2,0},{3,1},{4,6},{5,7},{6,4},{7,5},{8,10},{9,11},{10,... | collective-permute-start | bytes 417800 | tf_op jit(solution)/shard_map/ppermute | solution.py:354
  9.4 9.0 %collective-permute-start.3 = (bf16[272,256]{1,0:T(8,128)(2,1)S(1)}, bf16[272,256]{1,0:T(8,128)(2,1)S(1)}, u32[]{:S(2)}, u32[]{:S(2)}) collective-permute-start(bf16[272,256]{1,0:T(8,128)(2,1)S(1)} %panel_message.1), channel_id=1, source_target_pairs={{0,1},{1,0},{2,3},{3,2},{4,5},{5,4},{6,7},{7,6},{8,9},{9,8},{10,11... | collective-permute-start | bytes 417800 | tf_op jit(solution)/shard_map/ppermute | solution.py:354
  10.2 10.2 %collective-permute-start.1 = (bf16[400,256]{1,0:T(8,128)(2,1)S(1)}, bf16[400,256]{1,0:T(8,128)(2,1)S(1)}, u32[]{:S(2)}, u32[]{:S(2)}) collective-permute-start(bf16[400,256]{1,0:T(8,128)(2,1)S(1)} %get-tuple-element.19), channel_id=1, source_target_pairs={{0,8},{4,12},{8,0},{12,4},{1,9},{5,13},{9,1},{13,5},{2,10},{6,14},... | collective-permute-start | bytes 614408 | tf_op jit(solution)/shard_map/ppermute | solution.py:377
  11.7 8.6 %collective-permute-start.2 = (bf16[400,256]{1,0:T(8,128)(2,1)S(1)}, bf16[400,256]{1,0:T(8,128)(2,1)S(1)}, u32[]{:S(2)}, u32[]{:S(2)}) collective-permute-start(bf16[400,256]{1,0:T(8,128)(2,1)S(1)} %get-tuple-element.20), channel_id=1, source_target_pairs={{0,12},{4,8},{8,4},{12,0},{1,13},{5,9},{9,5},{13,1},{2,14},{6,10},... | collective-permute-start | bytes 614408 | tf_op jit(solution)/shard_map/ppermute | solution.py:377
  18.5 1.9 %collective-permute-start.8 = (bf16[272,256]{1,0:T(8,128)(2,1)S(1)}, bf16[272,256]{1,0:T(8,128)(2,1)S(1)}, u32[]{:S(2)}, u32[]{:S(2)}) collective-permute-start(bf16[272,256]{1,0:T(8,128)(2,1)S(1)} %collective-permute-done.7.refs_13_), channel_id=1, source_target_pairs={{0,16},{16,0},{1,17},{17,1},{2,18},{18,2},{3,19},{19,3},{4,20},{20... | collective-permute-start | bytes 417800 | tf_op jit(solution)/shard_map/ppermute | solution.py:357
  18.5 1.9 %collective-permute-start.6 = (bf16[272,256]{1,0:T(8,128)(2,1)S(1)}, bf16[272,256]{1,0:T(8,128)(2,1)S(1)}, u32[]{:S(2)}, u32[]{:S(2)}) collective-permute-start(bf16[272,256]{1,0:T(8,128)(2,1)S(1)} %collective-permute-done.5.refs_11_), channel_id=1, source_target_pairs={{0,16},{16,0},{1,17},{17,1},{2,18},{18,2},{3,19},{19,3},{4,20},{20... | collective-permute-start | bytes 417800 | tf_op jit(solution)/shard_map/ppermute | solution.py:357
  19.0 1.4 %collective-permute-start.4 = (bf16[272,256]{1,0:T(8,128)(2,1)S(1)}, bf16[272,256]{1,0:T(8,128)(2,1)S(1)}, u32[]{:S(2)}, u32[]{:S(2)}) collective-permute-start(bf16[272,256]{1,0:T(8,128)(2,1)S(1)} %collective-permute-done.3.refs_9_), channel_id=1, source_target_pairs={{0,16},{16,0},{1,17},{17,1},{2,18},{18,2},{3,19},{19,3},{4,20},{20... | collective-permute-start | bytes 417800 | tf_op jit(solution)/shard_map/ppermute | solution.py:357
  28.9 3.6 %collective-permute-start.12 = (bf16[1024,256]{1,0:T(8,128)(2,1)S(1)}, bf16[1024,256]{1,0:T(8,128)(2,1)S(1)}, u32[]{:S(2)}, u32[]{:S(2)}) collective-permute-start(bf16[1024,256]{1,0:T(8,128)(2,1)S(1)} %get-tuple-element.28), channel_id=1, source_target_pairs={{0,16},{16,0},{1,17},{17,1},{2,18},{18,2},{3,19},{19,3},{4,20},{20... | collective-permute-start | bytes 1572872 | tf_op jit(solution)/shard_map/ppermute | solution.py:431
  29.0 8.0 %collective-permute-start.9 = (bf16[400,256]{1,0:T(8,128)(2,1)S(1)}, bf16[400,256]{1,0:T(8,128)(2,1)S(1)}, u32[]{:S(2)}, u32[]{:S(2)}) collective-permute-start(bf16[400,256]{1,0:T(8,128)(2,1)S(1)} %get-tuple-element.22), channel_id=1, source_target_pairs={{4,0},{0,4},{12,8},{8,12},{5,1},{1,5},{13,9},{9,13},{6,2},{2,6},{1... | collective-permute-start | bytes 614408 | tf_op jit(solution)/shard_map/ppermute | solution.py:468
  30.5 11.4 %collective-permute-start.10 = (bf16[400,256]{1,0:T(8,128)(2,1)S(1)}, bf16[400,256]{1,0:T(8,128)(2,1)S(1)}, u32[]{:S(2)}, u32[]{:S(2)}) collective-permute-start(bf16[400,256]{1,0:T(8,128)(2,1)S(1)} %get-tuple-element.23), channel_id=1, source_target_pairs={{8,0},{12,4},{0,8},{4,12},{9,1},{13,5},{1,9},{5,13},{10,2},{14,6},... | collective-permute-start | bytes 614408 | tf_op jit(solution)/shard_map/ppermute | solution.py:468
  32.1 9.9 %collective-permute-start.11 = (bf16[400,256]{1,0:T(8,128)(2,1)S(1)}, bf16[400,256]{1,0:T(8,128)(2,1)S(1)}, u32[]{:S(2)}, u32[]{:S(2)}) collective-permute-start(bf16[400,256]{1,0:T(8,128)(2,1)S(1)} %get-tuple-element.24), channel_id=1, source_target_pairs={{12,0},{8,4},{4,8},{0,12},{13,1},{9,5},{5,9},{1,13},{14,2},{10,6},... | collective-permute-start | bytes 614408 | tf_op jit(solution)/shard_map/ppermute | solution.py:468
  32.7 10.8 %collective-permute-start.13 = (bf16[256,256]{1,0:T(8,128)(2,1)S(1)}, bf16[256,256]{1,0:T(8,128)(2,1)S(1)}, u32[]{:S(2)}, u32[]{:S(2)}) collective-permute-start(bf16[256,256]{1,0:T(8,128)(2,1)S(1)} %get-tuple-element.30), channel_id=1, source_target_pairs={{0,1},{1,0},{2,3},{3,2},{4,5},{5,4},{6,7},{7,6},{8,9},{9,8},{10,11... | collective-permute-start | bytes 393224 | tf_op jit(solution)/shard_map/ppermute | solution.py:453
  36.0 12.3 %collective-permute-start.14 = (bf16[256,256]{1,0:T(8,128)(2,1)S(1)}, bf16[256,256]{1,0:T(8,128)(2,1)S(1)}, u32[]{:S(2)}, u32[]{:S(2)}) collective-permute-start(bf16[256,256]{1,0:T(8,128)(2,1)S(1)} %get-tuple-element.31), channel_id=1, source_target_pairs={{0,2},{1,3},{2,0},{3,1},{4,6},{5,7},{6,4},{7,5},{8,10},{9,11},{10,... | collective-permute-start | bytes 393224 | tf_op jit(solution)/shard_map/ppermute | solution.py:453
  37.0 11.2 %collective-permute-start.15 = (bf16[256,256]{1,0:T(8,128)(2,1)S(1)}, bf16[256,256]{1,0:T(8,128)(2,1)S(1)}, u32[]{:S(2)}, u32[]{:S(2)}) collective-permute-start(bf16[256,256]{1,0:T(8,128)(2,1)S(1)} %get-tuple-element.32), channel_id=1, source_target_pairs={{0,3},{1,2},{2,1},{3,0},{4,7},{5,6},{6,5},{7,4},{8,11},{9,10},{10,... | collective-permute-start | bytes 393224 | tf_op jit(solution)/shard_map/ppermute | solution.py:453

commit v5 on v4

--- a/solution.py
+++ b/solution.py
@@ -17,6 +17,7 @@
     (),
 )
 LN2 = math.log(2.0)
+COST = 10**10
 
 
 def peers(axis):
@@ -34,44 +35,31 @@
     return lax.dynamic_index_in_dim(array, index, 0, keepdims=False)
 
 
-def panel_message_kernel(part_rows, panels, scales, out, held, sems):
+def message_kernel(per, part_rows, targets, panels, scales, queries, ids_far, pos_far, *refs):
+    (message, *outs, held, ids, positives, marks, sems) = refs
+    rows, nsel = queries.shape[1], ids_far.shape[1]
+    items, shard = scales.shape
+    reps = rows // LANES
+    copies = []
+
+    def fetch(source, target):
+        copies.append(pltpu.make_async_copy(source, target, sems.at[len(copies)]))
+        copies[-1].start()
+
     start = pl.multiple_of(lax.axis_index("tower") * part_rows, TILE)
-    copy = pltpu.make_async_copy(
-        panels.at[pl.ds(start, part_rows), :], out.at[0:part_rows, :], sems.at[0]
-    )
-    copy.start()
-    fetch = pltpu.make_async_copy(scales, held, sems.at[1])
-    fetch.start()
-    items, shard = scales.shape
-    out[part_rows : part_rows + items, :] = jnp.zeros((items, out.shape[1]), out.dtype)
-    fetch.wait()
-    out[part_rows : part_rows + items, 0:shard] = held[...]
-    copy.wait()
-
-
-def query_message_kernel(per, items, targets, queries, ids_far, positives_far, *refs):
-    (*outs, ids, positives, marks, sems) = refs
-    rows = queries.shape[1]
-    nsel = ids.shape[1]
-    reps = rows // LANES
-    goal = targets()
-    lists = [
-        pltpu.make_async_copy(ids_far, ids, sems.at[len(outs)]),
-        pltpu.make_async_copy(positives_far, positives, sems.at[len(outs) + 1]),
-    ]
-    for copy in lists:
-        copy.start()
-    copies = []
-    for n, out in enumerate(outs):
-        block = goal[n // per] * per + n % per
-        copies.append(
-            pltpu.make_async_copy(queries.at[block], out.at[0:rows, :], sems.at[n])
-        )
-        copies[-1].start()
-    for copy in lists:
+    fetch(ids_far, ids)
+    fetch(pos_far, positives)
+    fetch(scales, held)
+    fetch(panels.at[pl.ds(start, part_rows), :], message.at[0:part_rows, :])
+    goal = [to * per + i for to in targets() for i in range(per)]
+    for block, out in zip(goal, outs):
+        fetch(queries.at[block], out.at[0:rows, :])
+    for copy in copies[:3]:
         copy.wait()
-    for n, out in enumerate(outs):
-        block = goal[n // per] * per + n % per
+    below = pl.ds(part_rows, items)
+    message[below, :] = jnp.zeros((items, message.shape[1]), message.dtype)
+    message[below, 0:shard] = held[...]
+    for block, out in zip(goal, outs):
         place = positives[pl.ds(block, 1), :]
         marks[...] = jnp.zeros_like(marks)
         for c in range(reps):
@@ -80,8 +68,23 @@
             marks[c : c + 1, LANES : 2 * LANES] = (chunk % items).astype(jnp.float32)
         marks[reps : reps + 1, 0:nsel] = ids[pl.ds(block, 1), :].astype(jnp.float32)
         out[rows : rows + TILE, :] = marks[...].astype(out.dtype)
-    for copy in copies:
+    for copy in copies[3:]:
         copy.wait()
+
+
+def list_kernel(items, count, *refs):
+    messages, places, lists = refs[:count], refs[-2 * count : -count], refs[-count:]
+    for message, place, ids in zip(messages, places, lists):
+        rows = message.shape[0] - TILE
+        reps = rows // LANES
+        marks = message[rows : rows + TILE, :].astype(jnp.float32)
+        found = [
+            marks[n : n + 1, 0:LANES] * items + marks[n : n + 1, LANES : 2 * LANES]
+            for n in range(reps)
+        ]
+        found = jnp.concatenate(found, axis=1).astype(jnp.int32)
+        place[...] = jnp.broadcast_to(found, place.shape)
+        ids[...] = jnp.broadcast_to(marks[reps : reps + 1, 0:LANES], ids.shape).astype(jnp.int32)
 
 
 def score_kernel(dims, *refs):
@@ -94,12 +97,14 @@
 
     owner_far, ids_far, pos_far, scale_far, queries, own = take(6)
     messages = take(nq - nlocal)
+    places = take(nq - nlocal)
+    lists = take(nq - nlocal)
     pieces = take(n_piece)
     outs = take(nq)
     (keep,) = take(1)
     sends = take(ntow - 1 if split else 0)
     (panel, wide, query, score, sel, sel_wide, weight, term, grad, place) = refs[:10]
-    (owner, ids, far_ids, moved_ids, pos_own, scale_own, sems) = refs[10:]
+    (owner, ids, far_ids, pos_own, scale_own, sems) = refs[10:]
     part = shard // ntow
     cand = nsel * items
     width = panel.shape[1]
@@ -133,26 +138,9 @@
     moved = []
 
     for b in range(nlocal, nq):
-        marks = messages[b - nlocal][rows : rows + TILE, :].astype(jnp.float32)
-        found = [
-            marks[n : n + 1, 0:LANES] * items + marks[n : n + 1, LANES : 2 * LANES]
-            for n in range(reps)
-        ]
-        found = jnp.concatenate(found, axis=1).astype(jnp.int32)
-        place[b] = jnp.broadcast_to(found, (8, rows))
-        far = jnp.broadcast_to(marks[reps : reps + 1, 0:LANES], (8, LANES))
-        moved_ids[b] = far.astype(jnp.int32)
-        moved.append(fetch(moved_ids.at[b], far_ids.at[b]))
-    for copy in early + local + moved:
-        copy.wait()
-    for b in range(nlocal):
-        place[b] = jnp.broadcast_to(pos_own[pl.ds(mine * nlocal + b, 1), :], (8, rows))
-
-    def slot_of(b, j):
-        if b < nlocal:
-            return owner[0, ids[mine * nlocal + b, j]]
-        return owner[0, far_ids[b, 0, j]]
-
+        place[b] = places[b - nlocal][...]
+        moved.append(fetch(lists[b - nlocal], far_ids.at[b]))
+    early[2].wait()
     item_of = lax.broadcasted_iota(jnp.int32, (shard * items, items), 0) % items
     spread = item_of == lax.broadcasted_iota(jnp.int32, (shard * items, items), 1)
     spread = spread.astype(jnp.bfloat16)
@@ -172,8 +160,18 @@
     for n, to in enumerate(blk_to):
         widen(pieces[n * ntow][part * items : part * items + items, 0:LANES], rows_at(to * shard, shard))
 
-    line = lax.broadcasted_iota(jnp.int32, (8, rows), 0)
+    line = lax.broadcasted_iota(jnp.int32, (8, LANES), 0)
     state = [{} for _ in range(nq)]
+    for n, copy in enumerate(early + local + moved):
+        if n != 2:
+            copy.wait()
+    for b in range(nlocal):
+        place[b] = jnp.broadcast_to(pos_own[pl.ds(mine * nlocal + b, 1), :], (8, rows))
+
+    def slot_of(b, j):
+        if b < nlocal:
+            return owner[0, ids[mine * nlocal + b, j]]
+        return owner[0, far_ids[b, 0, j]]
 
     def gather(b):
         two = b % 2
@@ -193,6 +191,9 @@
 
     def spread_scale(two, first):
         return jnp.tile(sel_wide[two, first : first + 8, :], (1, reps))
+
+    def is_positive(pos, first):
+        return jnp.tile(line + first, (1, reps)) == pos
 
     def peaks(b):
         two = b % 2
@@ -212,7 +213,7 @@
             e = jnp.exp2(s - top)
             score[two, first : first + 8, :] = e
             total = total + e
-            pick = jnp.where(line == pos - first, s, pick)
+            pick = jnp.where(is_positive(pos, first), s, pick)
         total = jnp.sum(total, axis=0, keepdims=True)
         picked = jnp.sum(pick, axis=0, keepdims=True)
         loss = (top - picked) * LN2 + jnp.log(total)
@@ -230,7 +231,7 @@
             halves = []
             for first in range(start, start + TILE, 8):
                 chance = score[two, first : first + 8, :] * inverse
-                chance = jnp.where(line == pos - first, chance - LN2, chance)
+                chance = jnp.where(is_positive(pos, first), chance - LN2, chance)
                 halves.append(chance * spread_scale(two, first))
             weight[two, start : start + TILE, :] = jnp.concatenate(halves, axis=0).astype(
                 jnp.bfloat16
@@ -337,47 +338,55 @@
     flat_panels = panels.reshape(shard * items, width)
     flat_scales = scales.T
 
-    message = pl.pallas_call(
-        functools.partial(panel_message_kernel, part * items),
-        out_shape=jax.ShapeDtypeStruct((part * items + items, width), panels.dtype),
-        in_specs=[hbm, hbm],
-        out_specs=vmem,
+    def targets():
+        return [to for to, _, _ in peers("group")]
+
+    message, *leaving = pl.pallas_call(
+        functools.partial(message_kernel, per, part * items, targets),
+        out_shape=[jax.ShapeDtypeStruct((part * items + items, width), panels.dtype)]
+        + [jax.ShapeDtypeStruct((rows + TILE, width), queries.dtype)] * (nq - per),
+        in_specs=[hbm] * 5,
+        out_specs=[vmem] * (1 + nq - per),
         scratch_shapes=[
-            pltpu.VMEM((items, shard), scales.dtype),
-            pltpu.SemaphoreType.DMA((2,)),
+            pltpu.VMEM(flat_scales.shape, scales.dtype),
+            pltpu.VMEM(cluster_ids.shape, jnp.int32),
+            pltpu.VMEM(positives.shape, jnp.int32),
+            pltpu.VMEM((TILE, width), jnp.float32),
+            pltpu.SemaphoreType.DMA((4 + nq - per,)),
         ],
         compiler_params=params,
-        name="panel_message",
-    )(pin(flat_panels), pin(flat_scales))
+        name="messages",
+    )(pin(flat_panels), pin(flat_scales), pin(queries), pin(cluster_ids), pin(positives))
+
     pieces = []
-    for to, source, pattern in blk_peers:
-        piece = lax.ppermute(message, "blk", pattern)
+    near = [lax.ppermute(message, "blk", pattern) for _, _, pattern in blk_peers[:2]]
+    for n, (_, _, pattern) in enumerate(blk_peers):
+        if n < 2:
+            piece = near[n]
+        elif nblk == 4:
+            piece = lax.ppermute(near[1], "blk", blk_peers[0][2])
+        else:
+            piece = lax.ppermute(message, "blk", pattern)
         pieces.append(piece)
         for _, tow_source, tow_pattern in tow_peers:
             pieces.append(lax.ppermute(piece, "tower", tow_pattern))
 
-    def targets():
-        return [to for to, _, _ in peers("group")]
-
-    leaving = pl.pallas_call(
-        functools.partial(query_message_kernel, per, items, targets),
-        out_shape=[jax.ShapeDtypeStruct((rows + TILE, width), queries.dtype)] * (nq - per),
-        in_specs=[hbm, hbm, hbm],
-        out_specs=[vmem] * (nq - per),
-        scratch_shapes=[
-            pltpu.VMEM(cluster_ids.shape, jnp.int32),
-            pltpu.VMEM(positives.shape, jnp.int32),
-            pltpu.VMEM((TILE, width), jnp.float32),
-            pltpu.SemaphoreType.DMA((nq - per + 2,)),
-        ],
-        compiler_params=params,
-        name="query_message",
-    )(pin(queries), pin(cluster_ids), pin(positives))
     arrived = [
         lax.ppermute(leaving[n * per + i], "group", pattern)
         for n, (_, _, pattern) in enumerate(group_peers)
         for i in range(per)
     ]
+    far, first = nq - per, pieces[1:2]
+    lists = pl.pallas_call(
+        functools.partial(list_kernel, items, far),
+        out_shape=[jax.ShapeDtypeStruct((8, rows), jnp.int32)] * far
+        + [jax.ShapeDtypeStruct((8, LANES), jnp.int32)] * far,
+        in_specs=[vmem] * (far + len(first)),
+        out_specs=[vmem] * (2 * far),
+        compiler_params=params,
+        cost_estimate=pl.CostEstimate(flops=COST, bytes_accessed=COST // 1000, transcendentals=0),
+        name="lists",
+    )(*arrived, *first)
     dims = (nq, per, ntow, len(pieces), rows, nsel, items, slots, shard, split)
     sent_rows = slots * items // ntow
     keep_rows = sent_rows if split else slots * items
@@ -388,7 +397,7 @@
         out_shape=[pltpu.VMEM((rows + TILE, width), jnp.bfloat16)] * nq
         + [pltpu.VMEM((keep_rows, width), jnp.float32)]
         + [pltpu.VMEM((sent_rows, width), jnp.bfloat16)] * n_send,
-        in_specs=[hbm] * 6 + [vmem] * (nq - per + len(pieces)),
+        in_specs=[hbm] * 6 + [vmem] * (3 * (nq - per) + len(pieces)),
         out_specs=[vmem] * (nq + 1 + n_send),
         scratch_shapes=[
             pltpu.VMEM((slots * items, width), jnp.bfloat16),
@@ -404,7 +413,6 @@
             pltpu.SMEM(owner_map.shape, jnp.int32),
             pltpu.SMEM(cluster_ids.shape, jnp.int32),
             pltpu.SMEM((nq, 8, LANES), jnp.int32),
-            pltpu.VMEM((nq, 8, LANES), jnp.int32),
             pltpu.VMEM(positives.shape, jnp.int32),
             pltpu.VMEM(flat_scales.shape, flat_scales.dtype),
             pltpu.SemaphoreType.DMA((5 + nq,)),
@@ -419,6 +427,7 @@
         pin(queries),
         pin(flat_panels),
         *arrived,
+        *lists,
         *pieces,
     )
     query_grads, keep, sends = results[:nq], results[nq], results[nq + 1 :]

time: 49.2 us -> 46.5 us (0.945)
  Pallas kernels: 13 us -> 11.9 us
  starting transfers between devices: 22.4 us -> 21.4 us
  waiting for transfers between devices: 12.9 us -> 12.4 us
    ppermute x3, waiting for transfers between devices: 1.34 us -> 3.82 us  [shards(): lax.ppermute(leaving[n * per + i], 'group', pattern)]
    ppermute x3, waiting for transfers between devices: 5.25 us -> 3.92 us  [the longest x1 2.22 us: shards(): piece = lax.ppermute(near[1], 'blk', blk_peers[0][2])]
    ppermute x3, waiting for transfers between devices: 4.79 us -> 3.5 us  [shards(): lax.ppermute(sent, 'blk', p)]
    ppermute x3, starting transfers between devices: 4.54 us -> 3.49 us  [shards(): lax.ppermute(leaving[n * per + i], 'group', pattern)]
    pallas_call x2, Pallas kernels: 2.12 us -> 1.3 us  [the longest x1 1.29 us: shards(): pl.pallas_call(functools.partial(message_kernel, per, part * items, targe...]
    ppermute x3, starting transfers between devices: 0.58 us -> 0.01 us  [shards(): pieces.append(lax.ppermute(piece, 'tower', tow_pattern))]
  transfers between devices with their start and end apart: 16 -> 16, of which waited for: 4 -> 7; matrix products, arithmetic and copies ran while one was open for 0% -> 0% of each run, Pallas kernels for 6% -> 3%
where the time goes in v5:
time: 46.5 us; the launch traced here: 46.4 us
  starting transfers between devices  21.4 us (46%)
  waiting for transfers between devices  12.4 us (27%)
  Pallas kernels  11.9 us (26%)
  between operations  0.71 us (2%)
    pallas_call x1, Pallas kernels, shards(): pl.pallas_call(functools.partial(score_kernel, dims), out_shape=[pltpu.VM...  8.22 us
    ppermute x3, starting transfers between devices, shards(): lax.ppermute(sent, 'blk', p)  8.03 us
    ppermute x2, starting transfers between devices, shards(): lax.ppermute(message, 'blk', pattern)  5.68 us
    ppermute x3, waiting for transfers between devices, shards(): lax.ppermute(leaving[n * per + i], 'group', pattern)  3.82 us
    ppermute x3, starting transfers between devices, shards(): blocks.append(lax.ppermute(block, 'group', home))  3.55 us
    ppermute x3, waiting for transfers between devices, shards(): lax.ppermute(sent, 'blk', p)  3.5 us
    ppermute x3, starting transfers between devices, shards(): lax.ppermute(leaving[n * per + i], 'group', pattern)  3.49 us
    ppermute x1, waiting for transfers between devices, shards(): piece = lax.ppermute(near[1], 'blk', blk_peers[0][2])  2.22 us
  transfers between devices with their start and end apart: 16, of which 7 were waited for; matrix products, arithmetic and copies ran while one was open for 0% of the time, Pallas kernels for 3%

profile of v5, /device:TPU:0, one launch (start us, length us, event | category | flops | bytes accessed | tf_op | source)
XLA Modules:
  0.0 46.4 jit_solution(16009161395810482182)
XLA Ops:
  0.6 1.3 %messages.1 = (bf16[272,256]{1,0:T(8,128)(2,1)S(1)}, bf16[400,256]{1,0:T(8,128)(2,1)S(1)}, bf16[400,256]{1,0:T(8,128)(2,1)S(1)}, bf16[400,256]{1,0:T(8,128)(2,1)S(1)}) custom-call(bf16[512,256]{1,0:T(8,128)(2,1)} %bitcast.3, bf16[16,32]{1,0:T(8,128)(2,1)} %bitcast.5, bf16[4,384,256]{2,1,0:T(8,128)(2,1)} %refs_4_.1, s32[4,64]{1,0:T(4,128)} %refs_1_.1, ...), custom_call_target="tpu_custom_call" | custom-call | tf_op jit(solution)/shard_map/messages/pallas_call | solution.py:344
  1.9 4.1 %collective-permute-start.5 = (bf16[272,256]{1,0:T(8,128)(2,1)S(1)}, bf16[272,256]{1,0:T(8,128)(2,1)S(1)}, u32[]{:S(2)}, u32[]{:S(2)}) collective-permute-start(bf16[272,256]{1,0:T(8,128)(2,1)S(1)} %get-tuple-element.28), channel_id=1, source_target_pairs={{0,2},{1,3},{2,0},{3,1},{4,6},{5,7},{6,4},{7,5},{8,10},{9,11},{10,... | collective-permute-start | bytes 417800 | tf_op jit(solution)/shard_map/ppermute | solution.py:362
  6.0 1.6 %collective-permute-start.3 = (bf16[272,256]{1,0:T(8,128)(2,1)S(1)}, bf16[272,256]{1,0:T(8,128)(2,1)S(1)}, u32[]{:S(2)}, u32[]{:S(2)}) collective-permute-start(bf16[272,256]{1,0:T(8,128)(2,1)S(1)} %get-tuple-element.28), channel_id=1, source_target_pairs={{0,1},{1,0},{2,3},{3,2},{4,5},{5,4},{6,7},{7,6},{8,9},{9,8},{10,11... | collective-permute-start | bytes 417800 | tf_op jit(solution)/shard_map/ppermute | solution.py:362
  7.6 1.5 %collective-permute-start = (bf16[400,256]{1,0:T(8,128)(2,1)S(1)}, bf16[400,256]{1,0:T(8,128)(2,1)S(1)}, u32[]{:S(2)}, u32[]{:S(2)}) collective-permute-start(bf16[400,256]{1,0:T(8,128)(2,1)S(1)} %get-tuple-element.25), channel_id=1, source_target_pairs={{0,4},{4,0},{8,12},{12,8},{1,5},{5,1},{9,13},{13,9},{2,6},{6,2},{1... | collective-permute-start | bytes 614408 | tf_op jit(solution)/shard_map/ppermute | solution.py:375
  9.1 1.5 %collective-permute-start.1 = (bf16[400,256]{1,0:T(8,128)(2,1)S(1)}, bf16[400,256]{1,0:T(8,128)(2,1)S(1)}, u32[]{:S(2)}, u32[]{:S(2)}) collective-permute-start(bf16[400,256]{1,0:T(8,128)(2,1)S(1)} %get-tuple-element.26), channel_id=1, source_target_pairs={{0,8},{4,12},{8,0},{12,4},{1,9},{5,13},{9,1},{13,5},{2,10},{6,14},... | collective-permute-start | bytes 614408 | tf_op jit(solution)/shard_map/ppermute | solution.py:375
  10.6 0.5 %collective-permute-start.2 = (bf16[400,256]{1,0:T(8,128)(2,1)S(1)}, bf16[400,256]{1,0:T(8,128)(2,1)S(1)}, u32[]{:S(2)}, u32[]{:S(2)}) collective-permute-start(bf16[400,256]{1,0:T(8,128)(2,1)S(1)} %get-tuple-element.27), channel_id=1, source_target_pairs={{0,12},{4,8},{8,4},{12,0},{1,13},{5,9},{9,5},{13,1},{2,14},{6,10},... | collective-permute-start | bytes 614408 | tf_op jit(solution)/shard_map/ppermute | solution.py:375
  11.1 1.7 %collective-permute-done.5.refs_17_ = bf16[272,256]{1,0:T(8,128)(2,1)S(1)} collective-permute-done((bf16[272,256]{1,0:T(8,128)(2,1)S(1)}, bf16[272,256]{1,0:T(8,128)(2,1)S(1)}, u32[]{:S(2)}, u32[]{:S(2)}) %collective-permute-start.5) | collective-permute-done | bytes 139296 | tf_op jit(solution)/shard_map/ppermute | solution.py:362
  12.8 0.6 %collective-permute-start.7 = (bf16[272,256]{1,0:T(8,128)(2,1)S(1)}, bf16[272,256]{1,0:T(8,128)(2,1)S(1)}, u32[]{:S(2)}, u32[]{:S(2)}) collective-permute-start(bf16[272,256]{1,0:T(8,128)(2,1)S(1)} %collective-permute-done.5.refs_17_), channel_id=1, source_target_pairs={{0,1},{1,0},{2,3},{3,2},{4,5},{5,4},{6,7},{7,6},{8,9},{9,8},{10,11... | collective-permute-start | bytes 417800 | tf_op jit(solution)/shard_map/ppermute | solution.py:367
  13.4 0.0 collective-permute-done.3.refs_15_
  13.4 0.0 collective-permute-start.4
  13.4 2.2 %collective-permute-done.refs_0_.refs_6_ = bf16[400,256]{1,0:T(8,128)(2,1)S(1)} collective-permute-done((bf16[400,256]{1,0:T(8,128)(2,1)S(1)}, bf16[400,256]{1,0:T(8,128)(2,1)S(1)}, u32[]{:S(2)}, u32[]{:S(2)}) %collective-permute-start) | collective-permute-done | bytes 204832 | tf_op jit(solution)/shard_map/ppermute | solution.py:375
  15.6 0.0 collective-permute-start.6
  15.6 2.2 %collective-permute-done.7.refs_19_ = bf16[272,256]{1,0:T(8,128)(2,1)S(1)} collective-permute-done((bf16[272,256]{1,0:T(8,128)(2,1)S(1)}, bf16[272,256]{1,0:T(8,128)(2,1)S(1)}, u32[]{:S(2)}, u32[]{:S(2)}) %collective-permute-start.7) | collective-permute-done | bytes 139296 | tf_op jit(solution)/shard_map/ppermute | solution.py:367
  17.8 0.0 collective-permute-start.8
  17.9 1.6 %collective-permute-done.1.refs_1_.refs_7_ = bf16[400,256]{1,0:T(8,128)(2,1)S(1)} collective-permute-done((bf16[400,256]{1,0:T(8,128)(2,1)S(1)}, bf16[400,256]{1,0:T(8,128)(2,1)S(1)}, u32[]{:S(2)}, u32[]{:S(2)}) %collective-permute-start.1) | collective-permute-done | bytes 204832 | tf_op jit(solution)/shard_map/ppermute | solution.py:375
  19.5 0.0 collective-permute-done.6.refs_18_
  19.5 0.0 collective-permute-done.8.refs_20_
  19.5 8.2 %score.1 = (bf16[400,256]{1,0:T(8,128)(2,1)S(1)}, bf16[400,256]{1,0:T(8,128)(2,1)S(1)}, bf16[400,256]{1,0:T(8,128)(2,1)S(1)}, bf16[400,256]{1,0:T(8,128)(2,1)S(1...) custom-call(s32[1,128]{1,0:T(1,128)} %refs_0_.1, s32[4,64]{1,0:T(4,128)} %refs_1_.1, s32[4,384]{1,0:T(4,128)} %refs_2_.1, ...), custom_call_target="tpu_custom_call" | custom-call | tf_op jit(solution)/shard_map/score/pallas_call | solution.py:395
  27.7 0.1 collective-permute-start.12
  27.8 1.4 %collective-permute-start.9 = (bf16[400,256]{1,0:T(8,128)(2,1)S(1)}, bf16[400,256]{1,0:T(8,128)(2,1)S(1)}, u32[]{:S(2)}, u32[]{:S(2)}) collective-permute-start(bf16[400,256]{1,0:T(8,128)(2,1)S(1)} %get-tuple-element.36), channel_id=1, source_target_pairs={{4,0},{0,4},{12,8},{8,12},{5,1},{1,5},{13,9},{9,13},{6,2},{2,6},{1... | collective-permute-start | bytes 614408 | tf_op jit(solution)/shard_map/ppermute | solution.py:477
  29.2 1.5 %collective-permute-start.10 = (bf16[400,256]{1,0:T(8,128)(2,1)S(1)}, bf16[400,256]{1,0:T(8,128)(2,1)S(1)}, u32[]{:S(2)}, u32[]{:S(2)}) collective-permute-start(bf16[400,256]{1,0:T(8,128)(2,1)S(1)} %get-tuple-element.37), channel_id=1, source_target_pairs={{8,0},{12,4},{0,8},{4,12},{9,1},{13,5},{1,9},{5,13},{10,2},{14,6},... | collective-permute-start | bytes 614408 | tf_op jit(solution)/shard_map/ppermute | solution.py:477
  30.7 0.6 %collective-permute-start.11 = (bf16[400,256]{1,0:T(8,128)(2,1)S(1)}, bf16[400,256]{1,0:T(8,128)(2,1)S(1)}, u32[]{:S(2)}, u32[]{:S(2)}) collective-permute-start(bf16[400,256]{1,0:T(8,128)(2,1)S(1)} %get-tuple-element.38), channel_id=1, source_target_pairs={{12,0},{8,4},{4,8},{0,12},{13,1},{9,5},{5,9},{1,13},{14,2},{10,6},... | collective-permute-start | bytes 614408 | tf_op jit(solution)/shard_map/ppermute | solution.py:477
  31.4 0.1 tower_sum.1
  31.5 1.0 %collective-permute-start.13 = (bf16[256,256]{1,0:T(8,128)(2,1)S(1)}, bf16[256,256]{1,0:T(8,128)(2,1)S(1)}, u32[]{:S(2)}, u32[]{:S(2)}) collective-permute-start(bf16[256,256]{1,0:T(8,128)(2,1)S(1)} %get-tuple-element.44), channel_id=1, source_target_pairs={{0,1},{1,0},{2,3},{3,2},{4,5},{5,4},{6,7},{7,6},{8,9},{9,8},{10,11... | collective-permute-start | bytes 393224 | tf_op jit(solution)/shard_map/ppermute | solution.py:462
  32.5 3.4 %collective-permute-start.14 = (bf16[256,256]{1,0:T(8,128)(2,1)S(1)}, bf16[256,256]{1,0:T(8,128)(2,1)S(1)}, u32[]{:S(2)}, u32[]{:S(2)}) collective-permute-start(bf16[256,256]{1,0:T(8,128)(2,1)S(1)} %get-tuple-element.45), channel_id=1, source_target_pairs={{0,2},{1,3},{2,0},{3,1},{4,6},{5,7},{6,4},{7,5},{8,10},{9,11},{10,... | collective-permute-start | bytes 393224 | tf_op jit(solution)/shard_map/ppermute | solution.py:462
  35.9 0.0 collective-permute-done.9.refs_1_
  35.9 3.6 %collective-permute-start.15 = (bf16[256,256]{1,0:T(8,128)(2,1)S(1)}, bf16[256,256]{1,0:T(8,128)(2,1)S(1)}, u32[]{:S(2)}, u32[]{:S(2)}) collective-permute-start(bf16[256,256]{1,0:T(8,128)(2,1)S(1)} %get-tuple-element.46), channel_id=1, source_target_pairs={{0,3},{1,2},{2,1},{3,0},{4,7},{5,6},{6,5},{7,4},{8,11},{9,10},{10,... | collective-permute-start | bytes 393224 | tf_op jit(solution)/shard_map/ppermute | solution.py:462
  39.5 0.2 collective-permute-done.10.refs_2_
  39.7 1.0 %collective-permute-done.11.refs_3_ = bf16[400,256]{1,0:T(8,128)(2,1)S(1)} collective-permute-done((bf16[400,256]{1,0:T(8,128)(2,1)S(1)}, bf16[400,256]{1,0:T(8,128)(2,1)S(1)}, u32[]{:S(2)}, u32[]{:S(2)}) %collective-permute-start.11) | collective-permute-done | bytes 204832 | tf_op jit(solution)/shard_map/ppermute | solution.py:477
  40.6 1.5 %home.1 = (bf16[4,384,256]{2,1,0:T(8,128)(2,1)}, bf16[4,384]{1,0:T(4,128)(2,1)}) custom-call(bf16[400,256]{1,0:T(8,128)(2,1)S(1)} %get-tuple-element.35.refs_0_, bf16[400,256]{1,0:T(8,128)(2,1)S(1)} %collective-permute-done.9.refs_1_, bf16[400,256]{1,0:T(8,128)(2,1)S(1)} %collective-permute-done.10.refs_2_, bf16[400,256]{1,0:T(8,128)(2,1)S(1)} %collective-permute-done.11.refs_3_), custom_call_target="tpu_custom_call" | custom-call | tf_op jit(solution)/shard_map/home/pallas_call | solution.py:478
  42.1 3.5 %collective-permute-done.14.refs_1_ = bf16[256,256]{1,0:T(8,128)(2,1)S(1)} collective-permute-done((bf16[256,256]{1,0:T(8,128)(2,1)S(1)}, bf16[256,256]{1,0:T(8,128)(2,1)S(1)}, u32[]{:S(2)}, u32[]{:S(2)}) %collective-permute-start.14) | collective-permute-done | bytes 131104 | tf_op jit(solution)/shard_map/ppermute | solution.py:462
  45.6 0.8 %shard_sum.1 = f32[256,256]{1,0:T(8,128)} custom-call(f32[256,256]{1,0:T(8,128)S(1)} %get-tuple-element.43.own, bf16[256,256]{1,0:T(8,128)(2,1)S(1)} %collective-permute-done.13.refs_0_, bf16[256,256]{1,0:T(8,128)(2,1)S(1)} %collective-permute-done.14.refs_1_, bf16[256,256]{1,0:T(8,128)(2,1)S(1)} %collective-permute-done.15.refs_2_), custom_call_target="tpu_custom_call" | custom-call | flops 1000000000 | bytes 10000000 | tf_op jit(solution)/shard_map/shard_sum/pallas_call | solution.py:463
  (6 shorter events, 0.0 us)
Async XLA Ops:
  1.9 10.9 %collective-permute-start.5 = (bf16[272,256]{1,0:T(8,128)(2,1)S(1)}, bf16[272,256]{1,0:T(8,128)(2,1)S(1)}, u32[]{:S(2)}, u32[]{:S(2)}) collective-permute-start(bf16[272,256]{1,0:T(8,128)(2,1)S(1)} %get-tuple-element.28), channel_id=1, source_target_pairs={{0,2},{1,3},{2,0},{3,1},{4,6},{5,7},{6,4},{7,5},{8,10},{9,11},{10,... | collective-permute-start | bytes 417800 | tf_op jit(solution)/shard_map/ppermute | solution.py:362
  6.0 7.4 %collective-permute-start.3 = (bf16[272,256]{1,0:T(8,128)(2,1)S(1)}, bf16[272,256]{1,0:T(8,128)(2,1)S(1)}, u32[]{:S(2)}, u32[]{:S(2)}) collective-permute-start(bf16[272,256]{1,0:T(8,128)(2,1)S(1)} %get-tuple-element.28), channel_id=1, source_target_pairs={{0,1},{1,0},{2,3},{3,2},{4,5},{5,4},{6,7},{7,6},{8,9},{9,8},{10,11... | collective-permute-start | bytes 417800 | tf_op jit(solution)/shard_map/ppermute | solution.py:362
  7.6 8.0 %collective-permute-start = (bf16[400,256]{1,0:T(8,128)(2,1)S(1)}, bf16[400,256]{1,0:T(8,128)(2,1)S(1)}, u32[]{:S(2)}, u32[]{:S(2)}) collective-permute-start(bf16[400,256]{1,0:T(8,128)(2,1)S(1)} %get-tuple-element.25), channel_id=1, source_target_pairs={{0,4},{4,0},{8,12},{12,8},{1,5},{5,1},{9,13},{13,9},{2,6},{6,2},{1... | collective-permute-start | bytes 614408 | tf_op jit(solution)/shard_map/ppermute | solution.py:375
  9.1 10.4 %collective-permute-start.1 = (bf16[400,256]{1,0:T(8,128)(2,1)S(1)}, bf16[400,256]{1,0:T(8,128)(2,1)S(1)}, u32[]{:S(2)}, u32[]{:S(2)}) collective-permute-start(bf16[400,256]{1,0:T(8,128)(2,1)S(1)} %get-tuple-element.26), channel_id=1, source_target_pairs={{0,8},{4,12},{8,0},{12,4},{1,9},{5,13},{9,1},{13,5},{2,10},{6,14},... | collective-permute-start | bytes 614408 | tf_op jit(solution)/shard_map/ppermute | solution.py:375
  10.6 8.8 %collective-permute-start.2 = (bf16[400,256]{1,0:T(8,128)(2,1)S(1)}, bf16[400,256]{1,0:T(8,128)(2,1)S(1)}, u32[]{:S(2)}, u32[]{:S(2)}) collective-permute-start(bf16[400,256]{1,0:T(8,128)(2,1)S(1)} %get-tuple-element.27), channel_id=1, source_target_pairs={{0,12},{4,8},{8,4},{12,0},{1,13},{5,9},{9,5},{13,1},{2,14},{6,10},... | collective-permute-start | bytes 614408 | tf_op jit(solution)/shard_map/ppermute | solution.py:375
  12.8 5.1 %collective-permute-start.7 = (bf16[272,256]{1,0:T(8,128)(2,1)S(1)}, bf16[272,256]{1,0:T(8,128)(2,1)S(1)}, u32[]{:S(2)}, u32[]{:S(2)}) collective-permute-start(bf16[272,256]{1,0:T(8,128)(2,1)S(1)} %collective-permute-done.5.refs_17_), channel_id=1, source_target_pairs={{0,1},{1,0},{2,3},{3,2},{4,5},{5,4},{6,7},{7,6},{8,9},{9,8},{10,11... | collective-permute-start | bytes 417800 | tf_op jit(solution)/shard_map/ppermute | solution.py:367
  13.4 6.1 %collective-permute-start.4 = (bf16[272,256]{1,0:T(8,128)(2,1)S(1)}, bf16[272,256]{1,0:T(8,128)(2,1)S(1)}, u32[]{:S(2)}, u32[]{:S(2)}) collective-permute-start(bf16[272,256]{1,0:T(8,128)(2,1)S(1)} %collective-permute-done.3.refs_15_), channel_id=1, source_target_pairs={{0,16},{16,0},{1,17},{17,1},{2,18},{18,2},{3,19},{19,3},{4,20},{20... | collective-permute-start | bytes 417800 | tf_op jit(solution)/shard_map/ppermute | solution.py:372
  15.6 3.9 %collective-permute-start.6 = (bf16[272,256]{1,0:T(8,128)(2,1)S(1)}, bf16[272,256]{1,0:T(8,128)(2,1)S(1)}, u32[]{:S(2)}, u32[]{:S(2)}) collective-permute-start(bf16[272,256]{1,0:T(8,128)(2,1)S(1)} %collective-permute-done.5.refs_17_), channel_id=1, source_target_pairs={{0,16},{16,0},{1,17},{17,1},{2,18},{18,2},{3,19},{19,3},{4,20},{20... | collective-permute-start | bytes 417800 | tf_op jit(solution)/shard_map/ppermute | solution.py:372
  17.8 1.7 %collective-permute-start.8 = (bf16[272,256]{1,0:T(8,128)(2,1)S(1)}, bf16[272,256]{1,0:T(8,128)(2,1)S(1)}, u32[]{:S(2)}, u32[]{:S(2)}) collective-permute-start(bf16[272,256]{1,0:T(8,128)(2,1)S(1)} %collective-permute-done.7.refs_19_), channel_id=1, source_target_pairs={{0,16},{16,0},{1,17},{17,1},{2,18},{18,2},{3,19},{19,3},{4,20},{20... | collective-permute-start | bytes 417800 | tf_op jit(solution)/shard_map/ppermute | solution.py:372
  27.7 3.6 %collective-permute-start.12 = (bf16[1024,256]{1,0:T(8,128)(2,1)S(1)}, bf16[1024,256]{1,0:T(8,128)(2,1)S(1)}, u32[]{:S(2)}, u32[]{:S(2)}) collective-permute-start(bf16[1024,256]{1,0:T(8,128)(2,1)S(1)} %get-tuple-element.42), channel_id=1, source_target_pairs={{0,16},{16,0},{1,17},{17,1},{2,18},{18,2},{3,19},{19,3},{4,20},{20... | collective-permute-start | bytes 1572872 | tf_op jit(solution)/shard_map/ppermute | solution.py:440
  27.8 8.1 %collective-permute-start.9 = (bf16[400,256]{1,0:T(8,128)(2,1)S(1)}, bf16[400,256]{1,0:T(8,128)(2,1)S(1)}, u32[]{:S(2)}, u32[]{:S(2)}) collective-permute-start(bf16[400,256]{1,0:T(8,128)(2,1)S(1)} %get-tuple-element.36), channel_id=1, source_target_pairs={{4,0},{0,4},{12,8},{8,12},{5,1},{1,5},{13,9},{9,13},{6,2},{2,6},{1... | collective-permute-start | bytes 614408 | tf_op jit(solution)/shard_map/ppermute | solution.py:477
  29.2 10.5 %collective-permute-start.10 = (bf16[400,256]{1,0:T(8,128)(2,1)S(1)}, bf16[400,256]{1,0:T(8,128)(2,1)S(1)}, u32[]{:S(2)}, u32[]{:S(2)}) collective-permute-start(bf16[400,256]{1,0:T(8,128)(2,1)S(1)} %get-tuple-element.37), channel_id=1, source_target_pairs={{8,0},{12,4},{0,8},{4,12},{9,1},{13,5},{1,9},{5,13},{10,2},{14,6},... | collective-permute-start | bytes 614408 | tf_op jit(solution)/shard_map/ppermute | solution.py:477
  30.7 9.9 %collective-permute-start.11 = (bf16[400,256]{1,0:T(8,128)(2,1)S(1)}, bf16[400,256]{1,0:T(8,128)(2,1)S(1)}, u32[]{:S(2)}, u32[]{:S(2)}) collective-permute-start(bf16[400,256]{1,0:T(8,128)(2,1)S(1)} %get-tuple-element.38), channel_id=1, source_target_pairs={{12,0},{8,4},{4,8},{0,12},{13,1},{9,5},{5,9},{1,13},{14,2},{10,6},... | collective-permute-start | bytes 614408 | tf_op jit(solution)/shard_map/ppermute | solution.py:477
  31.5 10.6 %collective-permute-start.13 = (bf16[256,256]{1,0:T(8,128)(2,1)S(1)}, bf16[256,256]{1,0:T(8,128)(2,1)S(1)}, u32[]{:S(2)}, u32[]{:S(2)}) collective-permute-start(bf16[256,256]{1,0:T(8,128)(2,1)S(1)} %get-tuple-element.44), channel_id=1, source_target_pairs={{0,1},{1,0},{2,3},{3,2},{4,5},{5,4},{6,7},{7,6},{8,9},{9,8},{10,11... | collective-permute-start | bytes 393224 | tf_op jit(solution)/shard_map/ppermute | solution.py:462
  32.5 13.1 %collective-permute-start.14 = (bf16[256,256]{1,0:T(8,128)(2,1)S(1)}, bf16[256,256]{1,0:T(8,128)(2,1)S(1)}, u32[]{:S(2)}, u32[]{:S(2)}) collective-permute-start(bf16[256,256]{1,0:T(8,128)(2,1)S(1)} %get-tuple-element.45), channel_id=1, source_target_pairs={{0,2},{1,3},{2,0},{3,1},{4,6},{5,7},{6,4},{7,5},{8,10},{9,11},{10,... | collective-permute-start | bytes 393224 | tf_op jit(solution)/shard_map/ppermute | solution.py:462
  35.9 9.8 %collective-permute-start.15 = (bf16[256,256]{1,0:T(8,128)(2,1)S(1)}, bf16[256,256]{1,0:T(8,128)(2,1)S(1)}, u32[]{:S(2)}, u32[]{:S(2)}) collective-permute-start(bf16[256,256]{1,0:T(8,128)(2,1)S(1)} %get-tuple-element.46), channel_id=1, source_target_pairs={{0,3},{1,2},{2,1},{3,0},{4,7},{5,6},{6,5},{7,4},{8,11},{9,10},{10,... | collective-permute-start | bytes 393224 | tf_op jit(solution)/shard_map/ppermute | solution.py:462

commit v6 on v5

--- a/solution.py
+++ b/solution.py
@@ -289,11 +289,12 @@
         out[...] = total.astype(out.dtype)
 
 
-def shard_sum_kernel(own, *refs):
-    total = own[...]
-    for term in refs[:-1]:
+def shard_sum_kernel(*refs):
+    (*terms, out) = refs
+    total = terms[0][...].astype(jnp.float32)
+    for term in terms[1:]:
         total = total + term[...].astype(jnp.float32)
-    refs[-1][...] = total
+    out[...] = total.astype(out.dtype)
 
 
 def home_kernel(per, partners, *refs):
@@ -436,12 +437,16 @@
         return lax.axis_index(axis), [to for to, _, _ in peers(axis)]
 
     shard_rows = shard * items // ntow
+    wide_terms = [nblk == 4 and n == 1 for n in range(nblk - 1)]
     if split:
         got = [lax.ppermute(sent, "tower", p) for sent, (_, _, p) in zip(sends, tow_peers)]
         own, *leaving = pl.pallas_call(
             functools.partial(tower_sum_kernel, nblk, functools.partial(partners, "blk")),
             out_shape=[pltpu.VMEM((shard_rows, width), jnp.float32)]
-            + [pltpu.VMEM((shard_rows, width), jnp.bfloat16)] * (nblk - 1),
+            + [
+                pltpu.VMEM((shard_rows, width), jnp.float32 if stays else jnp.bfloat16)
+                for stays in wide_terms
+            ],
             in_specs=[vmem] * (1 + len(got)),
             out_specs=[vmem] * nblk,
             compiler_params=params,
@@ -459,11 +464,24 @@
         leaving = [pick(total, to).astype(jnp.bfloat16) for to, _, _ in blk_peers]
     own, *rest = (own, *leaving, *query_grads)
     leaving, query_grads = rest[: nblk - 1], rest[nblk - 1 :]
-    terms = [lax.ppermute(sent, "blk", p) for sent, (_, _, p) in zip(leaving, blk_peers)]
+    if nblk == 4:
+        (_, _, near), (_, _, over) = blk_peers[:2]
+        to_near, to_over, to_far = leaving
+        joined = pl.pallas_call(
+            shard_sum_kernel,
+            out_shape=pltpu.VMEM((shard_rows, width), jnp.bfloat16),
+            in_specs=[vmem, vmem],
+            out_specs=vmem,
+            compiler_params=params,
+            name="join",
+        )(to_over, lax.ppermute(to_far, "blk", near))
+        terms = [lax.ppermute(joined, "blk", over), lax.ppermute(to_near, "blk", near)]
+    else:
+        terms = [lax.ppermute(sent, "blk", p) for sent, (_, _, p) in zip(leaving, blk_peers)]
     panel_grads = pl.pallas_call(
         shard_sum_kernel,
         out_shape=jax.ShapeDtypeStruct((shard_rows, width), jnp.float32),
-        in_specs=[vmem] * nblk,
+        in_specs=[vmem] * (1 + len(terms)),
         out_specs=vmem,
         compiler_params=params,
         cost_estimate=pl.CostEstimate(flops=10**9, bytes_accessed=10**7, transcendentals=0),

time: 46.5 us -> 45.6 us (0.981)
  starting transfers between devices: 21.4 us -> 18 us
  waiting for transfers between devices: 12.4 us -> 14.9 us
    ppermute x3, waiting for transfers between devices: 1.11 us -> 5.18 us  [shards(): blocks.append(lax.ppermute(block, 'group', home))]
    ppermute x3, waiting for transfers between devices: 3.5 us -> 0.03 us  [the longest x1 0.02 us: shards(): lax.ppermute(to_far, 'blk', near)]
    ppermute x3, starting transfers between devices: 8.03 us -> 4.7 us  [the longest x1 2.61 us: shards(): lax.ppermute(joined, 'blk', over)]
    ppermute x1, waiting for transfers between devices: 0.01 us -> 1.9 us  [shards(): lax.ppermute(sent, 'tower', p)]
where the time goes in v6:
time: 45.6 us; the launch traced here: 45.5 us
  starting transfers between devices  18 us (39%)
  waiting for transfers between devices  14.9 us (33%)
  Pallas kernels  11.9 us (26%)
  between operations  0.72 us (2%)
    pallas_call x1, Pallas kernels, shards(): pl.pallas_call(functools.partial(score_kernel, dims), out_shape=[pltpu.VM...  8.17 us
    ppermute x2, starting transfers between devices, shards(): lax.ppermute(message, 'blk', pattern)  5.68 us
    ppermute x3, waiting for transfers between devices, shards(): blocks.append(lax.ppermute(block, 'group', home))  5.18 us
    ppermute x3, waiting for transfers between devices, shards(): lax.ppermute(leaving[n * per + i], 'group', pattern)  3.82 us
    ppermute x3, starting transfers between devices, shards(): blocks.append(lax.ppermute(block, 'group', home))  3.49 us
    ppermute x3, starting transfers between devices, shards(): lax.ppermute(leaving[n * per + i], 'group', pattern)  3.49 us
    ppermute x1, starting transfers between devices, shards(): lax.ppermute(joined, 'blk', over)  2.61 us
    ppermute x1, waiting for transfers between devices, shards(): piece = lax.ppermute(near[1], 'blk', blk_peers[0][2])  2.22 us
  transfers between devices with their start and end apart: 16, of which 7 were waited for; matrix products, arithmetic and copies ran while one was open for 0% of the time, Pallas kernels for 3%

profile of v6, /device:TPU:0, one launch (start us, length us, event | category | flops | bytes accessed | tf_op | source)
XLA Modules:
  0.0 45.5 jit_solution(12411630518580975838)
XLA Ops:
  0.6 1.3 %messages.1 = (bf16[272,256]{1,0:T(8,128)(2,1)S(1)}, bf16[400,256]{1,0:T(8,128)(2,1)S(1)}, bf16[400,256]{1,0:T(8,128)(2,1)S(1)}, bf16[400,256]{1,0:T(8,128)(2,1)S(1)}) custom-call(bf16[512,256]{1,0:T(8,128)(2,1)} %bitcast.3, bf16[16,32]{1,0:T(8,128)(2,1)} %bitcast.5, bf16[4,384,256]{2,1,0:T(8,128)(2,1)} %refs_4_.1, s32[4,64]{1,0:T(4,128)} %refs_1_.1, ...), custom_call_target="tpu_custom_call" | custom-call | tf_op jit(solution)/shard_map/messages/pallas_call | solution.py:345
  1.9 4.1 %collective-permute-start.5 = (bf16[272,256]{1,0:T(8,128)(2,1)S(1)}, bf16[272,256]{1,0:T(8,128)(2,1)S(1)}, u32[]{:S(2)}, u32[]{:S(2)}) collective-permute-start(bf16[272,256]{1,0:T(8,128)(2,1)S(1)} %get-tuple-element.28), channel_id=1, source_target_pairs={{0,2},{1,3},{2,0},{3,1},{4,6},{5,7},{6,4},{7,5},{8,10},{9,11},{10,... | collective-permute-start | bytes 417800 | tf_op jit(solution)/shard_map/ppermute | solution.py:363
  6.0 1.6 %collective-permute-start.3 = (bf16[272,256]{1,0:T(8,128)(2,1)S(1)}, bf16[272,256]{1,0:T(8,128)(2,1)S(1)}, u32[]{:S(2)}, u32[]{:S(2)}) collective-permute-start(bf16[272,256]{1,0:T(8,128)(2,1)S(1)} %get-tuple-element.28), channel_id=1, source_target_pairs={{0,1},{1,0},{2,3},{3,2},{4,5},{5,4},{6,7},{7,6},{8,9},{9,8},{10,11... | collective-permute-start | bytes 417800 | tf_op jit(solution)/shard_map/ppermute | solution.py:363
  7.6 1.5 %collective-permute-start = (bf16[400,256]{1,0:T(8,128)(2,1)S(1)}, bf16[400,256]{1,0:T(8,128)(2,1)S(1)}, u32[]{:S(2)}, u32[]{:S(2)}) collective-permute-start(bf16[400,256]{1,0:T(8,128)(2,1)S(1)} %get-tuple-element.25), channel_id=1, source_target_pairs={{0,4},{4,0},{8,12},{12,8},{1,5},{5,1},{9,13},{13,9},{2,6},{6,2},{1... | collective-permute-start | bytes 614408 | tf_op jit(solution)/shard_map/ppermute | solution.py:376
  9.1 1.5 %collective-permute-start.1 = (bf16[400,256]{1,0:T(8,128)(2,1)S(1)}, bf16[400,256]{1,0:T(8,128)(2,1)S(1)}, u32[]{:S(2)}, u32[]{:S(2)}) collective-permute-start(bf16[400,256]{1,0:T(8,128)(2,1)S(1)} %get-tuple-element.26), channel_id=1, source_target_pairs={{0,8},{4,12},{8,0},{12,4},{1,9},{5,13},{9,1},{13,5},{2,10},{6,14},... | collective-permute-start | bytes 614408 | tf_op jit(solution)/shard_map/ppermute | solution.py:376
  10.6 0.5 %collective-permute-start.2 = (bf16[400,256]{1,0:T(8,128)(2,1)S(1)}, bf16[400,256]{1,0:T(8,128)(2,1)S(1)}, u32[]{:S(2)}, u32[]{:S(2)}) collective-permute-start(bf16[400,256]{1,0:T(8,128)(2,1)S(1)} %get-tuple-element.27), channel_id=1, source_target_pairs={{0,12},{4,8},{8,4},{12,0},{1,13},{5,9},{9,5},{13,1},{2,14},{6,10},... | collective-permute-start | bytes 614408 | tf_op jit(solution)/shard_map/ppermute | solution.py:376
  11.1 1.7 %collective-permute-done.5.refs_17_ = bf16[272,256]{1,0:T(8,128)(2,1)S(1)} collective-permute-done((bf16[272,256]{1,0:T(8,128)(2,1)S(1)}, bf16[272,256]{1,0:T(8,128)(2,1)S(1)}, u32[]{:S(2)}, u32[]{:S(2)}) %collective-permute-start.5) | collective-permute-done | bytes 139296 | tf_op jit(solution)/shard_map/ppermute | solution.py:363
  12.8 0.6 %collective-permute-start.7 = (bf16[272,256]{1,0:T(8,128)(2,1)S(1)}, bf16[272,256]{1,0:T(8,128)(2,1)S(1)}, u32[]{:S(2)}, u32[]{:S(2)}) collective-permute-start(bf16[272,256]{1,0:T(8,128)(2,1)S(1)} %collective-permute-done.5.refs_17_), channel_id=1, source_target_pairs={{0,1},{1,0},{2,3},{3,2},{4,5},{5,4},{6,7},{7,6},{8,9},{9,8},{10,11... | collective-permute-start | bytes 417800 | tf_op jit(solution)/shard_map/ppermute | solution.py:368
  13.4 0.0 collective-permute-done.3.refs_15_
  13.4 0.0 collective-permute-start.4
  13.4 2.2 %collective-permute-done.refs_0_.refs_6_ = bf16[400,256]{1,0:T(8,128)(2,1)S(1)} collective-permute-done((bf16[400,256]{1,0:T(8,128)(2,1)S(1)}, bf16[400,256]{1,0:T(8,128)(2,1)S(1)}, u32[]{:S(2)}, u32[]{:S(2)}) %collective-permute-start) | collective-permute-done | bytes 204832 | tf_op jit(solution)/shard_map/ppermute | solution.py:376
  15.6 2.2 %collective-permute-done.7.refs_19_ = bf16[272,256]{1,0:T(8,128)(2,1)S(1)} collective-permute-done((bf16[272,256]{1,0:T(8,128)(2,1)S(1)}, bf16[272,256]{1,0:T(8,128)(2,1)S(1)}, u32[]{:S(2)}, u32[]{:S(2)}) %collective-permute-start.7) | collective-permute-done | bytes 139296 | tf_op jit(solution)/shard_map/ppermute | solution.py:368
  17.9 1.6 %collective-permute-done.1.refs_1_.refs_7_ = bf16[400,256]{1,0:T(8,128)(2,1)S(1)} collective-permute-done((bf16[400,256]{1,0:T(8,128)(2,1)S(1)}, bf16[400,256]{1,0:T(8,128)(2,1)S(1)}, u32[]{:S(2)}, u32[]{:S(2)}) %collective-permute-start.1) | collective-permute-done | bytes 204832 | tf_op jit(solution)/shard_map/ppermute | solution.py:376
  19.5 0.0 collective-permute-done.2.refs_2_.refs_8_
  19.5 0.0 collective-permute-done.4.refs_3_.refs_16_
  19.5 8.2 %score.1 = (bf16[400,256]{1,0:T(8,128)(2,1)S(1)}, bf16[400,256]{1,0:T(8,128)(2,1)S(1)}, bf16[400,256]{1,0:T(8,128)(2,1)S(1)}, bf16[400,256]{1,0:T(8,128)(2,1)S(1...) custom-call(s32[1,128]{1,0:T(1,128)} %refs_0_.1, s32[4,64]{1,0:T(4,128)} %refs_1_.1, s32[4,384]{1,0:T(4,128)} %refs_2_.1, ...), custom_call_target="tpu_custom_call" | custom-call | tf_op jit(solution)/shard_map/score/pallas_call | solution.py:396
  27.7 0.1 collective-permute-start.12
  27.8 1.9 %collective-permute-done.12.refs_0_ = bf16[1024,256]{1,0:T(8,128)(2,1)S(1)} collective-permute-done((bf16[1024,256]{1,0:T(8,128)(2,1)S(1)}, bf16[1024,256]{1,0:T(8,128)(2,1)S(1)}, u32[]{:S(2)}, u32[]{:S(2)}) %collective-permute-start.12) | collective-permute-done | bytes 524320 | tf_op jit(solution)/shard_map/ppermute | solution.py:442
  29.7 0.1 tower_sum.1
  29.8 0.9 %collective-permute-start.13 = (bf16[256,256]{1,0:T(8,128)(2,1)S(1)}, bf16[256,256]{1,0:T(8,128)(2,1)S(1)}, u32[]{:S(2)}, u32[]{:S(2)}) collective-permute-start(bf16[256,256]{1,0:T(8,128)(2,1)S(1)} %get-tuple-element.45), channel_id=1, source_target_pairs={{0,1},{1,0},{2,3},{3,2},{4,5},{5,4},{6,7},{7,6},{8,9},{9,8},{10,11... | collective-permute-start | bytes 393224 | tf_op jit(solution)/shard_map/ppermute | solution.py:477
  30.7 1.5 %collective-permute-start.9 = (bf16[400,256]{1,0:T(8,128)(2,1)S(1)}, bf16[400,256]{1,0:T(8,128)(2,1)S(1)}, u32[]{:S(2)}, u32[]{:S(2)}) collective-permute-start(bf16[400,256]{1,0:T(8,128)(2,1)S(1)} %get-tuple-element.36), channel_id=1, source_target_pairs={{4,0},{0,4},{12,8},{8,12},{5,1},{1,5},{13,9},{9,13},{6,2},{2,6},{1... | collective-permute-start | bytes 614408 | tf_op jit(solution)/shard_map/ppermute | solution.py:495
  32.3 1.5 %collective-permute-start.10 = (bf16[400,256]{1,0:T(8,128)(2,1)S(1)}, bf16[400,256]{1,0:T(8,128)(2,1)S(1)}, u32[]{:S(2)}, u32[]{:S(2)}) collective-permute-start(bf16[400,256]{1,0:T(8,128)(2,1)S(1)} %get-tuple-element.37), channel_id=1, source_target_pairs={{8,0},{12,4},{0,8},{4,12},{9,1},{13,5},{1,9},{5,13},{10,2},{14,6},... | collective-permute-start | bytes 614408 | tf_op jit(solution)/shard_map/ppermute | solution.py:495
  33.8 0.5 %collective-permute-start.11 = (bf16[400,256]{1,0:T(8,128)(2,1)S(1)}, bf16[400,256]{1,0:T(8,128)(2,1)S(1)}, u32[]{:S(2)}, u32[]{:S(2)}) collective-permute-start(bf16[400,256]{1,0:T(8,128)(2,1)S(1)} %get-tuple-element.38), channel_id=1, source_target_pairs={{12,0},{8,4},{4,8},{0,12},{13,1},{9,5},{5,9},{1,13},{14,2},{10,6},... | collective-permute-start | bytes 614408 | tf_op jit(solution)/shard_map/ppermute | solution.py:495
  34.2 1.1 %collective-permute-start.15 = (bf16[256,256]{1,0:T(8,128)(2,1)S(1)}, bf16[256,256]{1,0:T(8,128)(2,1)S(1)}, u32[]{:S(2)}, u32[]{:S(2)}) collective-permute-start(bf16[256,256]{1,0:T(8,128)(2,1)S(1)} %get-tuple-element.46), channel_id=1, source_target_pairs={{0,1},{1,0},{2,3},{3,2},{4,5},{5,4},{6,7},{7,6},{8,9},{9,8},{10,11... | collective-permute-start | bytes 393224 | tf_op jit(solution)/shard_map/ppermute | solution.py:478
  35.4 0.0 collective-permute-done.13.refs_1_
  35.4 2.6 %collective-permute-start.14 = (bf16[256,256]{1,0:T(8,128)(2,1)S(1)}, bf16[256,256]{1,0:T(8,128)(2,1)S(1)}, u32[]{:S(2)}, u32[]{:S(2)}) collective-permute-start(bf16[256,256]{1,0:T(8,128)(2,1)S(1)} %join.1), channel_id=1, source_target_pairs={{0,2},{1,3},{2,0},{3,1},{4,6},{5,7},{6,4},{7,5},{8,10},{9,11},{10,... | collective-permute-start | bytes 393224 | tf_op jit(solution)/shard_map/ppermute | solution.py:478
  38.0 0.7 %collective-permute-done.9.refs_1_ = bf16[400,256]{1,0:T(8,128)(2,1)S(1)} collective-permute-done((bf16[400,256]{1,0:T(8,128)(2,1)S(1)}, bf16[400,256]{1,0:T(8,128)(2,1)S(1)}, u32[]{:S(2)}, u32[]{:S(2)}) %collective-permute-start.9) | collective-permute-done | bytes 204832 | tf_op jit(solution)/shard_map/ppermute | solution.py:495
  38.7 4.5 %collective-permute-done.10.refs_2_ = bf16[400,256]{1,0:T(8,128)(2,1)S(1)} collective-permute-done((bf16[400,256]{1,0:T(8,128)(2,1)S(1)}, bf16[400,256]{1,0:T(8,128)(2,1)S(1)}, u32[]{:S(2)}, u32[]{:S(2)}) %collective-permute-start.10) | collective-permute-done | bytes 204832 | tf_op jit(solution)/shard_map/ppermute | solution.py:495
  43.2 0.0 collective-permute-done.11.refs_3_
  43.2 1.5 %home.1 = (bf16[4,384,256]{2,1,0:T(8,128)(2,1)}, bf16[4,384]{1,0:T(4,128)(2,1)}) custom-call(bf16[400,256]{1,0:T(8,128)(2,1)S(1)} %get-tuple-element.35.refs_0_, bf16[400,256]{1,0:T(8,128)(2,1)S(1)} %collective-permute-done.9.refs_1_, bf16[400,256]{1,0:T(8,128)(2,1)S(1)} %collective-permute-done.10.refs_2_, bf16[400,256]{1,0:T(8,128)(2,1)S(1)} %collective-permute-done.11.refs_3_), custom_call_target="tpu_custom_call" | custom-call | tf_op jit(solution)/shard_map/home/pallas_call | solution.py:496
  44.7 0.0 collective-permute-done.15.refs_2_
  44.7 0.8 %shard_sum.1 = f32[256,256]{1,0:T(8,128)} custom-call(f32[256,256]{1,0:T(8,128)S(1)} %get-tuple-element.43.refs_0_, bf16[256,256]{1,0:T(8,128)(2,1)S(1)} %collective-permute-done.14.refs_1_, bf16[256,256]{1,0:T(8,128)(2,1)S(1)} %collective-permute-done.15.refs_2_), custom_call_target="tpu_custom_call" | custom-call | flops 1000000000 | bytes 10000000 | tf_op jit(solution)/shard_map/shard_sum/pallas_call | solution.py:481
  (7 shorter events, 0.1 us)
Async XLA Ops:
  1.9 10.9 %collective-permute-start.5 = (bf16[272,256]{1,0:T(8,128)(2,1)S(1)}, bf16[272,256]{1,0:T(8,128)(2,1)S(1)}, u32[]{:S(2)}, u32[]{:S(2)}) collective-permute-start(bf16[272,256]{1,0:T(8,128)(2,1)S(1)} %get-tuple-element.28), channel_id=1, source_target_pairs={{0,2},{1,3},{2,0},{3,1},{4,6},{5,7},{6,4},{7,5},{8,10},{9,11},{10,... | collective-permute-start | bytes 417800 | tf_op jit(solution)/shard_map/ppermute | solution.py:363
  6.0 7.4 %collective-permute-start.3 = (bf16[272,256]{1,0:T(8,128)(2,1)S(1)}, bf16[272,256]{1,0:T(8,128)(2,1)S(1)}, u32[]{:S(2)}, u32[]{:S(2)}) collective-permute-start(bf16[272,256]{1,0:T(8,128)(2,1)S(1)} %get-tuple-element.28), channel_id=1, source_target_pairs={{0,1},{1,0},{2,3},{3,2},{4,5},{5,4},{6,7},{7,6},{8,9},{9,8},{10,11... | collective-permute-start | bytes 417800 | tf_op jit(solution)/shard_map/ppermute | solution.py:363
  7.6 8.0 %collective-permute-start = (bf16[400,256]{1,0:T(8,128)(2,1)S(1)}, bf16[400,256]{1,0:T(8,128)(2,1)S(1)}, u32[]{:S(2)}, u32[]{:S(2)}) collective-permute-start(bf16[400,256]{1,0:T(8,128)(2,1)S(1)} %get-tuple-element.25), channel_id=1, source_target_pairs={{0,4},{4,0},{8,12},{12,8},{1,5},{5,1},{9,13},{13,9},{2,6},{6,2},{1... | collective-permute-start | bytes 614408 | tf_op jit(solution)/shard_map/ppermute | solution.py:376
  9.1 10.4 %collective-permute-start.1 = (bf16[400,256]{1,0:T(8,128)(2,1)S(1)}, bf16[400,256]{1,0:T(8,128)(2,1)S(1)}, u32[]{:S(2)}, u32[]{:S(2)}) collective-permute-start(bf16[400,256]{1,0:T(8,128)(2,1)S(1)} %get-tuple-element.26), channel_id=1, source_target_pairs={{0,8},{4,12},{8,0},{12,4},{1,9},{5,13},{9,1},{13,5},{2,10},{6,14},... | collective-permute-start | bytes 614408 | tf_op jit(solution)/shard_map/ppermute | solution.py:376
  10.6 8.8 %collective-permute-start.2 = (bf16[400,256]{1,0:T(8,128)(2,1)S(1)}, bf16[400,256]{1,0:T(8,128)(2,1)S(1)}, u32[]{:S(2)}, u32[]{:S(2)}) collective-permute-start(bf16[400,256]{1,0:T(8,128)(2,1)S(1)} %get-tuple-element.27), channel_id=1, source_target_pairs={{0,12},{4,8},{8,4},{12,0},{1,13},{5,9},{9,5},{13,1},{2,14},{6,10},... | collective-permute-start | bytes 614408 | tf_op jit(solution)/shard_map/ppermute | solution.py:376
  12.8 5.1 %collective-permute-start.7 = (bf16[272,256]{1,0:T(8,128)(2,1)S(1)}, bf16[272,256]{1,0:T(8,128)(2,1)S(1)}, u32[]{:S(2)}, u32[]{:S(2)}) collective-permute-start(bf16[272,256]{1,0:T(8,128)(2,1)S(1)} %collective-permute-done.5.refs_17_), channel_id=1, source_target_pairs={{0,1},{1,0},{2,3},{3,2},{4,5},{5,4},{6,7},{7,6},{8,9},{9,8},{10,11... | collective-permute-start | bytes 417800 | tf_op jit(solution)/shard_map/ppermute | solution.py:368
  13.4 6.1 %collective-permute-start.4 = (bf16[272,256]{1,0:T(8,128)(2,1)S(1)}, bf16[272,256]{1,0:T(8,128)(2,1)S(1)}, u32[]{:S(2)}, u32[]{:S(2)}) collective-permute-start(bf16[272,256]{1,0:T(8,128)(2,1)S(1)} %collective-permute-done.3.refs_15_), channel_id=1, source_target_pairs={{0,16},{16,0},{1,17},{17,1},{2,18},{18,2},{3,19},{19,3},{4,20},{20... | collective-permute-start | bytes 417800 | tf_op jit(solution)/shard_map/ppermute | solution.py:373
  15.6 3.9 %collective-permute-start.6 = (bf16[272,256]{1,0:T(8,128)(2,1)S(1)}, bf16[272,256]{1,0:T(8,128)(2,1)S(1)}, u32[]{:S(2)}, u32[]{:S(2)}) collective-permute-start(bf16[272,256]{1,0:T(8,128)(2,1)S(1)} %collective-permute-done.5.refs_17_), channel_id=1, source_target_pairs={{0,16},{16,0},{1,17},{17,1},{2,18},{18,2},{3,19},{19,3},{4,20},{20... | collective-permute-start | bytes 417800 | tf_op jit(solution)/shard_map/ppermute | solution.py:373
  17.8 1.7 %collective-permute-start.8 = (bf16[272,256]{1,0:T(8,128)(2,1)S(1)}, bf16[272,256]{1,0:T(8,128)(2,1)S(1)}, u32[]{:S(2)}, u32[]{:S(2)}) collective-permute-start(bf16[272,256]{1,0:T(8,128)(2,1)S(1)} %collective-permute-done.7.refs_19_), channel_id=1, source_target_pairs={{0,16},{16,0},{1,17},{17,1},{2,18},{18,2},{3,19},{19,3},{4,20},{20... | collective-permute-start | bytes 417800 | tf_op jit(solution)/shard_map/ppermute | solution.py:373
  27.7 2.0 %collective-permute-start.12 = (bf16[1024,256]{1,0:T(8,128)(2,1)S(1)}, bf16[1024,256]{1,0:T(8,128)(2,1)S(1)}, u32[]{:S(2)}, u32[]{:S(2)}) collective-permute-start(bf16[1024,256]{1,0:T(8,128)(2,1)S(1)} %get-tuple-element.42), channel_id=1, source_target_pairs={{0,16},{16,0},{1,17},{17,1},{2,18},{18,2},{3,19},{19,3},{4,20},{20... | collective-permute-start | bytes 1572872 | tf_op jit(solution)/shard_map/ppermute | solution.py:442
  29.8 5.6 %collective-permute-start.13 = (bf16[256,256]{1,0:T(8,128)(2,1)S(1)}, bf16[256,256]{1,0:T(8,128)(2,1)S(1)}, u32[]{:S(2)}, u32[]{:S(2)}) collective-permute-start(bf16[256,256]{1,0:T(8,128)(2,1)S(1)} %get-tuple-element.45), channel_id=1, source_target_pairs={{0,1},{1,0},{2,3},{3,2},{4,5},{5,4},{6,7},{7,6},{8,9},{9,8},{10,11... | collective-permute-start | bytes 393224 | tf_op jit(solution)/shard_map/ppermute | solution.py:477
  30.7 8.0 %collective-permute-start.9 = (bf16[400,256]{1,0:T(8,128)(2,1)S(1)}, bf16[400,256]{1,0:T(8,128)(2,1)S(1)}, u32[]{:S(2)}, u32[]{:S(2)}) collective-permute-start(bf16[400,256]{1,0:T(8,128)(2,1)S(1)} %get-tuple-element.36), channel_id=1, source_target_pairs={{4,0},{0,4},{12,8},{8,12},{5,1},{1,5},{13,9},{9,13},{6,2},{2,6},{1... | collective-permute-start | bytes 614408 | tf_op jit(solution)/shard_map/ppermute | solution.py:495
  32.3 10.9 %collective-permute-start.10 = (bf16[400,256]{1,0:T(8,128)(2,1)S(1)}, bf16[400,256]{1,0:T(8,128)(2,1)S(1)}, u32[]{:S(2)}, u32[]{:S(2)}) collective-permute-start(bf16[400,256]{1,0:T(8,128)(2,1)S(1)} %get-tuple-element.37), channel_id=1, source_target_pairs={{8,0},{12,4},{0,8},{4,12},{9,1},{13,5},{1,9},{5,13},{10,2},{14,6},... | collective-permute-start | bytes 614408 | tf_op jit(solution)/shard_map/ppermute | solution.py:495
  33.8 9.5 %collective-permute-start.11 = (bf16[400,256]{1,0:T(8,128)(2,1)S(1)}, bf16[400,256]{1,0:T(8,128)(2,1)S(1)}, u32[]{:S(2)}, u32[]{:S(2)}) collective-permute-start(bf16[400,256]{1,0:T(8,128)(2,1)S(1)} %get-tuple-element.38), channel_id=1, source_target_pairs={{12,0},{8,4},{4,8},{0,12},{13,1},{9,5},{5,9},{1,13},{14,2},{10,6},... | collective-permute-start | bytes 614408 | tf_op jit(solution)/shard_map/ppermute | solution.py:495
  34.2 10.5 %collective-permute-start.15 = (bf16[256,256]{1,0:T(8,128)(2,1)S(1)}, bf16[256,256]{1,0:T(8,128)(2,1)S(1)}, u32[]{:S(2)}, u32[]{:S(2)}) collective-permute-start(bf16[256,256]{1,0:T(8,128)(2,1)S(1)} %get-tuple-element.46), channel_id=1, source_target_pairs={{0,1},{1,0},{2,3},{3,2},{4,5},{5,4},{6,7},{7,6},{8,9},{9,8},{10,11... | collective-permute-start | bytes 393224 | tf_op jit(solution)/shard_map/ppermute | solution.py:478
  35.4 9.3 %collective-permute-start.14 = (bf16[256,256]{1,0:T(8,128)(2,1)S(1)}, bf16[256,256]{1,0:T(8,128)(2,1)S(1)}, u32[]{:S(2)}, u32[]{:S(2)}) collective-permute-start(bf16[256,256]{1,0:T(8,128)(2,1)S(1)} %join.1), channel_id=1, source_target_pairs={{0,2},{1,3},{2,0},{3,1},{4,6},{5,7},{6,4},{7,5},{8,10},{9,11},{10,... | collective-permute-start | bytes 393224 | tf_op jit(solution)/shard_map/ppermute | solution.py:478

commit v7 on v6

--- a/solution.py
+++ b/solution.py
@@ -295,6 +295,10 @@
     for term in terms[1:]:
         total = total + term[...].astype(jnp.float32)
     out[...] = total.astype(out.dtype)
+
+
+def land_kernel(block, out):
+    out[...] = block[...]
 
 
 def home_kernel(per, partners, *refs):
@@ -493,6 +497,15 @@
         home = [(d, s) for s, d in pattern]
         for block in query_grads[(n + 1) * per : (n + 2) * per]:
             blocks.append(lax.ppermute(block, "group", home))
+    blocks[-1] = pl.pallas_call(
+        land_kernel,
+        out_shape=jax.ShapeDtypeStruct(blocks[-1].shape, blocks[-1].dtype),
+        in_specs=[vmem],
+        out_specs=vmem,
+        compiler_params=params,
+        cost_estimate=pl.CostEstimate(flops=COST, bytes_accessed=COST // 1000, transcendentals=0),
+        name="land",
+    )(blocks[-1])
     back_q, back_l = pl.pallas_call(
         functools.partial(home_kernel, per, functools.partial(partners, "group")),
         out_shape=[

time: 45.6 us -> 45.3 us (level)
  waiting for transfers between devices: 14.9 us -> 13.2 us
  starting transfers between devices: 18 us -> 19.4 us
    ppermute x3, waiting for transfers between devices: 5.18 us -> 1.88 us  [shards(): blocks.append(lax.ppermute(block, 'group', home))]
    ppermute x1, waiting for transfers between devices: 0.01 us -> 2.32 us  [shards(): lax.ppermute(joined, 'blk', over)]
    ppermute x1, waiting for transfers between devices: 1.9 us -> 0.01 us  [shards(): lax.ppermute(sent, 'tower', p)]
    ppermute x1, waiting for transfers between devices: 0.02 us -> 1.27 us  [shards(): lax.ppermute(to_far, 'blk', near)]
    ppermute x3, starting transfers between devices: 3.49 us -> 4.64 us  [shards(): blocks.append(lax.ppermute(block, 'group', home))]
  transfers between devices with their start and end apart: 16 -> 16, of which waited for: 7 -> 7; matrix products, arithmetic and copies ran while one was open for 0% -> 0% of each run, Pallas kernels for 3% -> 4%
where the time goes in v7:
time: 45.3 us; the launch traced here: 45.2 us
  starting transfers between devices  19.4 us (43%)
  waiting for transfers between devices  13.2 us (29%)
  Pallas kernels  11.9 us (26%)
  between operations  0.71 us (2%)
    pallas_call x1, Pallas kernels, shards(): pl.pallas_call(functools.partial(score_kernel, dims), out_shape=[pltpu.VM...  8.19 us
    ppermute x2, starting transfers between devices, shards(): lax.ppermute(message, 'blk', pattern)  5.68 us
    ppermute x3, starting transfers between devices, shards(): blocks.append(lax.ppermute(block, 'group', home))  4.64 us
    ppermute x3, waiting for transfers between devices, shards(): lax.ppermute(leaving[n * per + i], 'group', pattern)  3.82 us
    ppermute x3, starting transfers between devices, shards(): lax.ppermute(leaving[n * per + i], 'group', pattern)  3.49 us
    ppermute x1, starting transfers between devices, shards(): lax.ppermute(joined, 'blk', over)  2.76 us
    ppermute x1, waiting for transfers between devices, shards(): lax.ppermute(joined, 'blk', over)  2.32 us
    ppermute x1, waiting for transfers between devices, shards(): piece = lax.ppermute(near[1], 'blk', blk_peers[0][2])  2.22 us
  transfers between devices with their start and end apart: 16, of which 7 were waited for; matrix products, arithmetic and copies ran while one was open for 0% of the time, Pallas kernels for 4%

profile of v7, /device:TPU:0, one launch (start us, length us, event | category | flops | bytes accessed | tf_op | source)
XLA Modules:
  0.0 45.2 jit_solution(7938262603559937320)
XLA Ops:
  0.6 1.3 %messages.1 = (bf16[272,256]{1,0:T(8,128)(2,1)S(1)}, bf16[400,256]{1,0:T(8,128)(2,1)S(1)}, bf16[400,256]{1,0:T(8,128)(2,1)S(1)}, bf16[400,256]{1,0:T(8,128)(2,1)S(1)}) custom-call(bf16[512,256]{1,0:T(8,128)(2,1)} %bitcast.3, bf16[16,32]{1,0:T(8,128)(2,1)} %bitcast.5, bf16[4,384,256]{2,1,0:T(8,128)(2,1)} %refs_4_.1, s32[4,64]{1,0:T(4,128)} %refs_1_.1, ...), custom_call_target="tpu_custom_call" | custom-call | tf_op jit(solution)/shard_map/messages/pallas_call | solution.py:349
  1.9 4.1 %collective-permute-start.5 = (bf16[272,256]{1,0:T(8,128)(2,1)S(1)}, bf16[272,256]{1,0:T(8,128)(2,1)S(1)}, u32[]{:S(2)}, u32[]{:S(2)}) collective-permute-start(bf16[272,256]{1,0:T(8,128)(2,1)S(1)} %get-tuple-element.28), channel_id=1, source_target_pairs={{0,2},{1,3},{2,0},{3,1},{4,6},{5,7},{6,4},{7,5},{8,10},{9,11},{10,... | collective-permute-start | bytes 417800 | tf_op jit(solution)/shard_map/ppermute | solution.py:367
  6.0 1.6 %collective-permute-start.3 = (bf16[272,256]{1,0:T(8,128)(2,1)S(1)}, bf16[272,256]{1,0:T(8,128)(2,1)S(1)}, u32[]{:S(2)}, u32[]{:S(2)}) collective-permute-start(bf16[272,256]{1,0:T(8,128)(2,1)S(1)} %get-tuple-element.28), channel_id=1, source_target_pairs={{0,1},{1,0},{2,3},{3,2},{4,5},{5,4},{6,7},{7,6},{8,9},{9,8},{10,11... | collective-permute-start | bytes 417800 | tf_op jit(solution)/shard_map/ppermute | solution.py:367
  7.6 1.5 %collective-permute-start = (bf16[400,256]{1,0:T(8,128)(2,1)S(1)}, bf16[400,256]{1,0:T(8,128)(2,1)S(1)}, u32[]{:S(2)}, u32[]{:S(2)}) collective-permute-start(bf16[400,256]{1,0:T(8,128)(2,1)S(1)} %get-tuple-element.25), channel_id=1, source_target_pairs={{0,4},{4,0},{8,12},{12,8},{1,5},{5,1},{9,13},{13,9},{2,6},{6,2},{1... | collective-permute-start | bytes 614408 | tf_op jit(solution)/shard_map/ppermute | solution.py:380
  9.1 1.5 %collective-permute-start.1 = (bf16[400,256]{1,0:T(8,128)(2,1)S(1)}, bf16[400,256]{1,0:T(8,128)(2,1)S(1)}, u32[]{:S(2)}, u32[]{:S(2)}) collective-permute-start(bf16[400,256]{1,0:T(8,128)(2,1)S(1)} %get-tuple-element.26), channel_id=1, source_target_pairs={{0,8},{4,12},{8,0},{12,4},{1,9},{5,13},{9,1},{13,5},{2,10},{6,14},... | collective-permute-start | bytes 614408 | tf_op jit(solution)/shard_map/ppermute | solution.py:380
  10.6 0.5 %collective-permute-start.2 = (bf16[400,256]{1,0:T(8,128)(2,1)S(1)}, bf16[400,256]{1,0:T(8,128)(2,1)S(1)}, u32[]{:S(2)}, u32[]{:S(2)}) collective-permute-start(bf16[400,256]{1,0:T(8,128)(2,1)S(1)} %get-tuple-element.27), channel_id=1, source_target_pairs={{0,12},{4,8},{8,4},{12,0},{1,13},{5,9},{9,5},{13,1},{2,14},{6,10},... | collective-permute-start | bytes 614408 | tf_op jit(solution)/shard_map/ppermute | solution.py:380
  11.1 1.7 %collective-permute-done.5.refs_17_ = bf16[272,256]{1,0:T(8,128)(2,1)S(1)} collective-permute-done((bf16[272,256]{1,0:T(8,128)(2,1)S(1)}, bf16[272,256]{1,0:T(8,128)(2,1)S(1)}, u32[]{:S(2)}, u32[]{:S(2)}) %collective-permute-start.5) | collective-permute-done | bytes 139296 | tf_op jit(solution)/shard_map/ppermute | solution.py:367
  12.8 0.6 %collective-permute-start.7 = (bf16[272,256]{1,0:T(8,128)(2,1)S(1)}, bf16[272,256]{1,0:T(8,128)(2,1)S(1)}, u32[]{:S(2)}, u32[]{:S(2)}) collective-permute-start(bf16[272,256]{1,0:T(8,128)(2,1)S(1)} %collective-permute-done.5.refs_17_), channel_id=1, source_target_pairs={{0,1},{1,0},{2,3},{3,2},{4,5},{5,4},{6,7},{7,6},{8,9},{9,8},{10,11... | collective-permute-start | bytes 417800 | tf_op jit(solution)/shard_map/ppermute | solution.py:372
  13.4 0.0 collective-permute-done.3.refs_15_
  13.4 0.0 collective-permute-start.4
  13.4 2.2 %collective-permute-done.refs_0_.refs_6_ = bf16[400,256]{1,0:T(8,128)(2,1)S(1)} collective-permute-done((bf16[400,256]{1,0:T(8,128)(2,1)S(1)}, bf16[400,256]{1,0:T(8,128)(2,1)S(1)}, u32[]{:S(2)}, u32[]{:S(2)}) %collective-permute-start) | collective-permute-done | bytes 204832 | tf_op jit(solution)/shard_map/ppermute | solution.py:380
  15.6 0.0 collective-permute-start.6
  15.6 2.2 %collective-permute-done.7.refs_19_ = bf16[272,256]{1,0:T(8,128)(2,1)S(1)} collective-permute-done((bf16[272,256]{1,0:T(8,128)(2,1)S(1)}, bf16[272,256]{1,0:T(8,128)(2,1)S(1)}, u32[]{:S(2)}, u32[]{:S(2)}) %collective-permute-start.7) | collective-permute-done | bytes 139296 | tf_op jit(solution)/shard_map/ppermute | solution.py:372
  17.8 0.0 collective-permute-start.8
  17.9 1.6 %collective-permute-done.1.refs_1_.refs_7_ = bf16[400,256]{1,0:T(8,128)(2,1)S(1)} collective-permute-done((bf16[400,256]{1,0:T(8,128)(2,1)S(1)}, bf16[400,256]{1,0:T(8,128)(2,1)S(1)}, u32[]{:S(2)}, u32[]{:S(2)}) %collective-permute-start.1) | collective-permute-done | bytes 204832 | tf_op jit(solution)/shard_map/ppermute | solution.py:380
  19.5 0.0 collective-permute-done.8.refs_20_
  19.5 8.2 %score.1 = (bf16[400,256]{1,0:T(8,128)(2,1)S(1)}, bf16[400,256]{1,0:T(8,128)(2,1)S(1)}, bf16[400,256]{1,0:T(8,128)(2,1)S(1)}, bf16[400,256]{1,0:T(8,128)(2,1)S(1...) custom-call(s32[1,128]{1,0:T(1,128)} %refs_0_.1, s32[4,64]{1,0:T(4,128)} %refs_1_.1, s32[4,384]{1,0:T(4,128)} %refs_2_.1, ...), custom_call_target="tpu_custom_call" | custom-call | tf_op jit(solution)/shard_map/score/pallas_call | solution.py:400
  27.7 0.1 collective-permute-start.12
  27.8 2.3 %collective-permute-start.11 = (bf16[400,256]{1,0:T(8,128)(2,1)S(1)}, bf16[400,256]{1,0:T(8,128)(2,1)S(1)}, u32[]{:S(2)}, u32[]{:S(2)}) collective-permute-start(bf16[400,256]{1,0:T(8,128)(2,1)S(1)} %get-tuple-element.38), channel_id=1, source_target_pairs={{12,0},{8,4},{4,8},{0,12},{13,1},{9,5},{5,9},{1,13},{14,2},{10,6},... | collective-permute-start | bytes 614408 | tf_op jit(solution)/shard_map/ppermute | solution.py:499
  30.1 0.0 collective-permute-done.12.refs_0_
  30.1 0.1 tower_sum.1
  30.2 1.2 %collective-permute-start.13 = (bf16[256,256]{1,0:T(8,128)(2,1)S(1)}, bf16[256,256]{1,0:T(8,128)(2,1)S(1)}, u32[]{:S(2)}, u32[]{:S(2)}) collective-permute-start(bf16[256,256]{1,0:T(8,128)(2,1)S(1)} %get-tuple-element.45), channel_id=1, source_target_pairs={{0,1},{1,0},{2,3},{3,2},{4,5},{5,4},{6,7},{7,6},{8,9},{9,8},{10,11... | collective-permute-start | bytes 393224 | tf_op jit(solution)/shard_map/ppermute | solution.py:481
  31.5 0.8 %collective-permute-start.9 = (bf16[400,256]{1,0:T(8,128)(2,1)S(1)}, bf16[400,256]{1,0:T(8,128)(2,1)S(1)}, u32[]{:S(2)}, u32[]{:S(2)}) collective-permute-start(bf16[400,256]{1,0:T(8,128)(2,1)S(1)} %get-tuple-element.36), channel_id=1, source_target_pairs={{4,0},{0,4},{12,8},{8,12},{5,1},{1,5},{13,9},{9,13},{6,2},{2,6},{1... | collective-permute-start | bytes 614408 | tf_op jit(solution)/shard_map/ppermute | solution.py:499
  32.2 1.5 %collective-permute-start.10 = (bf16[400,256]{1,0:T(8,128)(2,1)S(1)}, bf16[400,256]{1,0:T(8,128)(2,1)S(1)}, u32[]{:S(2)}, u32[]{:S(2)}) collective-permute-start(bf16[400,256]{1,0:T(8,128)(2,1)S(1)} %get-tuple-element.37), channel_id=1, source_target_pairs={{8,0},{12,4},{0,8},{4,12},{9,1},{13,5},{1,9},{5,13},{10,2},{14,6},... | collective-permute-start | bytes 614408 | tf_op jit(solution)/shard_map/ppermute | solution.py:499
  33.8 0.9 %collective-permute-start.15 = (bf16[256,256]{1,0:T(8,128)(2,1)S(1)}, bf16[256,256]{1,0:T(8,128)(2,1)S(1)}, u32[]{:S(2)}, u32[]{:S(2)}) collective-permute-start(bf16[256,256]{1,0:T(8,128)(2,1)S(1)} %get-tuple-element.46), channel_id=1, source_target_pairs={{0,1},{1,0},{2,3},{3,2},{4,5},{5,4},{6,7},{7,6},{8,9},{9,8},{10,11... | collective-permute-start | bytes 393224 | tf_op jit(solution)/shard_map/ppermute | solution.py:482
  34.7 1.3 %collective-permute-done.13.refs_1_ = bf16[256,256]{1,0:T(8,128)(2,1)S(1)} collective-permute-done((bf16[256,256]{1,0:T(8,128)(2,1)S(1)}, bf16[256,256]{1,0:T(8,128)(2,1)S(1)}, u32[]{:S(2)}, u32[]{:S(2)}) %collective-permute-start.13) | collective-permute-done | bytes 131104 | tf_op jit(solution)/shard_map/ppermute | solution.py:481
  36.0 2.8 %collective-permute-start.14 = (bf16[256,256]{1,0:T(8,128)(2,1)S(1)}, bf16[256,256]{1,0:T(8,128)(2,1)S(1)}, u32[]{:S(2)}, u32[]{:S(2)}) collective-permute-start(bf16[256,256]{1,0:T(8,128)(2,1)S(1)} %join.1), channel_id=1, source_target_pairs={{0,2},{1,3},{2,0},{3,1},{4,6},{5,7},{6,4},{7,5},{8,10},{9,11},{10,... | collective-permute-start | bytes 393224 | tf_op jit(solution)/shard_map/ppermute | solution.py:482
  38.8 1.9 %collective-permute-done.9.refs_1_ = bf16[400,256]{1,0:T(8,128)(2,1)S(1)} collective-permute-done((bf16[400,256]{1,0:T(8,128)(2,1)S(1)}, bf16[400,256]{1,0:T(8,128)(2,1)S(1)}, u32[]{:S(2)}, u32[]{:S(2)}) %collective-permute-start.9) | collective-permute-done | bytes 204832 | tf_op jit(solution)/shard_map/ppermute | solution.py:499
  40.7 0.0 collective-permute-done.10.refs_2_
  40.7 1.5 %home.1 = (bf16[4,384,256]{2,1,0:T(8,128)(2,1)}, bf16[4,384]{1,0:T(4,128)(2,1)}) custom-call(bf16[400,256]{1,0:T(8,128)(2,1)S(1)} %get-tuple-element.35.refs_0_, bf16[400,256]{1,0:T(8,128)(2,1)S(1)} %collective-permute-done.9.refs_1_, bf16[400,256]{1,0:T(8,128)(2,1)S(1)} %collective-permute-done.10.refs_2_, bf16[400,256]{1,0:T(8,128)(2,1)S(1)} %land.1.refs_3_), custom_call_target="tpu_custom_call" | custom-call | tf_op jit(solution)/shard_map/home/pallas_call | solution.py:509
  42.2 2.3 %collective-permute-done.14.refs_1_ = bf16[256,256]{1,0:T(8,128)(2,1)S(1)} collective-permute-done((bf16[256,256]{1,0:T(8,128)(2,1)S(1)}, bf16[256,256]{1,0:T(8,128)(2,1)S(1)}, u32[]{:S(2)}, u32[]{:S(2)}) %collective-permute-start.14) | collective-permute-done | bytes 131104 | tf_op jit(solution)/shard_map/ppermute | solution.py:482
  44.5 0.7 %shard_sum.1 = f32[256,256]{1,0:T(8,128)} custom-call(f32[256,256]{1,0:T(8,128)S(1)} %get-tuple-element.43.refs_0_, bf16[256,256]{1,0:T(8,128)(2,1)S(1)} %collective-permute-done.14.refs_1_, bf16[256,256]{1,0:T(8,128)(2,1)S(1)} %collective-permute-done.15.refs_2_), custom_call_target="tpu_custom_call" | custom-call | flops 1000000000 | bytes 10000000 | tf_op jit(solution)/shard_map/shard_sum/pallas_call | solution.py:485
  (8 shorter events, 0.1 us)
Async XLA Ops:
  1.9 10.9 %collective-permute-start.5 = (bf16[272,256]{1,0:T(8,128)(2,1)S(1)}, bf16[272,256]{1,0:T(8,128)(2,1)S(1)}, u32[]{:S(2)}, u32[]{:S(2)}) collective-permute-start(bf16[272,256]{1,0:T(8,128)(2,1)S(1)} %get-tuple-element.28), channel_id=1, source_target_pairs={{0,2},{1,3},{2,0},{3,1},{4,6},{5,7},{6,4},{7,5},{8,10},{9,11},{10,... | collective-permute-start | bytes 417800 | tf_op jit(solution)/shard_map/ppermute | solution.py:367
  6.0 7.4 %collective-permute-start.3 = (bf16[272,256]{1,0:T(8,128)(2,1)S(1)}, bf16[272,256]{1,0:T(8,128)(2,1)S(1)}, u32[]{:S(2)}, u32[]{:S(2)}) collective-permute-start(bf16[272,256]{1,0:T(8,128)(2,1)S(1)} %get-tuple-element.28), channel_id=1, source_target_pairs={{0,1},{1,0},{2,3},{3,2},{4,5},{5,4},{6,7},{7,6},{8,9},{9,8},{10,11... | collective-permute-start | bytes 417800 | tf_op jit(solution)/shard_map/ppermute | solution.py:367
  7.6 8.0 %collective-permute-start = (bf16[400,256]{1,0:T(8,128)(2,1)S(1)}, bf16[400,256]{1,0:T(8,128)(2,1)S(1)}, u32[]{:S(2)}, u32[]{:S(2)}) collective-permute-start(bf16[400,256]{1,0:T(8,128)(2,1)S(1)} %get-tuple-element.25), channel_id=1, source_target_pairs={{0,4},{4,0},{8,12},{12,8},{1,5},{5,1},{9,13},{13,9},{2,6},{6,2},{1... | collective-permute-start | bytes 614408 | tf_op jit(solution)/shard_map/ppermute | solution.py:380
  9.1 10.4 %collective-permute-start.1 = (bf16[400,256]{1,0:T(8,128)(2,1)S(1)}, bf16[400,256]{1,0:T(8,128)(2,1)S(1)}, u32[]{:S(2)}, u32[]{:S(2)}) collective-permute-start(bf16[400,256]{1,0:T(8,128)(2,1)S(1)} %get-tuple-element.26), channel_id=1, source_target_pairs={{0,8},{4,12},{8,0},{12,4},{1,9},{5,13},{9,1},{13,5},{2,10},{6,14},... | collective-permute-start | bytes 614408 | tf_op jit(solution)/shard_map/ppermute | solution.py:380
  10.6 8.8 %collective-permute-start.2 = (bf16[400,256]{1,0:T(8,128)(2,1)S(1)}, bf16[400,256]{1,0:T(8,128)(2,1)S(1)}, u32[]{:S(2)}, u32[]{:S(2)}) collective-permute-start(bf16[400,256]{1,0:T(8,128)(2,1)S(1)} %get-tuple-element.27), channel_id=1, source_target_pairs={{0,12},{4,8},{8,4},{12,0},{1,13},{5,9},{9,5},{13,1},{2,14},{6,10},... | collective-permute-start | bytes 614408 | tf_op jit(solution)/shard_map/ppermute | solution.py:380
  12.8 5.1 %collective-permute-start.7 = (bf16[272,256]{1,0:T(8,128)(2,1)S(1)}, bf16[272,256]{1,0:T(8,128)(2,1)S(1)}, u32[]{:S(2)}, u32[]{:S(2)}) collective-permute-start(bf16[272,256]{1,0:T(8,128)(2,1)S(1)} %collective-permute-done.5.refs_17_), channel_id=1, source_target_pairs={{0,1},{1,0},{2,3},{3,2},{4,5},{5,4},{6,7},{7,6},{8,9},{9,8},{10,11... | collective-permute-start | bytes 417800 | tf_op jit(solution)/shard_map/ppermute | solution.py:372
  13.4 6.1 %collective-permute-start.4 = (bf16[272,256]{1,0:T(8,128)(2,1)S(1)}, bf16[272,256]{1,0:T(8,128)(2,1)S(1)}, u32[]{:S(2)}, u32[]{:S(2)}) collective-permute-start(bf16[272,256]{1,0:T(8,128)(2,1)S(1)} %collective-permute-done.3.refs_15_), channel_id=1, source_target_pairs={{0,16},{16,0},{1,17},{17,1},{2,18},{18,2},{3,19},{19,3},{4,20},{20... | collective-permute-start | bytes 417800 | tf_op jit(solution)/shard_map/ppermute | solution.py:377
  15.6 3.9 %collective-permute-start.6 = (bf16[272,256]{1,0:T(8,128)(2,1)S(1)}, bf16[272,256]{1,0:T(8,128)(2,1)S(1)}, u32[]{:S(2)}, u32[]{:S(2)}) collective-permute-start(bf16[272,256]{1,0:T(8,128)(2,1)S(1)} %collective-permute-done.5.refs_17_), channel_id=1, source_target_pairs={{0,16},{16,0},{1,17},{17,1},{2,18},{18,2},{3,19},{19,3},{4,20},{20... | collective-permute-start | bytes 417800 | tf_op jit(solution)/shard_map/ppermute | solution.py:377
  17.8 1.7 %collective-permute-start.8 = (bf16[272,256]{1,0:T(8,128)(2,1)S(1)}, bf16[272,256]{1,0:T(8,128)(2,1)S(1)}, u32[]{:S(2)}, u32[]{:S(2)}) collective-permute-start(bf16[272,256]{1,0:T(8,128)(2,1)S(1)} %collective-permute-done.7.refs_19_), channel_id=1, source_target_pairs={{0,16},{16,0},{1,17},{17,1},{2,18},{18,2},{3,19},{19,3},{4,20},{20... | collective-permute-start | bytes 417800 | tf_op jit(solution)/shard_map/ppermute | solution.py:377
  27.7 2.4 %collective-permute-start.12 = (bf16[1024,256]{1,0:T(8,128)(2,1)S(1)}, bf16[1024,256]{1,0:T(8,128)(2,1)S(1)}, u32[]{:S(2)}, u32[]{:S(2)}) collective-permute-start(bf16[1024,256]{1,0:T(8,128)(2,1)S(1)} %get-tuple-element.42), channel_id=1, source_target_pairs={{0,16},{16,0},{1,17},{17,1},{2,18},{18,2},{3,19},{19,3},{4,20},{20... | collective-permute-start | bytes 1572872 | tf_op jit(solution)/shard_map/ppermute | solution.py:446
  27.8 11.0 %collective-permute-start.11 = (bf16[400,256]{1,0:T(8,128)(2,1)S(1)}, bf16[400,256]{1,0:T(8,128)(2,1)S(1)}, u32[]{:S(2)}, u32[]{:S(2)}) collective-permute-start(bf16[400,256]{1,0:T(8,128)(2,1)S(1)} %get-tuple-element.38), channel_id=1, source_target_pairs={{12,0},{8,4},{4,8},{0,12},{13,1},{9,5},{5,9},{1,13},{14,2},{10,6},... | collective-permute-start | bytes 614408 | tf_op jit(solution)/shard_map/ppermute | solution.py:499
  30.2 5.7 %collective-permute-start.13 = (bf16[256,256]{1,0:T(8,128)(2,1)S(1)}, bf16[256,256]{1,0:T(8,128)(2,1)S(1)}, u32[]{:S(2)}, u32[]{:S(2)}) collective-permute-start(bf16[256,256]{1,0:T(8,128)(2,1)S(1)} %get-tuple-element.45), channel_id=1, source_target_pairs={{0,1},{1,0},{2,3},{3,2},{4,5},{5,4},{6,7},{7,6},{8,9},{9,8},{10,11... | collective-permute-start | bytes 393224 | tf_op jit(solution)/shard_map/ppermute | solution.py:481
  31.5 9.2 %collective-permute-start.9 = (bf16[400,256]{1,0:T(8,128)(2,1)S(1)}, bf16[400,256]{1,0:T(8,128)(2,1)S(1)}, u32[]{:S(2)}, u32[]{:S(2)}) collective-permute-start(bf16[400,256]{1,0:T(8,128)(2,1)S(1)} %get-tuple-element.36), channel_id=1, source_target_pairs={{4,0},{0,4},{12,8},{8,12},{5,1},{1,5},{13,9},{9,13},{6,2},{2,6},{1... | collective-permute-start | bytes 614408 | tf_op jit(solution)/shard_map/ppermute | solution.py:499
  32.2 8.4 %collective-permute-start.10 = (bf16[400,256]{1,0:T(8,128)(2,1)S(1)}, bf16[400,256]{1,0:T(8,128)(2,1)S(1)}, u32[]{:S(2)}, u32[]{:S(2)}) collective-permute-start(bf16[400,256]{1,0:T(8,128)(2,1)S(1)} %get-tuple-element.37), channel_id=1, source_target_pairs={{8,0},{12,4},{0,8},{4,12},{9,1},{13,5},{1,9},{5,13},{10,2},{14,6},... | collective-permute-start | bytes 614408 | tf_op jit(solution)/shard_map/ppermute | solution.py:499
  33.8 8.4 %collective-permute-start.15 = (bf16[256,256]{1,0:T(8,128)(2,1)S(1)}, bf16[256,256]{1,0:T(8,128)(2,1)S(1)}, u32[]{:S(2)}, u32[]{:S(2)}) collective-permute-start(bf16[256,256]{1,0:T(8,128)(2,1)S(1)} %get-tuple-element.46), channel_id=1, source_target_pairs={{0,1},{1,0},{2,3},{3,2},{4,5},{5,4},{6,7},{7,6},{8,9},{9,8},{10,11... | collective-permute-start | bytes 393224 | tf_op jit(solution)/shard_map/ppermute | solution.py:482
  36.0 8.5 %collective-permute-start.14 = (bf16[256,256]{1,0:T(8,128)(2,1)S(1)}, bf16[256,256]{1,0:T(8,128)(2,1)S(1)}, u32[]{:S(2)}, u32[]{:S(2)}) collective-permute-start(bf16[256,256]{1,0:T(8,128)(2,1)S(1)} %join.1), channel_id=1, source_target_pairs={{0,2},{1,3},{2,0},{3,1},{4,6},{5,7},{6,4},{7,5},{8,10},{9,11},{10,... | collective-permute-start | bytes 393224 | tf_op jit(solution)/shard_map/ppermute | solution.py:482
